TPU v7x, 512 devices: a whole 4x8x8 slice. The times are simulated.
512 devices in a mesh: dp: 8 (over z), ctx: 64 (over x, y, core).
Axes of the slice: x: 4, y: 8, z: 8, core: 2. Of those that a mesh axis runs over, the one named last changes fastest.
Arguments:
- inputs: bfloat16 [8, 8192, 5120], P('dp', 'ctx'), may hold values from -16 to 16
- queries: bfloat16 [8, 8192, 512], P('dp', 'ctx'), may hold values from -4.5 to 4.5
- key_rows: bfloat16 [8, 8192, 512], P('dp', 'ctx'), may hold values from -4.5 to 4.5
- values: bfloat16 [8, 8192, 512], P('dp', 'ctx'), may hold values from -6 to 6
- frozen_output_gradient: bfloat16 [8, 8192, 512], P('dp', 'ctx'), may hold values from -6 to 6
- out_grad: bfloat16 [8, 8192, 5120], P('dp', 'ctx'), may hold values from -16 to 16
- block_lists: int32 [8, 256, 12], P('dp', 'ctx'), may hold values from -1 to 255, as said below
- down_qkv: bfloat16 [3, 5120, 64], P(None, ('dp', 'ctx')), may hold values from -0.078125 to 0.078125
- up_qkv: bfloat16 [3, 64, 512], replicated, may hold values from -0.75 to 0.75
- output_down_projection: bfloat16 [512, 64], replicated, may hold values from -0.25 to 0.25
- up_out: bfloat16 [64, 5120], P(None, ('dp', 'ctx')), may hold values from -0.078125 to 0.078125
Outputs:
- grad_queries: bfloat16 [8, 8192, 512], P('dp', 'ctx')
- grad_keys: bfloat16 [8, 8192, 512], P('dp', 'ctx')
- grad_values: bfloat16 [8, 8192, 512], P('dp', 'ctx')
- grad_down_qkv: float32 [3, 5120, 64], P(None, ('dp', 'ctx'))
- grad_up_qkv: float32 [3, 64, 512], replicated
- grad_down_out: float32 [512, 64], replicated
- grad_up_out: float32 [64, 5120], P(None, ('dp', 'ctx'))
Inputs may be any that keep to these rules, and one draw needn't show every extreme that they name: `block_lists`: row b of a sample lists the 4 blocks of its own frame (frame b // 4), half of 4 distinct blocks of each adjacent frame, and one block of each frame at distance 2 and 3; a slot is -1 where that frame lies outside the video.
All inputs are finite; a program needn't handle non-finite values.
Results may differ from a plain program's by a relative error of at most 0.025.
Values may be sent and summed in bfloat16 or wider, within the bound.
No kernel may reach another device: no remote copies, remote signals or barrier semaphores. Data moves between devices by JAX's collectives and lax.ppermute only.
A program may use at most 64 MiB of HBM per device.

v0:
```python
from functools import partial
from functools import reduce
import math

import jax
import jax.numpy as jnp
from jax import lax
from jax.sharding import PartitionSpec as P

HDIM = 128
BLK_DEV = 4


adapter_strength = 2.0
reach_frames = 3


def passed_along(shard, axis, by):
    peers = lax.axis_size(axis)
    pairs = [(i, i + by) for i in range(peers) if 0 <= i + by < peers]
    return lax.ppermute(shard, axis, pairs)


def tile_allowed(lists, first_block, block_count, block_rows):
    block_ids = first_block + jnp.arange(block_count, dtype=jnp.int32)
    matched = (
        jnp.any(lists[:, None, :] == block_ids[None, :, None], axis=-1) & (block_ids >= 0)[None, :]
    )
    return jnp.repeat(jnp.repeat(matched, block_rows, 0), block_rows, 1)


def fold_columns(carry, group, start, x_columns, y_columns, rank_size):
    down_part = jnp.einsum(
        "tk,tr->kr", x_columns, group[:, : 3 * rank_size], preferred_element_type=jnp.float32
    )
    up_part = jnp.einsum(
        "tr,tk->rk", group[:, 3 * rank_size :], y_columns, preferred_element_type=jnp.float32
    )
    return (down_part, up_part)


def shards(
    inputs,
    queries,
    key_rows,
    values,
    frozen_output_gradient,
    out_grad,
    block_lists,
    down_qkv,
    up_qkv,
    output_down_projection,
    up_out,
):
    row_count = queries.shape[1]
    feature_count = queries.shape[2]
    head_count = feature_count // HDIM
    rank_size = output_down_projection.shape[1]
    slice_rows = down_qkv.shape[1]
    block_rows = row_count // BLK_DEV
    scaling = HDIM ** (-0.5)
    size_dp = lax.axis_size("dp")
    size_ctx = lax.axis_size("ctx")
    frame_index = lax.axis_index("ctx")
    grad_scale = adapter_strength / math.sqrt(size_dp * size_ctx * row_count)
    down_full, up_out_full = (
        lax.all_gather(down_qkv, ("dp", "ctx"), axis=1, tiled=True),
        lax.all_gather(up_out, ("dp", "ctx"), axis=1, tiled=True),
    )
    input_rows = inputs[0]
    outg_rows = out_grad[0]
    low_in = jnp.einsum(
        "td,cdr->tcr", input_rows, down_full, preferred_element_type=jnp.float32
    ).astype(jnp.bfloat16)
    output_low_rank = jnp.einsum(
        "td,rd->tr", outg_rows, up_out_full, preferred_element_type=jnp.float32
    ).astype(jnp.bfloat16)
    adapter_gradient = jnp.einsum(
        "zj,gj->zg", output_low_rank, output_down_projection, preferred_element_type=jnp.float32
    )
    output_gradient_rows = (
        frozen_output_gradient[0].astype(jnp.float32) + adapter_strength * adapter_gradient
    ).astype(jnp.bfloat16)
    kv_pair = jnp.stack([key_rows[0], values[0]])
    offsets = list(range(-reach_frames, reach_frames + 1))
    windows = {}
    windows[0] = kv_pair
    for offset in offsets:
        if offset != 0:
            windows[offset] = passed_along(kv_pair, "ctx", -offset)
    query_heads = queries[0].reshape(row_count, head_count, HDIM)
    grad_heads = output_gradient_rows.reshape(row_count, head_count, HDIM)
    lists_here = block_lists[0]
    score_tiles = []
    for offset in offsets:
        key_heads = windows[offset][0].reshape(row_count, head_count, HDIM)
        allowed = tile_allowed(lists_here, (frame_index + offset) * BLK_DEV, BLK_DEV, block_rows)
        tile = (
            jnp.einsum("qhd,khd->hqk", query_heads, key_heads, preferred_element_type=jnp.float32)
            * scaling
        )
        score_tiles.append(jnp.where(allowed[None], tile, -jnp.inf))
    highest = reduce(jnp.maximum, [jnp.max(tile, axis=-1, keepdims=True) for tile in score_tiles])
    total_mass = reduce(
        jnp.add, [jnp.sum(jnp.exp(tile - highest), axis=-1, keepdims=True) for tile in score_tiles]
    )
    log_total = highest + jnp.log(total_mass)
    prob_tiles = [jnp.exp(tile - log_total) for tile in score_tiles]
    prob_low = [tile.astype(jnp.bfloat16) for tile in prob_tiles]
    attn_sum = jnp.zeros((row_count, head_count, HDIM), jnp.float32)
    for offset, probs in zip(offsets, prob_low):
        value_heads = windows[offset][1].reshape(row_count, head_count, HDIM)
        attn_sum = attn_sum + jnp.einsum(
            "hqk,khd->qhd", probs, value_heads, preferred_element_type=jnp.float32
        )
    attn = attn_sum.reshape(row_count, feature_count).astype(jnp.bfloat16)
    delta = jnp.sum(
        grad_heads.astype(jnp.float32)
        * attn.reshape(row_count, head_count, HDIM).astype(jnp.float32),
        axis=-1,
    )
    delta_cols = jnp.transpose(delta)[:, :, None]
    dq_sum = jnp.zeros((row_count, head_count, HDIM), jnp.float32)
    partials = {}
    for offset, probs, probs_bf in zip(offsets, prob_tiles, prob_low):
        key_heads = windows[offset][0].reshape(row_count, head_count, HDIM)
        value_heads = windows[offset][1].reshape(row_count, head_count, HDIM)
        dprob = jnp.einsum(
            "qhd,khd->hqk", grad_heads, value_heads, preferred_element_type=jnp.float32
        )
        dscore = (probs * (dprob - delta_cols)).astype(jnp.bfloat16)
        dq_sum = dq_sum + jnp.einsum(
            "hqk,khd->qhd", dscore, key_heads, preferred_element_type=jnp.float32
        )
        dk_part = (
            jnp.einsum("hqk,qhd->khd", dscore, query_heads, preferred_element_type=jnp.float32)
            * scaling
        )
        dv_part = jnp.einsum(
            "hqk,qhd->khd", probs_bf, grad_heads, preferred_element_type=jnp.float32
        )
        partials[offset] = jnp.stack(
            [dk_part.reshape(row_count, feature_count), dv_part.reshape(row_count, feature_count)]
        )
    grad_q = (dq_sum * scaling).reshape(row_count, feature_count).astype(jnp.bfloat16)
    kv_total = partials[0]
    for offset in offsets:
        if offset != 0:
            kv_total = kv_total + passed_along(
                partials[offset].astype(jnp.bfloat16), "ctx", offset
            ).astype(jnp.float32)
    grad_k = kv_total[0].astype(jnp.bfloat16)
    grad_v = kv_total[1].astype(jnp.bfloat16)
    gathered_gradients = jnp.stack([grad_q, grad_k, grad_v], axis=1)
    term_up = (
        jnp.einsum("tcr,tch->crh", low_in, gathered_gradients, preferred_element_type=jnp.float32)
        * grad_scale
    )
    term_down_out = (
        jnp.einsum("th,tr->hr", attn, output_low_rank, preferred_element_type=jnp.float32)
        * grad_scale
    )
    sum_up, sum_down_out = lax.psum((term_up, term_down_out), ("dp", "ctx"))
    low_attn = jnp.dot(attn, output_down_projection, preferred_element_type=jnp.float32).astype(
        jnp.bfloat16
    )
    factor_qkv = jnp.einsum(
        "tch,crh->tcr", gathered_gradients, up_qkv, preferred_element_type=jnp.float32
    ).astype(jnp.bfloat16)
    factors = jnp.concatenate([factor_qkv.reshape(row_count, 3 * rank_size), low_attn], axis=1)
    x_parts, y_parts = (
        lax.all_to_all(
            input_rows.reshape(row_count, size_dp, size_ctx, slice_rows),
            "ctx",
            split_axis=2,
            concat_axis=0,
            tiled=True,
        ),
        lax.all_to_all(
            outg_rows.reshape(row_count, size_dp, size_ctx, slice_rows),
            "ctx",
            split_axis=2,
            concat_axis=0,
            tiled=True,
        ),
    )
    x_columns = x_parts.reshape(size_ctx * row_count, size_dp * slice_rows)
    y_columns = y_parts.reshape(size_ctx * row_count, size_dp * slice_rows)
    start_carry = (
        jnp.zeros((size_dp * slice_rows, 3 * rank_size), jnp.float32),
        jnp.zeros((rank_size, size_dp * slice_rows), jnp.float32),
    )
    fold_fn = partial(fold_columns, x_columns=x_columns, y_columns=y_columns, rank_size=rank_size)
    down_cols, up_cols = fold_fn(
        start_carry, lax.all_gather(factors, "ctx", axis=0, tiled=True), jnp.int32(0)
    )
    grad_down_rows, grad_up_out = (
        lax.psum_scatter(
            (down_cols * grad_scale).astype(jnp.bfloat16), "dp", scatter_dimension=0, tiled=True
        ).astype(jnp.float32),
        lax.psum_scatter(
            (up_cols * grad_scale).astype(jnp.bfloat16), "dp", scatter_dimension=1, tiled=True
        ).astype(jnp.float32),
    )
    grad_down_qkv = jnp.transpose(grad_down_rows.reshape(slice_rows, 3, rank_size), (1, 0, 2))
    return (
        grad_q[None],
        grad_k[None],
        grad_v[None],
        grad_down_qkv,
        sum_up,
        sum_down_out,
        grad_up_out,
    )


def solution(mesh):
    placed = (
        P("dp", "ctx", None),
        P("dp", "ctx", None),
        P("dp", "ctx", None),
        P("dp", "ctx", None),
        P("dp", "ctx", None),
        P("dp", "ctx", None),
        P("dp", "ctx", None),
        P(None, ("dp", "ctx"), None),
        P(),
        P(),
        P(None, ("dp", "ctx")),
    )
    return jax.shard_map(
        shards,
        mesh=mesh,
        in_specs=placed,
        out_specs=(
            P("dp", "ctx", None),
            P("dp", "ctx", None),
            P("dp", "ctx", None),
            P(None, ("dp", "ctx"), None),
            P(),
            P(),
            P(None, ("dp", "ctx")),
        ),
        check_vma=False,
    )
```

profile of v0, /device:TPU:1, one launch (start us, length us, event | category | flops | bytes accessed | tf_op | source)
XLA Modules:
  0.0 568.7 jit_solution(12279539671826993815)
XLA Ops:
  7.2 1.1 copy.357
  8.3 1.0 copy.356
  9.4 1.3 collective-permute-start.5
  10.7 1.3 collective-permute-start.4
  12.0 8.8 %collective-permute-start.3 = (bf16[2,128,512]{1,2,0:T(8,128)(2,1)S(1)}, bf16[2,128,512]{1,2,0:T(8,128)(2,1)}, u32[]{:S(2)}, u32[]{:S(2)}) collective-permute-start(bf16[2,128,512]{1,2,0:T(8,128)(2,1)S(1)} %pad_maximum_fusion.1), channel_id=1, source_target_pairs={{1,0},{2,1},{3,2},{4,3},{5,4},{6,5},{7,6},{8,7},{9,8},{10,9},{11,1... | collective-permute-start | bytes 786440 | tf_op jit(solution)/shard_map/ppermute | solution.py:21
  20.8 4.2 collective-permute-start.2
  24.9 4.5 collective-permute-start
  29.8 79.0 %all-gather = bf16[512,10,64]{2,1,0:T(8,128)(2,1)S(1)} all-gather(bf16[1,10,64]{2,1,0:T(8,128)(2,1)} %bitcast.384), channel_id=1, replica_groups=mesh['dp'=8,'ctx'=64] {'dp','ctx'}, dimensions={0}, use_global_device_ids=true | all-gather | bytes 656640 | tf_op jit(solution)/shard_map/all_gather | solution.py:68
  108.7 1.6 reshape.260
  110.3 2.4 fusion.99
  113.0 0.6 compare_reduce_fusion.5
  116.1 0.3 fusion.146
  116.4 1.3 collective-permute-start.1
  117.7 1.0 fusion.142
  119.3 1.0 fusion.140
  120.9 1.0 fusion.137
  122.2 1.8 collective-permute-done.1
  125.4 0.3 convolution_bitcast_fusion.7
  128.0 0.9 convolution_convert_fusion.1
  129.8 0.8 copy.473
  131.1 1.6 pad_maximum_fusion.7
  132.7 6.7 %collective-permute-start.11 = (bf16[2,128,512]{2,1,0:T(8,128)(2,1)}, bf16[2,128,512]{2,1,0:T(8,128)(2,1)}, u32[]{:S(2)}, u32[]{:S(2)}) collective-permute-start(bf16[2,128,512]{2,1,0:T(8,128)(2,1)} %pad_maximum_fusion.7), channel_id=1, source_target_pairs={{0,3},{1,4},{2,5},{3,6},{4,7},{5,8},{6,9},{7,10},{8,11},{9,12},{10... | collective-permute-start | bytes 786440 | tf_op jit(solution)/shard_map/ppermute | solution.py:21
  139.4 1.7 copy.465
  141.6 1.6 pad_maximum_fusion.6
  143.2 2.0 collective-permute-start.10
  145.2 0.8 copy.457
  146.4 1.6 pad_maximum_fusion.5
  148.1 2.1 collective-permute-start.9
  150.8 0.7 pad_maximum_fusion.4
  151.5 3.3 collective-permute-start.8
  155.4 0.7 pad_maximum_fusion.3
  156.1 1.3 collective-permute-start.7
  158.0 0.7 pad_maximum_fusion.2
  160.1 0.3 fusion.123
  160.6 1.3 collective-permute-start.6
  162.9 3.6 collective-permute-done.7
  166.5 9.4 %collective-permute-done.6 = bf16[2,128,512]{2,1,0:T(8,128)(2,1)S(1)} collective-permute-done((bf16[2,128,512]{2,1,0:T(8,128)(2,1)}, bf16[2,128,512]{2,1,0:T(8,128)(2,1)S(1)}, u32[]{:S(2)}, u32[]{:S(2)}) %collective-permute-start.6) | collective-permute-done | bytes 262176 | tf_op jit(solution)/shard_map/ppermute | solution.py:21
  175.9 1.5 fusion.107
  177.7 0.6 pad_maximum_fusion.10
  178.4 0.5 copy-done.2
  178.8 1.4 copy.475
  180.3 2.4 reshape_squeeze.70
  182.6 2.6 copy.476
  185.2 12.8 %all-to-all-start = ((bf16[128,8,64,10]{0,1,3,2:T(8,128)(2,1)}), bf16[128,8,64,10]{0,1,3,2:T(8,128)(2,1)}, u32[]{:S(2)}, u32[]{:S(2)}) async-start(bf16[128,8,64,10]{0,1,3,2:T(8,128)(2,1)} %copy.476), calls=%async_computation | async-start | bytes 2621440 | tf_op jit(solution)/shard_map/all_to_all | solution.py:172
  198.0 1.5 copy.479
  199.5 2.4 reshape_squeeze.71
  201.8 2.6 copy.480
  204.5 29.7 %all-to-all-done = bf16[128,8,64,10]{0,1,3,2:T(8,128)(2,1)} async-done(((bf16[128,8,64,10]{0,1,3,2:T(8,128)(2,1)}), bf16[128,8,64,10]{0,1,3,2:T(8,128)(2,1)}, u32[]{:S(2)}, u32[]{:S(2)}) %all-to-all-start) | async-done | bytes 1310752 | tf_op jit(solution)/shard_map/all_to_all | solution.py:172
  234.2 5.9 %all-to-all-start.1 = ((bf16[128,8,64,10]{0,1,3,2:T(8,128)(2,1)}), bf16[128,8,64,10]{0,1,3,2:T(8,128)(2,1)S(1)}, u32[]{:S(2)}, u32[]{:S(2)}) async-start(bf16[128,8,64,10]{0,1,3,2:T(8,128)(2,1)} %copy.480), calls=%async_computation.1 | async-start | bytes 2621440 | tf_op jit(solution)/shard_map/all_to_all | solution.py:179
  240.4 1.3 dynamic-slice
  242.3 0.8 copy.482
  243.1 0.8 convolution_multiply_fusion.16
  243.9 2.7 copy.477
  246.7 34.6 %all-to-all-done.1 = bf16[128,8,64,10]{0,1,3,2:T(8,128)(2,1)S(1)} async-done(((bf16[128,8,64,10]{0,1,3,2:T(8,128)(2,1)}), bf16[128,8,64,10]{0,1,3,2:T(8,128)(2,1)S(1)}, u32[]{:S(2)}, u32[]{:S(2)}) %all-to-all-start.1) | async-done | bytes 1310752 | tf_op jit(solution)/shard_map/all_to_all | solution.py:179
  281.3 1.4 copy.481
  282.7 4.8 convolution_multiply_fusion
  287.6 3.2 fusion.88
  290.8 2.2 fusion.96
  293.0 22.8 %all-reduce.3 = (bf16[80,192]{1,0:T(8,128)(2,1)S(1)}, bf16[64,80]{0,1:T(8,128)(2,1)S(1)}) all-reduce(bf16[80,192]{1,0:T(8,128)(2,1)S(1)} %fusion.88, bf16[64,80]{0,1:T(8,128)(2,1)S(1)} %fusion.96), channel_id=2, replica_groups=mesh['dp'=8,'ctx'=64] {'dp'}, use_global_device_ids=true, to_apply=%region_22.23.clone | all-reduce | flops 20480 | bytes 81920
  315.8 0.7 reshape.258
  316.5 0.6 dynamic-slice_convert_fusion.1
  317.1 241.8 %all-reduce.6.cloned.1.call-done = (f32[3,64,512]{2,1,0:T(8,128)}, f32[512,64]{0,1:T(8,128)}) async-done(((f32[3,64,512]{2,1,0:T(8,128)}, f32[512,64]{0,1:T(8,128)}), (f32[3,64,512]{2,1,0:T(8,128)}, f32[512,64]{0,1:T(8,128)})) %all-reduce.6.cloned.1.call-update) | async-done | bytes 524304 | tf_op jit(solution)/shard_map/psum | solution.py:163
  558.8 1.8 copy.579
  560.6 1.6 copy.580
  (166 shorter events, 14.9 us)
Async XLA Ops:
  7.2 170.3 %copy-start = (bf16[3,64,512]{2,1,0:T(8,128)(2,1)S(1)}, bf16[3,64,512]{2,1,0:T(8,128)(2,1)}, u32[]{:S(2)}) copy-start(bf16[3,64,512]{2,1,0:T(8,128)(2,1)} %param.19) | copy-start | bytes 589828
  7.2 275.5 %all-gather.6.cloned.1.call-start = ((), (), s32[]{:S(2)}) async-start(), calls=%async_computation.3 | async-start | bytes 5253120 | tf_op jit(solution)/shard_map/all_gather | solution.py:67
  9.4 107.1 %collective-permute-start.5 = (bf16[2,128,512]{1,2,0:T(8,128)(2,1)S(1)}, bf16[2,128,512]{1,2,0:T(8,128)(2,1)}, u32[]{:S(2)}, u32[]{:S(2)}) collective-permute-start(bf16[2,128,512]{1,2,0:T(8,128)(2,1)S(1)} %pad_maximum_fusion.1), channel_id=1, source_target_pairs={{3,0},{4,1},{5,2},{6,3},{7,4},{8,5},{9,6},{10,7},{11,8},{12,9},{13... | collective-permute-start | bytes 786440 | tf_op jit(solution)/shard_map/ppermute | solution.py:21
  10.7 108.4 %collective-permute-start.4 = (bf16[2,128,512]{1,2,0:T(8,128)(2,1)S(1)}, bf16[2,128,512]{1,2,0:T(8,128)(2,1)S(1)}, u32[]{:S(2)}, u32[]{:S(2)}) collective-permute-start(bf16[2,128,512]{1,2,0:T(8,128)(2,1)S(1)} %pad_maximum_fusion.1), channel_id=1, source_target_pairs={{2,0},{3,1},{4,2},{5,3},{6,4},{7,5},{8,6},{9,7},{10,8},{11,9},{12,... | collective-permute-start | bytes 786440 | tf_op jit(solution)/shard_map/ppermute | solution.py:21
  12.0 107.4 %collective-permute-start.3 = (bf16[2,128,512]{1,2,0:T(8,128)(2,1)S(1)}, bf16[2,128,512]{1,2,0:T(8,128)(2,1)}, u32[]{:S(2)}, u32[]{:S(2)}) collective-permute-start(bf16[2,128,512]{1,2,0:T(8,128)(2,1)S(1)} %pad_maximum_fusion.1), channel_id=1, source_target_pairs={{1,0},{2,1},{3,2},{4,3},{5,4},{6,5},{7,6},{8,7},{9,8},{10,9},{11,1... | collective-permute-start | bytes 786440 | tf_op jit(solution)/shard_map/ppermute | solution.py:21
  20.8 99.9 %collective-permute-start.2 = (bf16[2,128,512]{1,2,0:T(8,128)(2,1)S(1)}, bf16[2,128,512]{1,2,0:T(8,128)(2,1)S(1)}, u32[]{:S(2)}, u32[]{:S(2)}) collective-permute-start(bf16[2,128,512]{1,2,0:T(8,128)(2,1)S(1)} %pad_maximum_fusion.1), channel_id=1, source_target_pairs={{0,1},{1,2},{2,3},{3,4},{4,5},{5,6},{6,7},{7,8},{8,9},{9,10},{10,1... | collective-permute-start | bytes 786440 | tf_op jit(solution)/shard_map/ppermute | solution.py:21
  24.9 96.0 %collective-permute-start = (bf16[2,128,512]{1,2,0:T(8,128)(2,1)S(1)}, bf16[2,128,512]{1,2,0:T(8,128)(2,1)}, u32[]{:S(2)}, u32[]{:S(2)}) collective-permute-start(bf16[2,128,512]{1,2,0:T(8,128)(2,1)S(1)} %pad_maximum_fusion.1), channel_id=1, source_target_pairs={{0,3},{1,4},{2,5},{3,6},{4,7},{5,8},{6,9},{7,10},{8,11},{9,12},{10... | collective-permute-start | bytes 786440 | tf_op jit(solution)/shard_map/ppermute | solution.py:21
  29.5 258.0 %all-gather.4.cloned.1.call-start = ((), (), s32[]{:S(2)}) async-start(), calls=%async_computation.2 | async-start | bytes 4259840 | tf_op jit(solution)/shard_map/all_gather | solution.py:195
  110.3 2.5 copy-start.7
  110.3 2.5 copy-start.10
  110.3 2.7 copy-start.14
  110.3 3.4 copy-start.6
  110.3 3.6 copy-start.11
  112.7 0.9 copy-start.8
  116.4 7.5 %collective-permute-start.1 = (bf16[2,128,512]{1,2,0:T(8,128)(2,1)S(1)}, bf16[2,128,512]{1,2,0:T(8,128)(2,1)S(1)}, u32[]{:S(2)}, u32[]{:S(2)}) collective-permute-start(bf16[2,128,512]{1,2,0:T(8,128)(2,1)S(1)} %pad_maximum_fusion.1), channel_id=1, source_target_pairs={{0,2},{1,3},{2,4},{3,5},{4,6},{5,7},{6,8},{7,9},{8,10},{9,11},{10,... | collective-permute-start | bytes 786440 | tf_op jit(solution)/shard_map/ppermute | solution.py:21
  132.7 27.9 %collective-permute-start.11 = (bf16[2,128,512]{2,1,0:T(8,128)(2,1)}, bf16[2,128,512]{2,1,0:T(8,128)(2,1)}, u32[]{:S(2)}, u32[]{:S(2)}) collective-permute-start(bf16[2,128,512]{2,1,0:T(8,128)(2,1)} %pad_maximum_fusion.7), channel_id=1, source_target_pairs={{0,3},{1,4},{2,5},{3,6},{4,7},{5,8},{6,9},{7,10},{8,11},{9,12},{10... | collective-permute-start | bytes 786440 | tf_op jit(solution)/shard_map/ppermute | solution.py:21
  143.2 19.7 %collective-permute-start.10 = (bf16[2,128,512]{2,1,0:T(8,128)(2,1)}, bf16[2,128,512]{2,1,0:T(8,128)(2,1)}, u32[]{:S(2)}, u32[]{:S(2)}) collective-permute-start(bf16[2,128,512]{2,1,0:T(8,128)(2,1)} %pad_maximum_fusion.6), channel_id=1, source_target_pairs={{0,2},{1,3},{2,4},{3,5},{4,6},{5,7},{6,8},{7,9},{8,10},{9,11},{10,... | collective-permute-start | bytes 786440 | tf_op jit(solution)/shard_map/ppermute | solution.py:21
  148.1 14.8 %collective-permute-start.9 = (bf16[2,128,512]{2,1,0:T(8,128)(2,1)}, bf16[2,128,512]{2,1,0:T(8,128)(2,1)}, u32[]{:S(2)}, u32[]{:S(2)}) collective-permute-start(bf16[2,128,512]{2,1,0:T(8,128)(2,1)} %pad_maximum_fusion.5), channel_id=1, source_target_pairs={{0,1},{1,2},{2,3},{3,4},{4,5},{5,6},{6,7},{7,8},{8,9},{9,10},{10,1... | collective-permute-start | bytes 786440 | tf_op jit(solution)/shard_map/ppermute | solution.py:21
  151.5 11.4 %collective-permute-start.8 = (bf16[2,128,512]{2,1,0:T(8,128)(2,1)}, bf16[2,128,512]{2,1,0:T(8,128)(2,1)}, u32[]{:S(2)}, u32[]{:S(2)}) collective-permute-start(bf16[2,128,512]{2,1,0:T(8,128)(2,1)} %pad_maximum_fusion.4), channel_id=1, source_target_pairs={{1,0},{2,1},{3,2},{4,3},{5,4},{6,5},{7,6},{8,7},{9,8},{10,9},{11,1... | collective-permute-start | bytes 786440 | tf_op jit(solution)/shard_map/ppermute | solution.py:21
  156.1 10.4 %collective-permute-start.7 = (bf16[2,128,512]{2,1,0:T(8,128)(2,1)}, bf16[2,128,512]{2,1,0:T(8,128)(2,1)}, u32[]{:S(2)}, u32[]{:S(2)}) collective-permute-start(bf16[2,128,512]{2,1,0:T(8,128)(2,1)} %pad_maximum_fusion.3), channel_id=1, source_target_pairs={{2,0},{3,1},{4,2},{5,3},{6,4},{7,5},{8,6},{9,7},{10,8},{11,9},{12,... | collective-permute-start | bytes 786440 | tf_op jit(solution)/shard_map/ppermute | solution.py:21
  160.6 15.3 %collective-permute-start.6 = (bf16[2,128,512]{2,1,0:T(8,128)(2,1)}, bf16[2,128,512]{2,1,0:T(8,128)(2,1)S(1)}, u32[]{:S(2)}, u32[]{:S(2)}) collective-permute-start(bf16[2,128,512]{2,1,0:T(8,128)(2,1)} %pad_maximum_fusion.2), channel_id=1, source_target_pairs={{3,0},{4,1},{5,2},{6,3},{7,4},{8,5},{9,6},{10,7},{11,8},{12,9},{13... | collective-permute-start | bytes 786440 | tf_op jit(solution)/shard_map/ppermute | solution.py:21
  177.4 1.4 copy-start.2
  177.4 105.3 %copy-start.12 = (bf16[1,128,512]{2,1,0:T(8,128)(2,1)}, bf16[1,128,512]{2,1,0:T(8,128)(2,1)S(1)}, u32[]{:S(2)}) copy-start(bf16[1,128,512]{2,1,0:T(8,128)(2,1)S(1)} %get-tuple-element.90) | copy-start | bytes 393220
  177.4 105.3 %copy-start.13 = (bf16[1,128,512]{2,1,0:T(8,128)(2,1)}, bf16[1,128,512]{2,1,0:T(8,128)(2,1)S(1)}, u32[]{:S(2)}) copy-start(bf16[1,128,512]{2,1,0:T(8,128)(2,1)S(1)} %get-tuple-element.89) | copy-start | bytes 393220
  185.2 12.8 %copy-start.1 = (bf16[1,128,5120]{2,1,0:T(8,128)(2,1)S(1)}, bf16[1,128,5120]{2,1,0:T(8,128)(2,1)}, u32[]{:S(2)}) copy-start(bf16[1,128,5120]{2,1,0:T(8,128)(2,1)} %param.16) | copy-start | bytes 3932164
  185.2 49.0 %all-to-all-start = ((bf16[128,8,64,10]{0,1,3,2:T(8,128)(2,1)}), bf16[128,8,64,10]{0,1,3,2:T(8,128)(2,1)}, u32[]{:S(2)}, u32[]{:S(2)}) async-start(bf16[128,8,64,10]{0,1,3,2:T(8,128)(2,1)} %copy.476), calls=%async_computation | async-start | bytes 2621440 | tf_op jit(solution)/shard_map/all_to_all | solution.py:172
  204.5 38.7 %copy-start.9 = (bf16[128,64]{0,1:T(8,128)(2,1)S(1)}, bf16[128,64]{0,1:T(8,128)(2,1)}, u32[]{:S(2)}) copy-start(bf16[128,64]{0,1:T(8,128)(2,1)} %copy-done.8) | copy-start | bytes 49156
  234.2 47.1 %all-to-all-start.1 = ((bf16[128,8,64,10]{0,1,3,2:T(8,128)(2,1)}), bf16[128,8,64,10]{0,1,3,2:T(8,128)(2,1)S(1)}, u32[]{:S(2)}, u32[]{:S(2)}) async-start(bf16[128,8,64,10]{0,1,3,2:T(8,128)(2,1)} %copy.480), calls=%async_computation.1 | async-start | bytes 2621440 | tf_op jit(solution)/shard_map/all_to_all | solution.py:179
  240.2 318.7 %all-reduce.6.cloned.1.call-start = ((), (), s32[]{:S(2)}) async-start(), calls=%async_computation.4 | async-start | bytes 1048576 | tf_op jit(solution)/shard_map/psum | solution.py:163
  281.3 1.4 copy-start.3
  282.7 4.9 copy-start.4
  287.6 3.2 copy-start.5
Sparse Core Ops, SparseCore 0:
  29.6 125.5 all-gather.5
  178.5 106.4 all-gather.3
  290.7 268.1 all-reduce.5
where the time goes:
time: 570 us; the launch traced here: 569 us
  waiting for transfers between devices  321 us (56%)
  blocking collectives  102 us (18%)
  starting transfers between devices  57.1 us (10%)
  local copies, waits for them, and re-layouts  38.2 us (7%)
  matrix products  24.1 us (4%)
  between operations  15.5 us (3%)
  other arithmetic  11.2 us (2%)
    psum x1, waiting for transfers between devices, shards(): sum_up, sum_down_out = lax.psum((term_up, term_down_out), ('dp', 'ctx'))  242 us
    all_gather x1, blocking collectives, shards(): lax.all_gather(up_out, ('dp', 'ctx'), axis=1, tiled=True)  79 us
    ppermute x12, starting transfers between devices, passed_along(): return lax.ppermute(shard, axis, pairs)  38 us
    all_to_all x1, waiting for transfers between devices, shards(): lax.all_to_all(outg_rows.reshape(row_count, size_dp, size_ctx, slice_rows...  34.6 us
    all_to_all x1, waiting for transfers between devices, shards(): lax.all_to_all(input_rows.reshape(row_count, size_dp, size_ctx, slice_row...  29.7 us
    unnamed x1, blocking collectives  22.8 us
    ppermute x12, waiting for transfers between devices, passed_along(): return lax.ppermute(shard, axis, pairs)  14.8 us
    all_to_all x1, starting transfers between devices, shards(): lax.all_to_all(input_rows.reshape(row_count, size_dp, size_ctx, slice_row...  12.8 us
  transfers between devices with their start and end apart: 17, of which 6 were waited for; matrix products, arithmetic and copies ran while one was open for 12% of the time, Pallas kernels for 0%

commit v1 on v0

v1 whole, which is shorter than its diff:
```python
import math

import jax
import jax.numpy as jnp
from jax import lax
from jax.experimental import pallas as pl
from jax.experimental.pallas import tpu as pltpu
from jax.sharding import Mesh, PartitionSpec as P

HDIM = 128
BLK = 32
BLK_DEV = 4
NX, NY, NZ = 4, 8, 8
STRENGTH = 2.0
SCALING = HDIM**-0.5
MASKED = -1e30
BF = jnp.bfloat16
F32 = jnp.float32

SEGMENTS = ((0, 128), (128, 384), (384, 640), (640, 896), (896, 1024))


def dot(a, b, ca, cb):
    return lax.dot_general(a, b, (((ca,), (cb,)), ((), ())), preferred_element_type=F32)


def attention_kernel(
    q_ref, l2_ref, l1_ref, own_ref, r1_ref, r2_ref, fog_ref, low_ref, odp_ref, bias_ref,
    attn_ref, dq_ref, pl2_ref, pl1_ref, pown_ref, pr1_ref, pr2_ref,
):
    kv_refs = (l2_ref, l1_ref, own_ref, r1_ref, r2_ref)
    part_refs = (pl2_ref, pl1_ref, pown_ref, pr1_ref, pr2_ref)
    half = q_ref.shape[1]
    dout = (fog_ref[...].astype(F32) + STRENGTH * dot(low_ref[...], odp_ref[...], 1, 1)).astype(BF)
    bias = bias_ref[...]
    for head in range(half // HDIM):
        cols = slice(head * HDIM, (head + 1) * HDIM)
        vcols = slice(half + head * HDIM, half + (head + 1) * HDIM)
        q = q_ref[:, cols]
        dout_h = dout[:, cols]
        keys = [ref[:, cols] for ref in kv_refs]
        vals = [ref[:, vcols] for ref in kv_refs]
        scores = []
        for k, (a, b) in zip(keys, SEGMENTS):
            s = dot(q, k, 1, 1) * SCALING
            s = s.reshape(8, BLK, b - a) + bias[:, None, a:b]
            scores.append(s.reshape(8 * BLK, b - a))
        top = scores[0].max(axis=1, keepdims=True)
        for s in scores[1:]:
            top = jnp.maximum(top, s.max(axis=1, keepdims=True))
        weights = [jnp.exp(s - top) for s in scores]
        total = weights[0].sum(axis=1, keepdims=True)
        for w in weights[1:]:
            total = total + w.sum(axis=1, keepdims=True)
        inverse = 1.0 / total
        probs = [w * inverse for w in weights]
        probs_low = [p.astype(BF) for p in probs]
        attn = dot(probs_low[0], vals[0], 1, 0)
        for p, v in zip(probs_low[1:], vals[1:]):
            attn = attn + dot(p, v, 1, 0)
        attn = attn.astype(BF)
        attn_ref[:, cols] = attn
        delta = (dout_h.astype(F32) * attn.astype(F32)).sum(axis=1, keepdims=True)
        dq = None
        for k, v, p, p_low, out in zip(keys, vals, probs, probs_low, part_refs):
            dscore = (p * (dot(dout_h, v, 1, 1) - delta)).astype(BF)
            term = dot(dscore, k, 1, 0)
            dq = term if dq is None else dq + term
            out[:, cols] = (dot(dscore, q, 0, 0) * SCALING).astype(out.dtype)
            out[:, vcols] = dot(p_low, dout_h, 0, 0).astype(out.dtype)
        dq_ref[:, cols] = (dq * SCALING).astype(BF)


def attention(q, windows, fog, low_out, odp_half, bias):
    rows, half = q.shape
    shape = jax.ShapeDtypeStruct
    outs = [shape((rows, half), BF), shape((rows, half), BF)]
    outs += [shape((b - a, 2 * half), F32 if i == 2 else BF) for i, (a, b) in enumerate(SEGMENTS)]
    vmem = pl.BlockSpec(memory_space=pltpu.VMEM)
    return pl.pallas_call(
        attention_kernel,
        out_shape=outs,
        in_specs=[vmem] * 10,
        out_specs=[vmem] * 7,
        compiler_params=pltpu.CompilerParams(vmem_limit_bytes=40 * 1024 * 1024),
        cost_estimate=pl.CostEstimate(flops=1_400_000_000, bytes_accessed=4_000_000, transcendentals=524288),
        name="attention",
    )(q, *windows, fog, low_out, odp_half, bias)


def exchange(parts, axes):
    return lax.all_to_all(parts, axes, split_axis=0, concat_axis=0, tiled=True)


def spread(block, axes, peers):
    return exchange(jnp.broadcast_to(block[None], (peers,) + block.shape), axes)


def swap(block):
    return lax.ppermute(block, "c", [(0, 1), (1, 0)])


def chip_shift(block, by):
    chips = NX * NY
    return lax.ppermute(block, ("x", "y"), [(i, i + by) for i in range(chips) if 0 <= i + by < chips])


def shards(
    inputs, queries, key_rows, values, frozen_output_gradient, out_grad, block_lists,
    down_qkv, up_qkv, output_down_projection, up_out,
):
    x_own, y_own = inputs[0], out_grad[0]
    rows, feats = queries.shape[1:]
    half = feats // 2
    rank = output_down_projection.shape[1]
    width = x_own.shape[1]
    own_cols = down_qkv.shape[1]
    core = lax.axis_index("c")
    first = core == 0
    chip = lax.axis_index("x") * NY + lax.axis_index("y")
    grad_scale = STRENGTH / math.sqrt(NX * NY * NZ * 2 * rows)

    lists = jnp.pad(block_lists[0].astype(BF), ((0, 12), (0, half - block_lists.shape[2])))
    stack = jnp.concatenate([queries[0], frozen_output_gradient[0], key_rows[0], values[0]], axis=0)
    stack = jnp.stack([stack[:, :half], stack[:, half:]])
    stack = jnp.concatenate([stack, jnp.broadcast_to(lists[None], (2,) + lists.shape)], axis=1)
    chip_stack = exchange(stack, "c")
    q_chip = chip_stack[:, :rows].reshape(2 * rows, half)
    fog_chip = chip_stack[:, rows : 2 * rows].reshape(2 * rows, half)
    kv_chip = jnp.concatenate(
        [chip_stack[:, 2 * rows : 3 * rows], chip_stack[:, 3 * rows : 4 * rows]], axis=2
    ).reshape(2 * rows, 2 * half)
    lists_chip = chip_stack[:, 4 * rows : 4 * rows + BLK_DEV, : block_lists.shape[2]].reshape(
        2 * BLK_DEV, -1
    )
    windows = (
        chip_shift(kv_chip[rows:], 2),
        chip_shift(kv_chip, 1),
        kv_chip,
        chip_shift(kv_chip, -1),
        chip_shift(kv_chip[:rows], -2),
    )
    ids = (2 * chip - 3) * BLK_DEV + jnp.arange(8 * BLK_DEV, dtype=jnp.int32)
    allowed = jnp.any(lists_chip[:, :, None] == ids.astype(F32)[None, None, :], axis=1) & (ids >= 0)[None]
    bias = jnp.repeat(jnp.where(allowed, 0.0, MASKED).astype(F32), BLK, axis=1)

    x_other = swap(x_own)
    y_other = lax.ppermute(y_own, "c", [(0, 1)])
    a_own = jnp.where(first, x_own, y_own)
    a_other = jnp.where(first, x_other, y_other)

    shard = jnp.concatenate([down_qkv[0], down_qkv[1], up_out.T, down_qkv[2]], axis=1)
    line = spread(shard.reshape(2, -1), ("y", "c"), 2 * NY).reshape(2 * NY * own_cols, 4 * rank)
    line = lax.dynamic_slice_in_dim(line, core * 2 * rank, 2 * rank, 1)
    plane = spread(line, "z", NZ)
    whole = spread(plane, "x", NX)
    weights = jnp.transpose(whole, (1, 0, 2, 3)).reshape(width, 2 * rank)
    w_a, w_b = weights[:, :rank], weights[:, rank:]
    low_a = jnp.concatenate([dot(a_own, w_a, 1, 0), dot(a_other, w_a, 1, 0)], axis=0).astype(BF)
    low_b = jnp.concatenate([dot(x_own, w_b, 1, 0), dot(x_other, w_b, 1, 0)], axis=0).astype(BF)

    def ordered(pair):
        return jnp.where(first, pair, jnp.concatenate([pair[rows:], pair[:rows]], axis=0))

    low_a, low_b = ordered(low_a), ordered(low_b)
    low_out = jnp.where(first, lax.ppermute(low_a, "c", [(1, 0)]), low_a)
    odp_half = lax.dynamic_slice_in_dim(output_down_projection, core * half, half, 0)

    attn, dq, p_l2, p_l1, p_own, p_r1, p_r2 = attention(q_chip, windows, fog_chip, low_out, odp_half, bias)
    from_r2 = chip_shift(p_l2, -2)
    from_r1 = chip_shift(p_l1, -1)
    from_l1 = chip_shift(p_r1, 1)
    from_l2 = chip_shift(p_r2, 2)

    m_a = jnp.where(first, up_qkv[0].T, output_down_projection)
    m_b = jnp.where(first, up_qkv[1].T, up_qkv[2].T)

    def halves(matrix):
        mine = lax.dynamic_slice_in_dim(matrix, core * half, half, 0)
        theirs = lax.dynamic_slice_in_dim(matrix, (1 - core) * half, half, 0)
        return mine, theirs

    def role(kept, got, low, matrix):
        mine, theirs = halves(matrix)
        factor = (dot(kept, mine, 1, 0) + dot(got, theirs, 1, 0)).astype(BF)
        left = jnp.where(first, kept, got)
        right = jnp.where(first, got, kept)
        up = dot(low, jnp.concatenate([left, right], axis=1), 0, 0)
        return factor, up

    got_a = swap(jnp.where(first, attn, dq))
    kept_a = jnp.where(first, dq, attn)
    factor_a, up_a = role(kept_a, got_a, low_a, m_a)

    total = p_own + from_r1.astype(F32) + from_l1.astype(F32)
    total = total + jnp.concatenate([from_l2, from_r2], axis=0).astype(F32)
    total = total.astype(BF)
    dk, dv = total[:, :half], total[:, half:]
    got_b = swap(jnp.where(first, dv, dk))
    kept_b = jnp.where(first, dk, dv)
    factor_b, up_b = role(kept_b, got_b, low_b, m_b)

    def mine_first(pair):
        own = lax.dynamic_slice_in_dim(pair, core * rows, rows, 0)
        other = lax.dynamic_slice_in_dim(pair, (1 - core) * rows, rows, 0)
        return own, other

    fa_own, fa_other = mine_first(factor_a)
    fb_own, fb_other = mine_first(factor_b)
    g_a = dot(a_own, fa_own, 0, 0) + dot(a_other, fa_other, 0, 0)
    g_b = dot(x_own, fb_own, 0, 0) + dot(x_other, fb_other, 0, 0)
    g = (jnp.concatenate([g_a, g_b], axis=1) * grad_scale).astype(BF)
    line_rows = 2 * NY * own_cols
    g = jnp.transpose(g.reshape(NZ, NX, line_rows, 2 * rank), (1, 0, 2, 3))
    u_rows = 2 * rank * feats // (NX * NZ * 2 * rank)
    u = (jnp.concatenate([up_a, up_b], axis=0) * grad_scale).astype(BF)
    u = u.reshape(NX, NZ, u_rows, 2 * rank)
    step = exchange(jnp.concatenate([g, u], axis=2), "x")
    step = step.astype(F32).sum(axis=0).astype(BF)
    step = exchange(step, "z")
    step = step.astype(F32).sum(axis=0).astype(BF)
    g_line = step[:line_rows].reshape(2 * NY, own_cols, 2 * rank)
    u_line = jnp.broadcast_to(step[line_rows:][None], (2 * NY, u_rows, 2 * rank))
    step = exchange(jnp.concatenate([g_line, u_line], axis=1), ("y", "c"))
    step = step.reshape(NY, 2, own_cols + u_rows, 2 * rank).astype(F32).sum(axis=0)
    g_out = step[:, :own_cols]
    grad_down = jnp.stack([g_out[0, :, :rank], g_out[0, :, rank:], g_out[1, :, rank:]])
    grad_up_out = g_out[1, :, :rank].T
    u_all = spread(spread(step[:, own_cols:].astype(BF), "z", NZ), "x", NX)
    u_all = jnp.transpose(u_all, (2, 0, 1, 3, 4)).reshape(2, 2, rank, feats).astype(F32)
    grad_up = jnp.stack([u_all[0, 0], u_all[0, 1], u_all[1, 1]])
    grad_down_out = u_all[1, 0].T

    result = jnp.concatenate([dq, dk, dv], axis=1).reshape(2, rows, 3 * half)
    result = exchange(result, "c")
    grad_q, grad_k, grad_v = (
        jnp.concatenate([result[0, :, i * half : (i + 1) * half], result[1, :, i * half : (i + 1) * half]], axis=1)
        for i in range(3)
    )
    return grad_q[None], grad_k[None], grad_v[None], grad_down, grad_up, grad_down_out, grad_up_out


def solution(mesh):
    fine = Mesh(mesh.devices.reshape(NZ, NX, NY, 2), ("z", "x", "y", "c"))
    ctx = ("x", "y", "c")
    every = ("z", "x", "y", "c")
    tokens = P("z", ctx, None)
    return jax.shard_map(
        shards,
        mesh=fine,
        in_specs=(tokens,) * 7 + (P(None, every, None), P(), P(), P(None, every)),
        out_specs=(tokens,) * 3 + (P(None, every, None), P(), P(), P(None, every)),
        check_vma=False,
    )
```

time: 570 us -> 234 us (0.41)
  waiting for transfers between devices: 321 us -> 78.4 us
  blocking collectives: 102 us -> 0 us
  starting transfers between devices: 57.1 us -> 92.2 us
  between operations: 15.5 us -> 1.34 us
  local copies, waits for them, and re-layouts: 38.2 us -> 25.3 us
  matrix products: 24.1 us -> 18.3 us
    psum x1 -> x0, waiting for transfers between devices: 242 us -> none  [shards(): sum_up, sum_down_out = lax.psum((term_up, term_down_out), ('dp', 'ctx'))]
    all_gather x1 -> x0, blocking collectives: 79 us -> none  [shards(): lax.all_gather(up_out, ('dp', 'ctx'), axis=1, tiled=True)]
    all_to_all x2 -> x10, starting transfers between devices: 18.7 us -> 58.2 us  [exchange(): return lax.all_to_all(parts, axes, split_axis=0, concat_axis=0, tiled=True)]
    unnamed x1 -> x0, blocking collectives: 22.8 us -> none
    concatenate x0 -> x4, local copies, waits for them, and re-layouts: none -> 15.8 us  [shards(): g = (jnp.concatenate([g_a, g_b], axis=1) * grad_scale).astype(BF)]
    another operation x20 -> x3, local copies, waits for them, and re-layouts: 14.6 us -> 0.27 us  [the longest x2 4.99 us: shards(): outg_rows.reshape(row_count, size_dp, size_ctx, slice_rows)]
    ppermute x12 -> x13, waiting for transfers between devices: 14.8 us -> 0.83 us  [the longest x3 0.81 us: swap(): return lax.ppermute(block, 'c', [(0, 1), (1, 0)])]
    all_to_all x2 -> x10, waiting for transfers between devices: 64.4 us -> 77.6 us  [exchange(): return lax.all_to_all(parts, axes, split_axis=0, concat_axis=0, tiled=True)]
  transfers between devices with their start and end apart: 17 -> 23, of which waited for: 6 -> 11; matrix products, arithmetic and copies ran while one was open for 12% -> 14% of each run, Pallas kernels for 0% -> 0%
where the time goes in v1:
time: 234 us; the launch traced here: 232 us
  starting transfers between devices  92.2 us (39%)
  waiting for transfers between devices  78.4 us (34%)
  local copies, waits for them, and re-layouts  25.3 us (11%)
  matrix products  18.3 us (8%)
  other arithmetic  12.3 us (5%)
  Pallas kernels  4.4 us (2%)
    all_to_all x10, waiting for transfers between devices, exchange(): return lax.all_to_all(parts, axes, split_axis=0, concat_axis=0, tiled=True)  77.6 us
    all_to_all x10, starting transfers between devices, exchange(): return lax.all_to_all(parts, axes, split_axis=0, concat_axis=0, tiled=True)  58.2 us
    ppermute x8, starting transfers between devices, chip_shift(): lax.ppermute(block, ('x', 'y'), [(i, i + by) for i in range(chips) if 0 <...  19.3 us
    dot_general x14, matrix products, dot(): lax.dot_general(a, b, (((ca,), (cb,)), ((), ())), preferred_element_type=...  18.3 us
    concatenate x4, local copies, waits for them, and re-layouts, shards(): g = (jnp.concatenate([g_a, g_b], axis=1) * grad_scale).astype(BF)  15.8 us
    ppermute x3, starting transfers between devices, swap(): return lax.ppermute(block, 'c', [(0, 1), (1, 0)])  8.08 us
    ppermute x1, starting transfers between devices, shards(): low_out = jnp.where(first, lax.ppermute(low_a, 'c', [(1, 0)]), low_a)  5.29 us
  transfers between devices with their start and end apart: 23, of which 11 were waited for; matrix products, arithmetic and copies ran while one was open for 14% of the time, Pallas kernels for 0%

profile of v1, /device:TPU:1, one launch (start us, length us, event | category | flops | bytes accessed | tf_op | source)
XLA Modules:
  0.0 232.3 jit_solution(3520161806147332006)
XLA Ops:
  0.6 0.8 fusion.78
  1.5 0.8 pad_maximum_fusion.8
  2.3 0.7 broadcast_in_dim.34
  3.0 10.2 %all-to-all-start.1 = ((bf16[16,2,1280]{2,1,0:T(2,128)(2,1)}), bf16[16,2,1280]{2,1,0:T(2,128)(2,1)S(1)}, u32[]{:S(2)}, u32[]{:S(2)}) async-start(bf16[16,2,1280]{2,1,0:T(2,128)(2,1)} %broadcast_in_dim.34), calls=%async_computation.1 | async-start | bytes 163840 | tf_op jit(solution)/shard_map/all_to_all | solution.py:92
  13.1 1.1 pad_maximum_fusion.2
  14.4 0.8 pad_maximum_fusion.1
  15.2 6.1 %all-to-all-done.1 = bf16[16,2,1280]{2,1,0:T(2,128)(2,1)S(1)} async-done(((bf16[16,2,1280]{2,1,0:T(2,128)(2,1)}), bf16[16,2,1280]{2,1,0:T(2,128)(2,1)S(1)}, u32[]{:S(2)}, u32[]{:S(2)}) %all-to-all-start.1) | async-done | bytes 81952 | tf_op jit(solution)/shard_map/all_to_all | solution.py:92
  21.3 3.5 %all-to-all-start = ((bf16[2,528,256]{2,1,0:T(8,128)(2,1)}), bf16[2,528,256]{2,1,0:T(8,128)(2,1)S(1)}, u32[]{:S(2)}, u32[]{:S(2)}) async-start(bf16[2,528,256]{2,1,0:T(8,128)(2,1)} %pad_maximum_fusion.1), calls=%async_computation | async-start | bytes 1081344 | tf_op jit(solution)/shard_map/all_to_all | solution.py:92
  24.9 1.3 all-to-all-done
  26.2 0.8 broadcast_in_dim.35
  27.0 8.6 %all-to-all-start.2 = ((bf16[8,160,128]{2,1,0:T(8,128)(2,1)}), bf16[8,160,128]{2,1,0:T(8,128)(2,1)S(1)}, u32[]{:S(2)}, u32[]{:S(2)}) async-start(bf16[8,160,128]{2,1,0:T(8,128)(2,1)} %broadcast_in_dim.35), calls=%async_computation.2 | async-start | bytes 655360 | tf_op jit(solution)/shard_map/all_to_all | solution.py:92
  35.6 1.3 collective-permute-start.2
  36.9 4.0 %collective-permute-start.1 = (bf16[256,512]{1,0:T(8,128)(2,1)S(1)}, bf16[256,512]{1,0:T(8,128)(2,1)S(1)}, u32[]{:S(2)}, u32[]{:S(2)}) collective-permute-start(bf16[256,512]{1,0:T(8,128)(2,1)S(1)} %bitcast.118), channel_id=1, source_target_pairs={{0,2},{2,4},{4,6},{6,8},{8,10},{10,12},{12,14},{14,16},{16,18},{18... | collective-permute-start | bytes 786440 | tf_op jit(solution)/shard_map/ppermute | solution.py:105
  41.0 1.3 collective-permute-start.3
  42.3 3.1 %collective-permute-start.4 = (bf16[128,5120]{1,0:T(8,128)(2,1)}, bf16[128,5120]{1,0:T(8,128)(2,1)}, u32[]{:S(2)}, u32[]{:S(2)}) collective-permute-start(bf16[128,5120]{1,0:T(8,128)(2,1)} %bitcast.12), channel_id=1, source_target_pairs={{0,1},{1,0},{2,3},{3,2},{4,5},{5,4},{6,7},{7,6},{8,9},{9,8},{10,11... | collective-permute-start | bytes 3932168 | tf_op jit(solution)/shard_map/ppermute | solution.py:100
  45.4 1.3 collective-permute-start.5
  47.0 2.2 all-to-all-done.2
  49.2 1.3 broadcast_in_dim.36
  50.5 4.4 %all-to-all-start.3 = ((bf16[4,8,160,128]{3,2,1,0:T(8,128)(2,1)}), bf16[4,8,160,128]{3,2,1,0:T(8,128)(2,1)}, u32[]{:S(2)}, u32[]{:S(2)}) async-start(bf16[4,8,160,128]{3,2,1,0:T(8,128)(2,1)} %broadcast_in_dim.36), calls=%async_computation.3 | async-start | bytes 2621440 | tf_op jit(solution)/shard_map/all_to_all | solution.py:92
  55.3 16.2 %all-to-all-done.3 = bf16[4,8,160,128]{3,2,1,0:T(8,128)(2,1)} async-done(((bf16[4,8,160,128]{3,2,1,0:T(8,128)(2,1)}), bf16[4,8,160,128]{3,2,1,0:T(8,128)(2,1)}, u32[]{:S(2)}, u32[]{:S(2)}) %all-to-all-start.3) | async-done | bytes 1310752 | tf_op jit(solution)/shard_map/all_to_all | solution.py:92
  71.5 1.4 copy.153
  72.9 2.3 %fusion.13 = bf16[128,64]{1,0:T(8,128)(2,1)S(1)} fusion(bf16[5120,128]{1,0:T(8,128)(2,1)S(1)} %bitcast.122, pred[]{:T(512)S(6)} %eq.16, bf16[1,128,5120]{2,1,0:T(8,128)(2,1)} %param.16, bf16[1,128,5120]{2,1,0:T(8,128)(2,1)} %param.11), kind=kOutput, calls=%fused_computation.21 | convolution fusion | flops 84549632 | bytes 3948545 | tf_op jit(solution)/shard_map/dot_general | solution.py:24
  75.2 2.2 collective-permute-start
  77.5 1.9 fusion.16
  79.4 5.3 %collective-permute-start.6 = (bf16[256,64]{1,0:T(8,128)(2,1)S(1)}, bf16[256,64]{1,0:T(8,128)(2,1)S(1)}, u32[]{:S(2)}, u32[]{:S(2)}) collective-permute-start(bf16[256,64]{1,0:T(8,128)(2,1)S(1)} %maximum_select_fusion), channel_id=1, source_target_pairs={{1,0},{3,2},{5,4},{7,6},{9,8},{11,10},{13,12},{15,14},{17,16},{19,... | collective-permute-start | bytes 98312 | tf_op jit(solution)/shard_map/ppermute | solution.py:166
  84.7 2.3 fusion.19
  87.1 4.4 %attention.1 = (bf16[256,256]{1,0:T(8,128)(2,1)S(1)}, bf16[256,256]{1,0:T(8,128)(2,1)S(1)}, bf16[128,512]{1,0:T(8,128)(2,1)S(1)}, bf16[256,512]{1,0:T(8,128)(2,1...) custom-call(bf16[256,256]{1,0:T(8,128)(2,1)S(1)} %bitcast.121, ...), custom_call_target="tpu_custom_call" | custom-call | flops 1400000000 | bytes 4000000 | tf_op jit(solution)/shard_map/attention/pallas_call | solution.py:80
  91.6 1.9 collective-permute-start.11
  93.5 2.3 fusion.22
  96.0 3.5 %collective-permute-start.9 = (bf16[128,512]{1,0:T(8,128)(2,1)S(1)}, bf16[128,512]{1,0:T(8,128)(2,1)S(1)}, u32[]{:S(2)}, u32[]{:S(2)}) collective-permute-start(bf16[128,512]{1,0:T(8,128)(2,1)S(1)} %get-tuple-element.18), channel_id=1, source_target_pairs={{0,4},{2,6},{4,8},{6,10},{8,12},{10,14},{12,16},{14,18},{16,20},{1... | collective-permute-start | bytes 393224 | tf_op jit(solution)/shard_map/ppermute | solution.py:105
  99.6 1.3 collective-permute-start.10
  100.9 1.3 collective-permute-start.7
  102.2 4.4 %collective-permute-start.8 = (bf16[256,512]{1,0:T(8,128)(2,1)S(1)}, bf16[256,512]{1,0:T(8,128)(2,1)S(1)}, u32[]{:S(2)}, u32[]{:S(2)}) collective-permute-start(bf16[256,512]{1,0:T(8,128)(2,1)S(1)} %get-tuple-element.17), channel_id=1, source_target_pairs={{0,2},{2,4},{4,6},{6,8},{8,10},{10,12},{12,14},{14,16},{16,18},{18... | collective-permute-start | bytes 786440 | tf_op jit(solution)/shard_map/ppermute | solution.py:105
  107.0 2.2 fusion.25
  109.1 2.9 %convolution_add_fusion = f32[5120,64]{0,1:T(8,128)} fusion(f32[5120,64]{0,1:T(8,128)S(1)} %fusion.25, bf16[128,5120]{1,0:T(8,128)(2,1)} %collective-permute-done.4, bf16[128,5120]{1,0:T(8,128)(2,1)} %collective-permute-done.5, pred[]{:T(512)S(6)} %eq.16, bf16[256,64]{0,1:T(8,128)(2,1)S(1)} %fusion.11, s32[]{:T(128)S(6)} %select_n.117), kind=kOutput, calls=%fused_computation | convolution fusion | flops 84869120 | bytes 5259269 | tf_op jit(solution)/shard_map/dot_general | solution.py:24
  112.0 4.0 %concatenate.76 = f32[8,4,160,64]{2,1,0,3:T(4,128)} reshape(f32[5120,64]{0,1:T(8,128)} %convolution_add_fusion) | data formatting | bytes 2621440 | tf_op jit(solution)/shard_map/concatenate | solution.py:212
  116.0 4.2 %copy.158 = f32[8,4,160,64]{3,2,0,1:T(8,128)} copy(f32[8,4,160,64]{2,1,0,3:T(4,128)} %concatenate.76) | data formatting | bytes 2621440 | tf_op jit(solution)/shard_map/concatenate | solution.py:212
  120.6 3.0 %collective-permute-start.12 = (bf16[256,256]{1,0:T(8,128)(2,1)S(1)}, bf16[256,256]{1,0:T(8,128)(2,1)S(1)}, u32[]{:S(2)}, u32[]{:S(2)}) collective-permute-start(bf16[256,256]{1,0:T(8,128)(2,1)S(1)} %broadcast_select_fusion.10), channel_id=1, source_target_pairs={{0,1},{1,0},{2,3},{3,2},{4,5},{5,4},{6,7},{7,6},{8,9},{9,8},{10,11... | collective-permute-start | bytes 393224 | tf_op jit(solution)/shard_map/ppermute | solution.py:100
  123.8 0.8 collective-permute-done.12
  125.1 1.7 fusion.54
  126.8 1.7 fusion
  128.5 3.2 %concatenate.77 = f32[8,4,160,64]{2,1,0,3:T(4,128)} reshape(f32[5120,64]{0,1:T(8,128)S(1)} %fusion) | data formatting | bytes 2621440 | tf_op jit(solution)/shard_map/concatenate | solution.py:212
  131.7 4.4 %copy.159 = f32[8,4,160,64]{3,2,0,1:T(8,128)} copy(f32[8,4,160,64]{2,1,0,3:T(4,128)} %concatenate.77) | data formatting | bytes 2621440 | tf_op jit(solution)/shard_map/concatenate | solution.py:212
  136.1 2.5 %fusion.2 = bf16[4,8,160,128]{3,2,1,0:T(8,128)(2,1)S(1)} fusion(f32[8,4,160,64]{3,2,0,1:T(8,128)} %copy.159, f32[8,4,160,64]{3,2,0,1:T(8,128)S(1)} %copy-done), kind=kLoop, calls=%fused_computation.6 | loop fusion | flops 1966080 | bytes 3932160 | tf_op jit(solution)/shard_map/transpose | solution.py:214
  138.6 1.2 pad_maximum_fusion
  139.8 7.0 %all-to-all-start.5 = ((bf16[4,8,176,128]{3,2,1,0:T(8,128)(2,1)}), bf16[4,8,176,128]{3,2,1,0:T(8,128)(2,1)S(1)}, u32[]{:S(2)}, u32[]{:S(2)}) async-start(bf16[4,8,176,128]{3,2,1,0:T(8,128)(2,1)} %pad_maximum_fusion), calls=%async_computation.5 | async-start | bytes 2883584 | tf_op jit(solution)/shard_map/all_to_all | solution.py:92
  146.8 0.8 pad_maximum_fusion.3
  147.5 18.0 %all-to-all-done.5 = bf16[4,8,176,128]{3,2,1,0:T(8,128)(2,1)S(1)} async-done(((bf16[4,8,176,128]{3,2,1,0:T(8,128)(2,1)}), bf16[4,8,176,128]{3,2,1,0:T(8,128)(2,1)S(1)}, u32[]{:S(2)}, u32[]{:S(2)}) %all-to-all-start.5) | async-done | bytes 1441824 | tf_op jit(solution)/shard_map/all_to_all | solution.py:92
  165.5 5.0 %all-to-all-start.4 = ((bf16[2,128,768]{2,1,0:T(8,128)(2,1)}), bf16[2,128,768]{2,1,0:T(8,128)(2,1)S(1)}, u32[]{:S(2)}, u32[]{:S(2)}) async-start(bf16[2,128,768]{2,1,0:T(8,128)(2,1)} %bitcast.21), calls=%async_computation.4 | async-start | bytes 786432 | tf_op jit(solution)/shard_map/all_to_all | solution.py:92
  170.5 1.0 reduce_sum.33
  171.8 6.6 %all-to-all-start.6 = ((bf16[8,176,128]{2,1,0:T(8,128)(2,1)}), bf16[8,176,128]{2,1,0:T(8,128)(2,1)S(1)}, u32[]{:S(2)}, u32[]{:S(2)}) async-start(bf16[8,176,128]{2,1,0:T(8,128)(2,1)} %reduce_sum.33), calls=%async_computation.6 | async-start | bytes 720896 | tf_op jit(solution)/shard_map/all_to_all | solution.py:92
  178.4 14.4 %all-to-all-done.6 = bf16[8,176,128]{2,1,0:T(8,128)(2,1)S(1)} async-done(((bf16[8,176,128]{2,1,0:T(8,128)(2,1)}), bf16[8,176,128]{2,1,0:T(8,128)(2,1)S(1)}, u32[]{:S(2)}, u32[]{:S(2)}) %all-to-all-start.6) | async-done | bytes 360480 | tf_op jit(solution)/shard_map/all_to_all | solution.py:92
  192.9 0.7 pad_maximum_fusion.6
  193.6 6.3 %all-to-all-start.7 = ((bf16[16,26,128]{2,1,0:T(8,128)(2,1)}), bf16[16,26,128]{2,1,0:T(8,128)(2,1)S(1)}, u32[]{:S(2)}, u32[]{:S(2)}) async-start(bf16[16,26,128]{2,1,0:T(8,128)(2,1)} %pad_maximum_fusion.6), calls=%async_computation.7 | async-start | bytes 262144 | tf_op jit(solution)/shard_map/all_to_all | solution.py:92
  199.8 0.7 maximum_bitcast_fusion.2
  201.2 7.8 %all-to-all-done.7 = bf16[16,26,128]{2,1,0:T(8,128)(2,1)S(1)} async-done(((bf16[16,26,128]{2,1,0:T(8,128)(2,1)}), bf16[16,26,128]{2,1,0:T(8,128)(2,1)S(1)}, u32[]{:S(2)}, u32[]{:S(2)}) %all-to-all-start.7) | async-done | bytes 106528 | tf_op jit(solution)/shard_map/all_to_all | solution.py:92
  209.8 3.4 %all-to-all-start.8 = ((bf16[8,2,16,128]{3,2,1,0:T(8,128)(2,1)}), bf16[8,2,16,128]{3,2,1,0:T(8,128)(2,1)S(1)}, u32[]{:S(2)}, u32[]{:S(2)}) async-start(bf16[8,2,16,128]{3,2,1,0:T(8,128)(2,1)} %broadcast_in_dim.77), calls=%async_computation.8 | async-start | bytes 131072 | tf_op jit(solution)/shard_map/all_to_all | solution.py:92
  213.2 0.7 maximum_bitcast_fusion
  213.8 7.1 %all-to-all-done.8 = bf16[8,2,16,128]{3,2,1,0:T(8,128)(2,1)S(1)} async-done(((bf16[8,2,16,128]{3,2,1,0:T(8,128)(2,1)}), bf16[8,2,16,128]{3,2,1,0:T(8,128)(2,1)S(1)}, u32[]{:S(2)}, u32[]{:S(2)}) %all-to-all-start.8) | async-done | bytes 65568 | tf_op jit(solution)/shard_map/all_to_all | solution.py:92
  220.9 0.7 broadcast_in_dim.78
  221.6 3.4 %all-to-all-start.9 = ((bf16[4,8,2,16,128]{4,3,1,2,0:T(8,128)(2,1)}), bf16[4,8,2,16,128]{4,3,1,2,0:T(8,128)(2,1)S(1)}, u32[]{:S(2)}, u32[]{:S(2)}) async-start(bf16[4,8,2,16,128]{4,3,1,2,0:T(8,128)(2,1)} %broadcast_in_dim.78), calls=%async_computation.9 | async-start | bytes 524288 | tf_op jit(solution)/shard_map/all_to_all | solution.py:92
  226.4 4.3 %all-to-all-done.9 = bf16[4,8,2,16,128]{4,3,1,2,0:T(8,128)(2,1)S(1)} async-done(((bf16[4,8,2,16,128]{4,3,1,2,0:T(8,128)(2,1)}), bf16[4,8,2,16,128]{4,3,1,2,0:T(8,128)(2,1)S(1)}, u32[]{:S(2)}, u32[]{:S(2)}) %all-to-all-start.9) | async-done | bytes 262176 | tf_op jit(solution)/shard_map/all_to_all | solution.py:92
  230.8 0.7 slice_bitcast_fusion.2
  231.5 0.8 pad_maximum_fusion.4
  (85 shorter events, 5.7 us)
Async XLA Ops:
  0.6 13.7 %copy-start.3 = (s32[1,4,12]{2,1,0:T(4,128)S(1)}, s32[1,4,12]{2,1,0:T(4,128)}, u32[]{:S(2)}) copy-start(s32[1,4,12]{2,1,0:T(4,128)} %param.17) | copy-start | bytes 580
  3.0 18.4 %all-to-all-start.1 = ((bf16[16,2,1280]{2,1,0:T(2,128)(2,1)}), bf16[16,2,1280]{2,1,0:T(2,128)(2,1)S(1)}, u32[]{:S(2)}, u32[]{:S(2)}) async-start(bf16[16,2,1280]{2,1,0:T(2,128)(2,1)} %broadcast_in_dim.34), calls=%async_computation.1 | async-start | bytes 163840 | tf_op jit(solution)/shard_map/all_to_all | solution.py:92
  21.3 4.9 %all-to-all-start = ((bf16[2,528,256]{2,1,0:T(8,128)(2,1)}), bf16[2,528,256]{2,1,0:T(8,128)(2,1)S(1)}, u32[]{:S(2)}, u32[]{:S(2)}) async-start(bf16[2,528,256]{2,1,0:T(8,128)(2,1)} %pad_maximum_fusion.1), calls=%async_computation | async-start | bytes 1081344 | tf_op jit(solution)/shard_map/all_to_all | solution.py:92
  27.0 19.7 %copy-start.2 = (bf16[512,64]{0,1:T(8,128)(2,1)S(1)}, bf16[512,64]{0,1:T(8,128)(2,1)}, u32[]{:S(2)}) copy-start(bf16[512,64]{0,1:T(8,128)(2,1)} %param.20) | copy-start | bytes 196612
  27.0 22.2 %all-to-all-start.2 = ((bf16[8,160,128]{2,1,0:T(8,128)(2,1)}), bf16[8,160,128]{2,1,0:T(8,128)(2,1)S(1)}, u32[]{:S(2)}, u32[]{:S(2)}) async-start(bf16[8,160,128]{2,1,0:T(8,128)(2,1)} %broadcast_in_dim.35), calls=%async_computation.2 | async-start | bytes 655360 | tf_op jit(solution)/shard_map/all_to_all | solution.py:92
  35.6 51.5 %collective-permute-start.2 = (bf16[256,512]{1,0:T(8,128)(2,1)S(1)}, bf16[256,512]{1,0:T(8,128)(2,1)S(1)}, u32[]{:S(2)}, u32[]{:S(2)}) collective-permute-start(bf16[256,512]{1,0:T(8,128)(2,1)S(1)} %bitcast.117), channel_id=1, source_target_pairs={{2,0},{4,2},{6,4},{8,6},{10,8},{12,10},{14,12},{16,14},{18,16},{20... | collective-permute-start | bytes 786440 | tf_op jit(solution)/shard_map/ppermute | solution.py:105
  36.9 50.2 %collective-permute-start.1 = (bf16[256,512]{1,0:T(8,128)(2,1)S(1)}, bf16[256,512]{1,0:T(8,128)(2,1)S(1)}, u32[]{:S(2)}, u32[]{:S(2)}) collective-permute-start(bf16[256,512]{1,0:T(8,128)(2,1)S(1)} %bitcast.118), channel_id=1, source_target_pairs={{0,2},{2,4},{4,6},{6,8},{8,10},{10,12},{12,14},{14,16},{16,18},{18... | collective-permute-start | bytes 786440 | tf_op jit(solution)/shard_map/ppermute | solution.py:105
  41.0 46.1 %collective-permute-start.3 = (bf16[128,512]{1,0:T(8,128)(2,1)S(1)}, bf16[128,512]{1,0:T(8,128)(2,1)S(1)}, u32[]{:S(2)}, u32[]{:S(2)}) collective-permute-start(bf16[128,512]{1,0:T(8,128)(2,1)S(1)} %get-tuple-element.104), channel_id=1, source_target_pairs={{4,0},{6,2},{8,4},{10,6},{12,8},{14,10},{16,12},{18,14},{20,16},{2... | collective-permute-start | bytes 393224 | tf_op jit(solution)/shard_map/ppermute | solution.py:105
  42.3 32.9 %collective-permute-start.4 = (bf16[128,5120]{1,0:T(8,128)(2,1)}, bf16[128,5120]{1,0:T(8,128)(2,1)}, u32[]{:S(2)}, u32[]{:S(2)}) collective-permute-start(bf16[128,5120]{1,0:T(8,128)(2,1)} %bitcast.12), channel_id=1, source_target_pairs={{0,1},{1,0},{2,3},{3,2},{4,5},{5,4},{6,7},{7,6},{8,9},{9,8},{10,11... | collective-permute-start | bytes 3932168 | tf_op jit(solution)/shard_map/ppermute | solution.py:100
  45.4 32.0 %collective-permute-start.5 = (bf16[128,5120]{1,0:T(8,128)(2,1)}, bf16[128,5120]{1,0:T(8,128)(2,1)}, u32[]{:S(2)}, u32[]{:S(2)}) collective-permute-start(bf16[128,5120]{1,0:T(8,128)(2,1)} %bitcast.13), channel_id=1, source_target_pairs={{0,1},{2,3},{4,5},{6,7},{8,9},{10,11},{12,13},{14,15},{16,17},{18,... | collective-permute-start | bytes 3932168 | tf_op jit(solution)/shard_map/ppermute | solution.py:148
  50.5 4.8 %copy-start.1 = (bf16[3,64,512]{2,1,0:T(8,128)(2,1)S(1)}, bf16[3,64,512]{2,1,0:T(8,128)(2,1)}, u32[]{:S(2)}) copy-start(bf16[3,64,512]{2,1,0:T(8,128)(2,1)} %param.19) | copy-start | bytes 589828
  50.5 21.0 %all-to-all-start.3 = ((bf16[4,8,160,128]{3,2,1,0:T(8,128)(2,1)}), bf16[4,8,160,128]{3,2,1,0:T(8,128)(2,1)}, u32[]{:S(2)}, u32[]{:S(2)}) async-start(bf16[4,8,160,128]{3,2,1,0:T(8,128)(2,1)} %broadcast_in_dim.36), calls=%async_computation.3 | async-start | bytes 2621440 | tf_op jit(solution)/shard_map/all_to_all | solution.py:92
  75.2 11.9 %collective-permute-start = (bf16[128,512]{1,0:T(8,128)(2,1)S(1)}, bf16[128,512]{1,0:T(8,128)(2,1)S(1)}, u32[]{:S(2)}, u32[]{:S(2)}) collective-permute-start(bf16[128,512]{1,0:T(8,128)(2,1)S(1)} %get-tuple-element.105), channel_id=1, source_target_pairs={{0,4},{2,6},{4,8},{6,10},{8,12},{10,14},{12,16},{14,18},{16,20},{1... | collective-permute-start | bytes 393224 | tf_op jit(solution)/shard_map/ppermute | solution.py:105
  79.4 7.6 %collective-permute-start.6 = (bf16[256,64]{1,0:T(8,128)(2,1)S(1)}, bf16[256,64]{1,0:T(8,128)(2,1)S(1)}, u32[]{:S(2)}, u32[]{:S(2)}) collective-permute-start(bf16[256,64]{1,0:T(8,128)(2,1)S(1)} %maximum_select_fusion), channel_id=1, source_target_pairs={{1,0},{3,2},{5,4},{7,6},{9,8},{11,10},{13,12},{15,14},{17,16},{19,... | collective-permute-start | bytes 98312 | tf_op jit(solution)/shard_map/ppermute | solution.py:166
  91.6 15.0 %collective-permute-start.11 = (bf16[256,256]{1,0:T(8,128)(2,1)S(1)}, bf16[256,256]{1,0:T(8,128)(2,1)S(1)}, u32[]{:S(2)}, u32[]{:S(2)}) collective-permute-start(bf16[256,256]{1,0:T(8,128)(2,1)S(1)} %broadcast_select_fusion.12), channel_id=1, source_target_pairs={{0,1},{1,0},{2,3},{3,2},{4,5},{5,4},{6,7},{7,6},{8,9},{9,8},{10,11... | collective-permute-start | bytes 393224 | tf_op jit(solution)/shard_map/ppermute | solution.py:100
  96.0 24.4 %collective-permute-start.9 = (bf16[128,512]{1,0:T(8,128)(2,1)S(1)}, bf16[128,512]{1,0:T(8,128)(2,1)S(1)}, u32[]{:S(2)}, u32[]{:S(2)}) collective-permute-start(bf16[128,512]{1,0:T(8,128)(2,1)S(1)} %get-tuple-element.18), channel_id=1, source_target_pairs={{0,4},{2,6},{4,8},{6,10},{8,12},{10,14},{12,16},{14,18},{16,20},{1... | collective-permute-start | bytes 393224 | tf_op jit(solution)/shard_map/ppermute | solution.py:105
  99.6 20.8 %collective-permute-start.10 = (bf16[128,512]{1,0:T(8,128)(2,1)S(1)}, bf16[128,512]{1,0:T(8,128)(2,1)S(1)}, u32[]{:S(2)}, u32[]{:S(2)}) collective-permute-start(bf16[128,512]{1,0:T(8,128)(2,1)S(1)} %get-tuple-element.19), channel_id=1, source_target_pairs={{4,0},{6,2},{8,4},{10,6},{12,8},{14,10},{16,12},{18,14},{20,16},{2... | collective-permute-start | bytes 393224 | tf_op jit(solution)/shard_map/ppermute | solution.py:105
  100.9 19.5 %collective-permute-start.7 = (bf16[256,512]{1,0:T(8,128)(2,1)S(1)}, bf16[256,512]{1,0:T(8,128)(2,1)S(1)}, u32[]{:S(2)}, u32[]{:S(2)}) collective-permute-start(bf16[256,512]{1,0:T(8,128)(2,1)S(1)} %get-tuple-element.16), channel_id=1, source_target_pairs={{2,0},{4,2},{6,4},{8,6},{10,8},{12,10},{14,12},{16,14},{18,16},{20... | collective-permute-start | bytes 786440 | tf_op jit(solution)/shard_map/ppermute | solution.py:105
  102.2 18.2 %collective-permute-start.8 = (bf16[256,512]{1,0:T(8,128)(2,1)S(1)}, bf16[256,512]{1,0:T(8,128)(2,1)S(1)}, u32[]{:S(2)}, u32[]{:S(2)}) collective-permute-start(bf16[256,512]{1,0:T(8,128)(2,1)S(1)} %get-tuple-element.17), channel_id=1, source_target_pairs={{0,2},{2,4},{4,6},{6,8},{8,10},{10,12},{12,14},{14,16},{16,18},{18... | collective-permute-start | bytes 786440 | tf_op jit(solution)/shard_map/ppermute | solution.py:105
  120.6 4.0 %collective-permute-start.12 = (bf16[256,256]{1,0:T(8,128)(2,1)S(1)}, bf16[256,256]{1,0:T(8,128)(2,1)S(1)}, u32[]{:S(2)}, u32[]{:S(2)}) collective-permute-start(bf16[256,256]{1,0:T(8,128)(2,1)S(1)} %broadcast_select_fusion.10), channel_id=1, source_target_pairs={{0,1},{1,0},{2,3},{3,2},{4,5},{5,4},{6,7},{7,6},{8,9},{9,8},{10,11... | collective-permute-start | bytes 393224 | tf_op jit(solution)/shard_map/ppermute | solution.py:100
  131.7 4.4 %copy-start = (f32[8,4,160,64]{3,2,0,1:T(8,128)S(1)}, f32[8,4,160,64]{3,2,0,1:T(8,128)}, u32[]{:S(2)}) copy-start(f32[8,4,160,64]{3,2,0,1:T(8,128)} %copy.158) | copy-start | bytes 3932164
  139.8 25.7 %all-to-all-start.5 = ((bf16[4,8,176,128]{3,2,1,0:T(8,128)(2,1)}), bf16[4,8,176,128]{3,2,1,0:T(8,128)(2,1)S(1)}, u32[]{:S(2)}, u32[]{:S(2)}) async-start(bf16[4,8,176,128]{3,2,1,0:T(8,128)(2,1)} %pad_maximum_fusion), calls=%async_computation.5 | async-start | bytes 2883584 | tf_op jit(solution)/shard_map/all_to_all | solution.py:92
  165.5 6.3 %all-to-all-start.4 = ((bf16[2,128,768]{2,1,0:T(8,128)(2,1)}), bf16[2,128,768]{2,1,0:T(8,128)(2,1)S(1)}, u32[]{:S(2)}, u32[]{:S(2)}) async-start(bf16[2,128,768]{2,1,0:T(8,128)(2,1)} %bitcast.21), calls=%async_computation.4 | async-start | bytes 786432 | tf_op jit(solution)/shard_map/all_to_all | solution.py:92
  171.8 21.0 %all-to-all-start.6 = ((bf16[8,176,128]{2,1,0:T(8,128)(2,1)}), bf16[8,176,128]{2,1,0:T(8,128)(2,1)S(1)}, u32[]{:S(2)}, u32[]{:S(2)}) async-start(bf16[8,176,128]{2,1,0:T(8,128)(2,1)} %reduce_sum.33), calls=%async_computation.6 | async-start | bytes 720896 | tf_op jit(solution)/shard_map/all_to_all | solution.py:92
  193.6 15.4 %all-to-all-start.7 = ((bf16[16,26,128]{2,1,0:T(8,128)(2,1)}), bf16[16,26,128]{2,1,0:T(8,128)(2,1)S(1)}, u32[]{:S(2)}, u32[]{:S(2)}) async-start(bf16[16,26,128]{2,1,0:T(8,128)(2,1)} %pad_maximum_fusion.6), calls=%async_computation.7 | async-start | bytes 262144 | tf_op jit(solution)/shard_map/all_to_all | solution.py:92
  209.8 11.1 %all-to-all-start.8 = ((bf16[8,2,16,128]{3,2,1,0:T(8,128)(2,1)}), bf16[8,2,16,128]{3,2,1,0:T(8,128)(2,1)S(1)}, u32[]{:S(2)}, u32[]{:S(2)}) async-start(bf16[8,2,16,128]{3,2,1,0:T(8,128)(2,1)} %broadcast_in_dim.77), calls=%async_computation.8 | async-start | bytes 131072 | tf_op jit(solution)/shard_map/all_to_all | solution.py:92
  221.6 9.0 %all-to-all-start.9 = ((bf16[4,8,2,16,128]{4,3,1,2,0:T(8,128)(2,1)}), bf16[4,8,2,16,128]{4,3,1,2,0:T(8,128)(2,1)S(1)}, u32[]{:S(2)}, u32[]{:S(2)}) async-start(bf16[4,8,2,16,128]{4,3,1,2,0:T(8,128)(2,1)} %broadcast_in_dim.78), calls=%async_computation.9 | async-start | bytes 524288 | tf_op jit(solution)/shard_map/all_to_all | solution.py:92

commit v2 on v1

v2 whole, which is shorter than its diff:
```python
import math

import jax
import jax.numpy as jnp
from jax import lax
from jax.experimental import pallas as pl
from jax.experimental.pallas import tpu as pltpu
from jax.sharding import Mesh, PartitionSpec as P

HDIM = 128
BLK = 32
BLK_DEV = 4
NX, NY, NZ = 4, 8, 8
STRENGTH = 2.0
SCALING = HDIM**-0.5
MASKED = -1e30
BF = jnp.bfloat16
F32 = jnp.float32

SEGMENTS = ((0, 128), (128, 384), (384, 640), (640, 896), (896, 1024))


def dot(a, b, ca, cb):
    return lax.dot_general(a, b, (((ca,), (cb,)), ((), ())), preferred_element_type=F32)


def attention_kernel(
    core_ref, q_ref, l2_ref, l1_ref, own_ref, r1_ref, r2_ref, fog_ref, low_ref, odp_ref, bias_ref,
    kept_ref, send_ref, dq_ref, pl2_ref, pl1_ref, pown_ref, pr1_ref, pr2_ref, attn_ref,
):
    kv_refs = (l2_ref, l1_ref, own_ref, r1_ref, r2_ref)
    part_refs = (pl2_ref, pl1_ref, pown_ref, pr1_ref, pr2_ref)
    rows, half = q_ref.shape
    low_out = low_ref[1][:, : odp_ref.shape[1]]
    dout = (fog_ref[...].astype(F32) + STRENGTH * dot(low_out, odp_ref[...], 1, 1)).astype(BF)
    bias = bias_ref[...]
    for head in range(half // HDIM):
        cols = slice(head * HDIM, (head + 1) * HDIM)
        vcols = slice(half + head * HDIM, half + (head + 1) * HDIM)
        q = q_ref[:, cols]
        dout_h = dout[:, cols]
        keys = [ref[:, cols] for ref in kv_refs]
        vals = [ref[:, vcols] for ref in kv_refs]
        scores = []
        for k, (a, b) in zip(keys, SEGMENTS):
            s = dot(q, k, 1, 1) * SCALING
            s = s.reshape(8, BLK, b - a) + bias[:, None, a:b]
            scores.append(s.reshape(8 * BLK, b - a))
        top = scores[0].max(axis=1, keepdims=True)
        for s in scores[1:]:
            top = jnp.maximum(top, s.max(axis=1, keepdims=True))
        weights = [jnp.exp(s - top) for s in scores]
        total = weights[0].sum(axis=1, keepdims=True)
        for w in weights[1:]:
            total = total + w.sum(axis=1, keepdims=True)
        inverse = 1.0 / total
        probs = [w * inverse for w in weights]
        probs_low = [p.astype(BF) for p in probs]
        attn = dot(probs_low[0], vals[0], 1, 0)
        for p, v in zip(probs_low[1:], vals[1:]):
            attn = attn + dot(p, v, 1, 0)
        attn = attn.astype(BF)
        attn_ref[:, cols] = attn
        delta = (dout_h.astype(F32) * attn.astype(F32)).sum(axis=1, keepdims=True)
        dq = None
        for k, v, p, p_low, out in zip(keys, vals, probs, probs_low, part_refs):
            dscore = (p * (dot(dout_h, v, 1, 1) - delta)).astype(BF)
            term = dot(dscore, k, 1, 0)
            dq = term if dq is None else dq + term
            out[:, cols] = (dot(dscore, q, 0, 0) * SCALING).astype(out.dtype)
            out[:, vcols] = dot(p_low, dout_h, 0, 0).astype(out.dtype)
        dq_ref[:, cols] = (dq * SCALING).astype(BF)

    @pl.when(core_ref[0] == 0)
    def _():
        kept_ref[...] = dq_ref[...]
        send_ref[:rows] = attn_ref[...]

    @pl.when(core_ref[0] != 0)
    def _():
        kept_ref[...] = attn_ref[...]
        send_ref[:rows] = dq_ref[...]

    send_ref[rows:] = dq_ref[rows // 2 :]


def attention(core, q, windows, fog, low, odp_half, bias):
    rows, half = q.shape
    shape = jax.ShapeDtypeStruct
    outs = [shape((rows, half), BF), shape((rows + rows // 2, half), BF), shape((rows, half), BF)]
    outs += [shape((b - a, 2 * half), F32 if i == 2 else BF) for i, (a, b) in enumerate(SEGMENTS)]
    vmem = pl.BlockSpec(memory_space=pltpu.VMEM)
    return pl.pallas_call(
        attention_kernel,
        out_shape=outs,
        in_specs=[pl.BlockSpec(memory_space=pltpu.SMEM)] + [vmem] * 10,
        out_specs=[vmem] * 8,
        scratch_shapes=[pltpu.VMEM((rows, half), BF)],
        compiler_params=pltpu.CompilerParams(vmem_limit_bytes=40 * 1024 * 1024),
        cost_estimate=pl.CostEstimate(flops=1_400_000_000, bytes_accessed=4_000_000, transcendentals=524288),
        name="attention",
    )(core, q, *windows, fog, low, odp_half, bias)


Z_STEP = 2


def low_kernel(core_ref, xo_ref, xt_ref, yo_ref, yt_ref, w_ref, low_ref, own_acc, other_acc):
    core = core_ref[0]
    step = pl.program_id(0)
    rows = xo_ref.shape[0]
    ranks = w_ref.shape[3]
    block = NX * w_ref.shape[2]

    @pl.when(step == 0)
    def _():
        own_acc[...] = jnp.zeros_like(own_acc)
        other_acc[...] = jnp.zeros_like(other_acc)

    lane = lax.broadcasted_iota(jnp.int32, (rows, ranks), 1)
    from_y = (lane < ranks // 2) & (core == 1)
    for zz in range(Z_STEP):
        cols = slice(zz * block, (zz + 1) * block)
        w = jnp.concatenate([w_ref[i, zz] for i in range(NX)], axis=0)
        for x_ref, y_ref, acc in ((xo_ref, yo_ref, own_acc), (xt_ref, yt_ref, other_acc)):
            acc[...] += jnp.where(from_y, dot(y_ref[:, cols], w, 1, 0), dot(x_ref[:, cols], w, 1, 0))

    @pl.when(step == pl.num_programs(0) - 1)
    def _():
        low_ref[pl.ds(pl.multiple_of(core * rows, rows), rows)] = own_acc[...].astype(BF)
        low_ref[pl.ds(pl.multiple_of((1 - core) * rows, rows), rows)] = other_acc[...].astype(BF)


def low_factors(core, x_own, x_other, y_own, y_other, weights):
    rows, width = x_own.shape
    pieces, ranks = weights.shape[2:]
    wide = pl.BlockSpec((rows, width * Z_STEP // NZ), lambda i: (0, i))
    return pl.pallas_call(
        low_kernel,
        grid=(NZ // Z_STEP,),
        out_shape=jax.ShapeDtypeStruct((2 * rows, ranks), BF),
        in_specs=[pl.BlockSpec(memory_space=pltpu.SMEM)] + [wide] * 4
        + [pl.BlockSpec((NX, Z_STEP, pieces, ranks), lambda i: (0, i, 0, 0))],
        out_specs=pl.BlockSpec((2 * rows, ranks), lambda i: (0, 0)),
        scratch_shapes=[pltpu.VMEM((rows, ranks), F32), pltpu.VMEM((rows, ranks), F32)],
        compiler_params=pltpu.CompilerParams(vmem_limit_bytes=24 * 1024 * 1024),
        cost_estimate=pl.CostEstimate(flops=700_000_000, bytes_accessed=6_600_000, transcendentals=0),
        name="low_factors",
    )(core, x_own, x_other, y_own, y_other, weights)


def grad_kernel(
    scale, core_ref, xo_ref, xt_ref, yo_ref, yt_ref, kept_a_ref, got_a_ref, kept_b_ref, got_b_ref, low_ref,
    m_a_ref, m_b_ref, g_ref, f_ref, u_ref,
):
    core = core_ref[0]
    step = pl.program_id(0)
    rows = xo_ref.shape[0]
    half = kept_a_ref.shape[1]
    rank = m_a_ref.shape[1]
    block = xo_ref.shape[1] // Z_STEP
    piece = block // NX
    extra = g_ref.shape[2] - piece
    mine = pl.ds(pl.multiple_of(core * half, half), half)
    theirs = pl.ds(pl.multiple_of((1 - core) * half, half), half)

    @pl.when(step == 0)
    def _():
        for i, (kept_ref, got_ref, m_ref) in enumerate(
            ((kept_a_ref, got_a_ref, m_a_ref), (kept_b_ref, got_b_ref, m_b_ref))
        ):
            kept, got = kept_ref[...], got_ref[: 2 * rows]
            ranks = slice(i * rank, (i + 1) * rank)
            low = low_ref[:, ranks]
            f_ref[:, ranks] = (dot(kept, m_ref[mine], 1, 0) + dot(got, m_ref[theirs], 1, 0)).astype(BF)
            u_ref[ranks, mine] = (dot(low, kept, 0, 0) * scale).astype(BF)
            u_ref[ranks, theirs] = (dot(low, got, 0, 0) * scale).astype(BF)

    f_own = f_ref[pl.ds(pl.multiple_of(core * rows, rows), rows)]
    f_other = f_ref[pl.ds(pl.multiple_of((1 - core) * rows, rows), rows)]
    line = lax.broadcasted_iota(jnp.int32, (2 * rank, block), 0)
    from_y = (line < rank) & (core == 1)
    for zz in range(Z_STEP):
        cols = slice(zz * block, (zz + 1) * block)
        gx = dot(f_own, xo_ref[:, cols], 0, 0) + dot(f_other, xt_ref[:, cols], 0, 0)
        gy = dot(f_own, yo_ref[:, cols], 0, 0) + dot(f_other, yt_ref[:, cols], 0, 0)
        g = (jnp.where(from_y, gy, gx) * scale).T.astype(BF)
        at = pl.ds(pl.multiple_of((step * Z_STEP + zz) * extra, extra), extra)
        for i in range(NX):
            g_ref[i, zz, :piece] = g[i * piece : (i + 1) * piece]
            g_ref[i, zz, piece:] = u_ref[at, i * 2 * rank : (i + 1) * 2 * rank]


def grad_partials(scale, core, x_own, x_other, y_own, y_other, kept_a, got_a, kept_b, got_b, low, m_a, m_b):
    rows, width = x_own.shape
    feats, rank = m_a.shape
    piece = width // (NX * NZ)
    extra = 2 * rank // NZ
    wide = pl.BlockSpec((rows, width * Z_STEP // NZ), lambda i: (0, i))
    whole = [pl.BlockSpec(a.shape, lambda i: (0, 0)) for a in (kept_a, got_a, kept_b, got_b, low, m_a, m_b)]
    return pl.pallas_call(
        lambda *refs: grad_kernel(scale, *refs),
        grid=(NZ // Z_STEP,),
        out_shape=jax.ShapeDtypeStruct((NX, NZ, piece + extra, 2 * rank), BF),
        in_specs=[pl.BlockSpec(memory_space=pltpu.SMEM)] + [wide] * 4 + whole,
        out_specs=pl.BlockSpec((NX, Z_STEP, piece + extra, 2 * rank), lambda i: (0, i, 0, 0)),
        scratch_shapes=[pltpu.VMEM((2 * rows, 2 * rank), BF), pltpu.VMEM((2 * rank, feats), BF)],
        compiler_params=pltpu.CompilerParams(vmem_limit_bytes=24 * 1024 * 1024),
        cost_estimate=pl.CostEstimate(flops=800_000_000, bytes_accessed=7_500_000, transcendentals=0),
        name="grad_partials",
    )(core, x_own, x_other, y_own, y_other, kept_a, got_a, kept_b, got_b, low, m_a, m_b)


def exchange(parts, axes):
    return lax.all_to_all(parts, axes, split_axis=0, concat_axis=0, tiled=True)


def spread(block, axes, peers):
    return exchange(jnp.broadcast_to(block[None], (peers,) + block.shape), axes)


def swap(block):
    return lax.ppermute(block, "c", [(0, 1), (1, 0)])


def chip_shift(block, by):
    chips = NX * NY
    return lax.ppermute(block, ("x", "y"), [(i, i + by) for i in range(chips) if 0 <= i + by < chips])


def shards(
    inputs, queries, key_rows, values, frozen_output_gradient, out_grad, block_lists,
    down_qkv, up_qkv, output_down_projection, up_out,
):
    x_own, y_own = inputs[0], out_grad[0]
    rows, feats = queries.shape[1:]
    half = feats // 2
    rank = output_down_projection.shape[1]
    width = x_own.shape[1]
    own_cols = down_qkv.shape[1]
    core = lax.axis_index("c")
    first = core == 0
    chip = lax.axis_index("x") * NY + lax.axis_index("y")
    grad_scale = STRENGTH / math.sqrt(NX * NY * NZ * 2 * rows)

    core_id = core.astype(jnp.int32).reshape(1)

    shard = jnp.concatenate([down_qkv[0], down_qkv[1], up_out.T, down_qkv[2]], axis=1)
    line = spread(shard.reshape(2, -1), ("y", "c"), 2 * NY).reshape(2 * NY * own_cols, 4 * rank)
    line = lax.dynamic_slice_in_dim(line, core * 2 * rank, 2 * rank, 1)

    lists = jnp.pad(block_lists[0].astype(BF), ((0, 12), (0, half - block_lists.shape[2])))
    stack = jnp.concatenate([queries[0], frozen_output_gradient[0], key_rows[0], values[0]], axis=0)
    kept = jnp.concatenate([jnp.where(first, stack[:, :half], stack[:, half:]), lists], axis=0)
    got = swap(jnp.concatenate([jnp.where(first, stack[:, half:], stack[:, :half]), lists], axis=0))
    chip_stack = jnp.stack([jnp.where(first, kept, got), jnp.where(first, got, kept)])
    x_other = swap(x_own)
    y_other = lax.ppermute(y_own, "c", [(0, 1)])
    line, chip_stack, x_other, y_other = lax.optimization_barrier((line, chip_stack, x_other, y_other))

    q_chip = chip_stack[:, :rows].reshape(2 * rows, half)
    fog_chip = chip_stack[:, rows : 2 * rows].reshape(2 * rows, half)
    kv_chip = jnp.concatenate(
        [chip_stack[:, 2 * rows : 3 * rows], chip_stack[:, 3 * rows : 4 * rows]], axis=2
    ).reshape(2 * rows, 2 * half)
    lists_chip = chip_stack[:, 4 * rows : 4 * rows + BLK_DEV, : block_lists.shape[2]].reshape(
        2 * BLK_DEV, -1
    )
    windows = (
        chip_shift(kv_chip[rows:], 2),
        chip_shift(kv_chip, 1),
        kv_chip,
        chip_shift(kv_chip, -1),
        chip_shift(kv_chip[:rows], -2),
    )
    ids = (2 * chip - 3) * BLK_DEV + jnp.arange(8 * BLK_DEV, dtype=jnp.int32)
    allowed = jnp.any(lists_chip[:, :, None] == ids.astype(F32)[None, None, :], axis=1) & (ids >= 0)[None]
    bias = jnp.repeat(jnp.where(allowed, 0.0, MASKED).astype(F32), BLK, axis=1)

    plane = spread(line, "z", NZ)
    weights = spread(plane.reshape(-1, 2 * rank), "x", NX).reshape(NX, NZ, -1, 2 * rank)
    low = low_factors(core_id, x_own, x_other, y_own, y_other, weights)
    low_both = lax.all_gather(low, "c")
    odp_half = lax.dynamic_slice_in_dim(output_down_projection, core * half, half, 0)

    kept_a, send_a, dq, p_l2, p_l1, p_own, p_r1, p_r2 = attention(
        core_id, q_chip, windows, fog_chip, low_both, odp_half, bias
    )
    from_r1 = chip_shift(p_l1, -1)
    from_l1 = chip_shift(p_r1, 1)
    from_r2 = chip_shift(p_l2, -2)
    from_l2 = chip_shift(p_r2, 2)
    got_a = swap(send_a)
    m_a = jnp.where(first, up_qkv[0].T, output_down_projection)
    m_b = jnp.where(first, up_qkv[1].T, up_qkv[2].T)

    total = p_own + from_r1.astype(F32) + from_l1.astype(F32)
    total = total + jnp.concatenate([from_l2, from_r2], axis=0).astype(F32)
    total = total.astype(BF)
    dk, dv = total[:, :half], total[:, half:]
    kept_b = jnp.where(first, dk, dv)
    got_b = swap(
        jnp.concatenate([jnp.where(first, dv, dk), jnp.where(first, dk[rows:], dv[:rows])], axis=0)
    )
    g = grad_partials(
        grad_scale, core_id, x_own, x_other, y_own, y_other, kept_a, got_a, kept_b, got_b, low, m_a, m_b
    )

    line_rows = 2 * NY * own_cols
    u_rows = g.shape[2] - line_rows
    step = exchange(g.reshape(NX, -1, 2 * rank), "x")
    step = step.astype(F32).sum(axis=0).astype(BF).reshape(NZ, -1, 2 * rank)
    step = exchange(step, "z")
    step = step.astype(F32).sum(axis=0).astype(BF)
    g_line = step[:line_rows].reshape(2 * NY, own_cols, 2 * rank)
    u_line = jnp.broadcast_to(step[line_rows:][None], (2 * NY, u_rows, 2 * rank))
    step = exchange(jnp.concatenate([g_line, u_line], axis=1), ("y", "c"))
    step = step.reshape(NY, 2, own_cols + u_rows, 2 * rank).astype(F32).sum(axis=0)
    g_out = step[:, :own_cols]
    grad_down = jnp.stack([g_out[0, :, :rank], g_out[0, :, rank:], g_out[1, :, rank:]])
    grad_up_out = g_out[1, :, :rank].T
    u_mine = step[:, own_cols:].astype(BF).reshape(2 * u_rows, 2 * rank)
    u_all = spread(u_mine, ("x", "z"), NX * NZ).reshape(NX, NZ, 2, u_rows, 2 * rank)
    u_all = jnp.transpose(u_all, (2, 1, 3, 0, 4)).reshape(2, 2, rank, feats).astype(F32)
    grad_up = jnp.stack([u_all[0, 0], u_all[0, 1], u_all[1, 1]])
    grad_down_out = u_all[1, 0].T

    def own_frame(mine, from_zero, from_one):
        left = jnp.where(first, mine[:rows], from_zero)
        right = jnp.where(first, from_one, mine[rows:])
        return jnp.concatenate([left, right], axis=1)[None]

    grad_q = own_frame(dq, got_a[2 * rows :], got_a[:rows])
    grad_k = own_frame(dk, got_b[2 * rows :], got_b[:rows])
    grad_v = own_frame(dv, got_b[rows : 2 * rows], got_b[2 * rows :])
    return grad_q, grad_k, grad_v, grad_down, grad_up, grad_down_out, grad_up_out


def solution(mesh):
    fine = Mesh(mesh.devices.reshape(NZ, NX, NY, 2), ("z", "x", "y", "c"))
    ctx = ("x", "y", "c")
    every = ("z", "x", "y", "c")
    tokens = P("z", ctx, None)
    return jax.shard_map(
        shards,
        mesh=fine,
        in_specs=(tokens,) * 7 + (P(None, every, None), P(), P(), P(None, every)),
        out_specs=(tokens,) * 3 + (P(None, every, None), P(), P(), P(None, every)),
        check_vma=False,
    )
```

time: 234 us -> 209 us (0.89)
  blocking collectives: 0 us -> 27.2 us
  starting transfers between devices: 92.2 us -> 67.6 us
  matrix products: 18.3 us -> 0 us
  waiting for transfers between devices: 78.4 us -> 65.6 us
  Pallas kernels: 4.4 us -> 12.3 us
  local copies, waits for them, and re-layouts: 25.3 us -> 19.9 us
    all_to_all x10 -> x6, starting transfers between devices: 58.2 us -> 32.1 us  [exchange(): return lax.all_to_all(parts, axes, split_axis=0, concat_axis=0, tiled=True)]
    all_to_all x0 -> x1, blocking collectives: none -> 22 us  [exchange(): return lax.all_to_all(parts, axes, split_axis=0, concat_axis=0, tiled=True)]
    dot_general x14 -> x0, matrix products: 18.3 us -> none  [dot(): lax.dot_general(a, b, (((ca,), (cb,)), ((), ())), preferred_element_type=...]
    all_to_all x10 -> x6, waiting for transfers between devices: 77.6 us -> 59.7 us  [exchange(): return lax.all_to_all(parts, axes, split_axis=0, concat_axis=0, tiled=True)]
    concatenate x4 -> x0, local copies, waits for them, and re-layouts: 15.8 us -> none  [shards(): g = (jnp.concatenate([g_a, g_b], axis=1) * grad_scale).astype(BF)]
    unnamed x15 -> x56, local copies, waits for them, and re-layouts: 1.36 us -> 10.1 us
    ppermute x3 -> x4, starting transfers between devices: 8.08 us -> 16.3 us  [swap(): return lax.ppermute(block, 'c', [(0, 1), (1, 0)])]
    pallas_call x1 -> x3, Pallas kernels: 4.4 us -> 12.3 us  [the longest x1 6.37 us: attention(): pl.pallas_call(attention_kernel, out_shape=outs, in_specs=[pl.BlockSpec(m...]
  transfers between devices with their start and end apart: 23 -> 19, of which waited for: 11 -> 9; matrix products, arithmetic and copies ran while one was open for 14% -> 9% of each run, Pallas kernels for 0% -> 1%
where the time goes in v2:
time: 209 us; the launch traced here: 207 us
  starting transfers between devices  67.6 us (32%)
  waiting for transfers between devices  65.6 us (31%)
  blocking collectives  27.2 us (13%)
  local copies, waits for them, and re-layouts  19.9 us (10%)
  other arithmetic  13.3 us (6%)
  Pallas kernels  12.3 us (6%)
    all_to_all x6, waiting for transfers between devices, exchange(): return lax.all_to_all(parts, axes, split_axis=0, concat_axis=0, tiled=True)  59.7 us
    all_to_all x6, starting transfers between devices, exchange(): return lax.all_to_all(parts, axes, split_axis=0, concat_axis=0, tiled=True)  32.1 us
    all_to_all x1, blocking collectives, exchange(): return lax.all_to_all(parts, axes, split_axis=0, concat_axis=0, tiled=True)  22 us
    ppermute x8, starting transfers between devices, chip_shift(): lax.ppermute(block, ('x', 'y'), [(i, i + by) for i in range(chips) if 0 <...  17.9 us
    ppermute x4, starting transfers between devices, swap(): return lax.ppermute(block, 'c', [(0, 1), (1, 0)])  16.3 us
    unnamed x56, local copies, waits for them, and re-layouts  10.1 us
    pallas_call x1, Pallas kernels, attention(): pl.pallas_call(attention_kernel, out_shape=outs, in_specs=[pl.BlockSpec(m...  6.37 us
    ppermute x8, waiting for transfers between devices, chip_shift(): lax.ppermute(block, ('x', 'y'), [(i, i + by) for i in range(chips) if 0 <...  5.79 us
  transfers between devices with their start and end apart: 19, of which 9 were waited for; matrix products, arithmetic and copies ran while one was open for 9% of the time, Pallas kernels for 1%

profile of v2, /device:TPU:1, one launch (start us, length us, event | category | flops | bytes accessed | tf_op | source)
XLA Modules:
  0.0 207.2 jit_solution(12727622150288984683)
XLA Ops:
  0.6 8.8 %collective-permute-start.1 = (bf16[128,5120]{1,0:T(8,128)(2,1)}, bf16[128,5120]{1,0:T(8,128)(2,1)S(1)}, u32[]{:S(2)}, u32[]{:S(2)}) collective-permute-start(bf16[128,5120]{1,0:T(8,128)(2,1)} %bitcast.73), channel_id=1, source_target_pairs={{0,1},{1,0},{2,3},{3,2},{4,5},{5,4},{6,7},{7,6},{8,9},{9,8},{10,11... | collective-permute-start | bytes 3932168 | tf_op jit(solution)/shard_map/ppermute | solution.py:223
  9.4 1.3 collective-permute-start.2
  10.7 0.7 convert_bitcast_fusion.1
  11.4 1.2 pad_maximum_fusion.1
  12.7 3.1 %collective-permute-start = (bf16[528,256]{1,0:T(8,128)(2,1)S(1)}, bf16[528,256]{1,0:T(8,128)(2,1)S(1)}, u32[]{:S(2)}, u32[]{:S(2)}) collective-permute-start(bf16[528,256]{1,0:T(8,128)(2,1)S(1)} %fusion.2), channel_id=1, source_target_pairs={{0,1},{1,0},{2,3},{3,2},{4,5},{5,4},{6,7},{7,6},{8,9},{9,8},{10,11... | collective-permute-start | bytes 811016 | tf_op jit(solution)/shard_map/ppermute | solution.py:223
  15.9 0.7 broadcast_in_dim.56
  16.6 3.4 %all-to-all-start = ((bf16[16,2,1280]{2,1,0:T(2,128)(2,1)}), bf16[16,2,1280]{2,1,0:T(2,128)(2,1)S(1)}, u32[]{:S(2)}, u32[]{:S(2)}) async-start(bf16[16,2,1280]{2,1,0:T(2,128)(2,1)} %broadcast_in_dim.56), calls=%async_computation | async-start | bytes 163840 | tf_op jit(solution)/shard_map/all_to_all | solution.py:215
  20.0 8.1 %all-to-all-done = bf16[16,2,1280]{2,1,0:T(2,128)(2,1)S(1)} async-done(((bf16[16,2,1280]{2,1,0:T(2,128)(2,1)}), bf16[16,2,1280]{2,1,0:T(2,128)(2,1)S(1)}, u32[]{:S(2)}, u32[]{:S(2)}) %all-to-all-start) | async-done | bytes 81952 | tf_op jit(solution)/shard_map/all_to_all | solution.py:215
  28.1 0.7 reshape.83
  28.8 0.8 constant_dynamic-slice_fusion.1
  29.7 0.9 pad_maximum_fusion
  30.6 0.8 broadcast_in_dim.57
  31.4 8.6 %all-to-all-start.1 = ((bf16[8,160,128]{2,1,0:T(8,128)(2,1)}), bf16[8,160,128]{2,1,0:T(8,128)(2,1)S(1)}, u32[]{:S(2)}, u32[]{:S(2)}) async-start(bf16[8,160,128]{2,1,0:T(8,128)(2,1)} %broadcast_in_dim.57), calls=%async_computation.1 | async-start | bytes 655360 | tf_op jit(solution)/shard_map/all_to_all | solution.py:215
  40.0 13.8 %all-to-all-done.1 = bf16[8,160,128]{2,1,0:T(8,128)(2,1)S(1)} async-done(((bf16[8,160,128]{2,1,0:T(8,128)(2,1)}), bf16[8,160,128]{2,1,0:T(8,128)(2,1)S(1)}, u32[]{:S(2)}, u32[]{:S(2)}) %all-to-all-start.1) | async-done | bytes 327712 | tf_op jit(solution)/shard_map/all_to_all | solution.py:215
  53.8 1.2 broadcast_in_dim.59
  55.0 4.1 %all-to-all-start.2 = ((bf16[4,1280,128]{2,1,0:T(8,128)(2,1)}), bf16[4,1280,128]{2,1,0:T(8,128)(2,1)S(1)}, u32[]{:S(2)}, u32[]{:S(2)}) async-start(bf16[4,1280,128]{2,1,0:T(8,128)(2,1)} %broadcast_in_dim.59), calls=%async_computation.2 | async-start | bytes 2621440 | tf_op jit(solution)/shard_map/all_to_all | solution.py:215
  59.3 0.6 copy-done.17
  60.0 1.8 fusion.9
  61.8 2.1 %collective-permute-start.4 = (bf16[256,512]{1,0:T(8,128)(2,1)S(1)}, bf16[256,512]{1,0:T(8,128)(2,1)S(1)}, u32[]{:S(2)}, u32[]{:S(2)}) collective-permute-start(bf16[256,512]{1,0:T(8,128)(2,1)S(1)} %bitcast.79), channel_id=1, source_target_pairs={{0,2},{2,4},{4,6},{6,8},{8,10},{10,12},{12,14},{14,16},{16,18},{18... | collective-permute-start | bytes 786440 | tf_op jit(solution)/shard_map/ppermute | solution.py:228
  63.9 1.3 collective-permute-start.5
  65.2 0.7 slice.150
  65.9 0.7 fusion.6
  66.6 4.7 %collective-permute-start.3 = (bf16[128,512]{1,0:T(8,128)(2,1)}, bf16[128,512]{1,0:T(8,128)(2,1)}, u32[]{:S(2)}, u32[]{:S(2)}) collective-permute-start(bf16[128,512]{1,0:T(8,128)(2,1)} %get-tuple-element.94), channel_id=1, source_target_pairs={{0,4},{2,6},{4,8},{6,10},{8,12},{10,14},{12,16},{14,18},{16,20},{1... | collective-permute-start | bytes 393224 | tf_op jit(solution)/shard_map/ppermute | solution.py:228
  71.2 1.3 collective-permute-start.6
  72.8 0.7 reshape.88.bias_ref
  73.5 9.2 %all-to-all-done.2 = bf16[4,1280,128]{2,1,0:T(8,128)(2,1)S(1)} async-done(((bf16[4,1280,128]{2,1,0:T(8,128)(2,1)}), bf16[4,1280,128]{2,1,0:T(8,128)(2,1)S(1)}, u32[]{:S(2)}, u32[]{:S(2)}) %all-to-all-start.2) | async-done | bytes 1310752 | tf_op jit(solution)/shard_map/all_to_all | solution.py:215
  82.8 1.3 copy-done.1
  84.1 1.3 copy-done.4
  85.4 1.3 copy-done.7
  86.7 2.5 %low_factors.1.refs_9_ = bf16[256,128]{1,0:T(8,128)(2,1)S(1)} custom-call(s32[1]{0:T(128)} %bitcast.core_ref.refs_0_, bf16[128,5120]{1,0:T(8,128)(2,1)S(1)} %bitcast.74, bf16[128,5120]{1,0:T(8,128)(2,1)S(1)} %copy-done.4, bf16[128,5120]{1,0:T(8,128)(2,1)S(1)} %bitcast.77, bf16[128,5120]{1,0:T(8,128)(2,1)S(1)} %copy-done.7, bf16[4,8,160,128]{3,2,1,0:T(8,128)(2,1)S(1)} %bitcast.72), custom_call_target="tpu_custom_call" | custom-call | flops 700000000 | bytes 6600000 | tf_op jit(solution)/shard_map/low_factors/pallas_call | solution.py:138
  89.3 5.2 %all-gather = bf16[512,128]{1,0:T(8,128)(2,1)S(1)} all-gather(bf16[256,128]{1,0:T(8,128)(2,1)S(1)} %low_factors.1.refs_9_), channel_id=2, replica_groups=mesh['z'=8,'x'=4,'y'=8,'c'=2] {'c'}, dimensions={0}, use_global_device_ids=true | all-gather | bytes 196608 | tf_op jit(solution)/shard_map/all_gather | solution.py:283
  94.5 0.7 copy-done.12
  95.2 0.9 copy-done.13
  96.2 6.4 %attention.1 = (bf16[256,256]{1,0:T(8,128)(2,1)S(1)}, bf16[384,256]{1,0:T(8,128)(2,1)}, bf16[256,256]{1,0:T(8,128)(2,1)S(1)}, bf16[128,512]{1,0:T(8,128)(2,1)S(1...) custom-call(s32[1]{0:T(128)} %bitcast.core_ref.refs_0_, ...), custom_call_target="tpu_custom_call" | custom-call | flops 1400000000 | bytes 4000000 | tf_op jit(solution)/shard_map/attention/pallas_call | solution.py:93
  102.6 0.8 copy-done.9
  103.4 1.3 collective-permute-start.8
  104.6 4.7 %collective-permute-start.9 = (bf16[256,512]{1,0:T(8,128)(2,1)}, bf16[256,512]{1,0:T(8,128)(2,1)}, u32[]{:S(2)}, u32[]{:S(2)}) collective-permute-start(bf16[256,512]{1,0:T(8,128)(2,1)} %get-tuple-element.27), channel_id=1, source_target_pairs={{0,2},{2,4},{4,6},{6,8},{8,10},{10,12},{12,14},{14,16},{16,18},{18... | collective-permute-start | bytes 786440 | tf_op jit(solution)/shard_map/ppermute | solution.py:228
  109.4 0.8 copy.88
  110.1 0.8 copy.89
  111.0 1.3 collective-permute-start.10
  112.3 1.3 collective-permute-start.11
  113.6 1.0 bitcast_select_fusion.refs_10_
  114.6 2.0 collective-permute-start.7
  116.6 3.0 %collective-permute-done.10 = bf16[128,512]{1,0:T(8,128)(2,1)S(1)} collective-permute-done((bf16[128,512]{1,0:T(8,128)(2,1)}, bf16[128,512]{1,0:T(8,128)(2,1)S(1)}, u32[]{:S(2)}, u32[]{:S(2)}) %collective-permute-start.10) | collective-permute-done | bytes 131104 | tf_op jit(solution)/shard_map/ppermute | solution.py:228
  119.6 2.8 %collective-permute-done.11 = bf16[128,512]{1,0:T(8,128)(2,1)S(1)} collective-permute-done((bf16[128,512]{1,0:T(8,128)(2,1)S(1)}, bf16[128,512]{1,0:T(8,128)(2,1)S(1)}, u32[]{:S(2)}, u32[]{:S(2)}) %collective-permute-start.11) | collective-permute-done | bytes 131104 | tf_op jit(solution)/shard_map/ppermute | solution.py:228
  122.4 1.5 add_convert_fusion
  124.0 2.4 %collective-permute-start.12 = (bf16[384,256]{1,0:T(8,128)(2,1)S(1)}, bf16[384,256]{1,0:T(8,128)(2,1)S(1)}, u32[]{:S(2)}, u32[]{:S(2)}) collective-permute-start(bf16[384,256]{1,0:T(8,128)(2,1)S(1)} %pad_maximum_fusion.4), channel_id=1, source_target_pairs={{0,1},{1,0},{2,3},{3,2},{4,5},{5,4},{6,7},{7,6},{8,9},{9,8},{10,11... | collective-permute-start | bytes 589832 | tf_op jit(solution)/shard_map/ppermute | solution.py:223
  126.4 0.9 select_bitcast_fusion.2.refs_11_
  127.5 3.4 %grad_partials.1 = bf16[4,8,176,128]{3,2,1,0:T(8,128)(2,1)S(1)} custom-call(s32[1]{0:T(128)} %bitcast.core_ref.refs_0_, bf16[128,5120]{1,0:T(8,128)(2,1)S(1)} %bitcast.75, bf16[128,5120]{1,0:T(8,128)(2,1)S(1)} %copy-done.5, bf16[128,5120]{1,0:T(8,128)(2,1)S(1)} %bitcast.78, bf16[128,5120]{1,0:T(8,128)(2,1)S(1)} %copy-done.8, ...), custom_call_target="tpu_custom_call" | custom-call | flops 800000000 | bytes 7500000 | tf_op jit(solution)/shard_map/grad_partials/pallas_call | solution.py:201
  130.9 22.0 %all_to_all.35 = bf16[4,1408,128]{2,1,0:T(8,128)(2,1)} all-to-all(bf16[4,1408,128]{2,1,0:T(8,128)(2,1)S(1)} %bitcast.71), channel_id=1, replica_groups=mesh['z'=8,'x'=4,'y'=8,'c'=2] {'x'}, dimensions={0} | all-to-all | bytes 2883584 | tf_op jit(solution)/shard_map/all_to_all | solution.py:215
  152.9 2.4 %reduce_sum.33 = bf16[1408,128]{1,0:T(8,128)(2,1)} reduce(bf16[4,1408,128]{2,1,0:T(8,128)(2,1)} %all_to_all.35, bf16[]{:T(256)} %constant.13.clone.1), dimensions={0}, to_apply=%region_1.2 | reduce | flops 540672 | bytes 1802242 | tf_op jit(solution)/shard_map/reduce_sum | solution.py:312
  155.3 3.6 %all-to-all-start.4 = ((bf16[8,176,128]{2,1,0:T(8,128)(2,1)}), bf16[8,176,128]{2,1,0:T(8,128)(2,1)S(1)}, u32[]{:S(2)}, u32[]{:S(2)}) async-start(bf16[8,176,128]{2,1,0:T(8,128)(2,1)} %bitcast.31), calls=%async_computation.4 | async-start | bytes 720896 | tf_op jit(solution)/shard_map/all_to_all | solution.py:215
  158.9 0.7 maximum_bitcast_fusion
  159.5 10.9 %all-to-all-done.4 = bf16[8,176,128]{2,1,0:T(8,128)(2,1)S(1)} async-done(((bf16[8,176,128]{2,1,0:T(8,128)(2,1)}), bf16[8,176,128]{2,1,0:T(8,128)(2,1)S(1)}, u32[]{:S(2)}, u32[]{:S(2)}) %all-to-all-start.4) | async-done | bytes 360480 | tf_op jit(solution)/shard_map/all_to_all | solution.py:215
  170.6 0.7 pad_maximum_fusion.5
  171.3 8.6 %all-to-all-start.5 = ((bf16[16,26,128]{2,1,0:T(8,128)(2,1)}), bf16[16,26,128]{2,1,0:T(8,128)(2,1)S(1)}, u32[]{:S(2)}, u32[]{:S(2)}) async-start(bf16[16,26,128]{2,1,0:T(8,128)(2,1)} %pad_maximum_fusion.5), calls=%async_computation.5 | async-start | bytes 262144 | tf_op jit(solution)/shard_map/all_to_all | solution.py:215
  179.9 9.1 %all-to-all-done.5 = bf16[16,26,128]{2,1,0:T(8,128)(2,1)S(1)} async-done(((bf16[16,26,128]{2,1,0:T(8,128)(2,1)}), bf16[16,26,128]{2,1,0:T(8,128)(2,1)S(1)}, u32[]{:S(2)}, u32[]{:S(2)}) %all-to-all-start.5) | async-done | bytes 106528 | tf_op jit(solution)/shard_map/all_to_all | solution.py:215
  189.2 0.7 broadcast_in_dim.68
  189.9 3.9 %all-to-all-start.6 = ((bf16[32,32,128]{2,1,0:T(8,128)(2,1)}), bf16[32,32,128]{2,1,0:T(8,128)(2,1)S(1)}, u32[]{:S(2)}, u32[]{:S(2)}) async-start(bf16[32,32,128]{2,1,0:T(8,128)(2,1)} %broadcast_in_dim.68), calls=%async_computation.6 | async-start | bytes 524288 | tf_op jit(solution)/shard_map/all_to_all | solution.py:215
  193.8 0.7 maximum_bitcast_fusion.2
  194.5 0.7 maximum_bitcast_fusion.1
  196.5 8.6 %all-to-all-done.6 = bf16[32,32,128]{2,1,0:T(8,128)(2,1)S(1)} async-done(((bf16[32,32,128]{2,1,0:T(8,128)(2,1)}), bf16[32,32,128]{2,1,0:T(8,128)(2,1)S(1)}, u32[]{:S(2)}, u32[]{:S(2)}) %all-to-all-start.6) | async-done | bytes 262176 | tf_op jit(solution)/shard_map/all_to_all | solution.py:215
  205.7 0.7 slice_bitcast_fusion
  206.4 0.8 pad_maximum_fusion.2
  (93 shorter events, 3.3 us)
Async XLA Ops:
  0.6 30.0 %collective-permute-start.1 = (bf16[128,5120]{1,0:T(8,128)(2,1)}, bf16[128,5120]{1,0:T(8,128)(2,1)S(1)}, u32[]{:S(2)}, u32[]{:S(2)}) collective-permute-start(bf16[128,5120]{1,0:T(8,128)(2,1)} %bitcast.73), channel_id=1, source_target_pairs={{0,1},{1,0},{2,3},{3,2},{4,5},{5,4},{6,7},{7,6},{8,9},{9,8},{10,11... | collective-permute-start | bytes 3932168 | tf_op jit(solution)/shard_map/ppermute | solution.py:223
  9.4 21.2 %collective-permute-start.2 = (bf16[128,5120]{1,0:T(8,128)(2,1)}, bf16[128,5120]{1,0:T(8,128)(2,1)S(1)}, u32[]{:S(2)}, u32[]{:S(2)}) collective-permute-start(bf16[128,5120]{1,0:T(8,128)(2,1)} %bitcast.76), channel_id=1, source_target_pairs={{0,1},{2,3},{4,5},{6,7},{8,9},{10,11},{12,13},{14,15},{16,17},{18,... | collective-permute-start | bytes 3932168 | tf_op jit(solution)/shard_map/ppermute | solution.py:258
  11.4 4.4 %copy-start.21 = (bf16[3,10,64]{2,0,1:T(4,128)(2,1)S(1)}, bf16[3,10,64]{2,0,1:T(4,128)(2,1)}, u32[]{:S(2)}) copy-start(bf16[3,10,64]{2,0,1:T(4,128)(2,1)} %param.18) | copy-start | bytes 11524
  11.4 4.4 %copy-start.22 = (bf16[64,10]{0,1:T(8,128)(2,1)S(1)}, bf16[64,10]{0,1:T(8,128)(2,1)}, u32[]{:S(2)}) copy-start(bf16[64,10]{0,1:T(8,128)(2,1)} %param.21) | copy-start | bytes 3844
  12.7 16.9 %collective-permute-start = (bf16[528,256]{1,0:T(8,128)(2,1)S(1)}, bf16[528,256]{1,0:T(8,128)(2,1)S(1)}, u32[]{:S(2)}, u32[]{:S(2)}) collective-permute-start(bf16[528,256]{1,0:T(8,128)(2,1)S(1)} %fusion.2), channel_id=1, source_target_pairs={{0,1},{1,0},{2,3},{3,2},{4,5},{5,4},{6,7},{7,6},{8,9},{9,8},{10,11... | collective-permute-start | bytes 811016 | tf_op jit(solution)/shard_map/ppermute | solution.py:223
  16.6 11.5 %all-to-all-start = ((bf16[16,2,1280]{2,1,0:T(2,128)(2,1)}), bf16[16,2,1280]{2,1,0:T(2,128)(2,1)S(1)}, u32[]{:S(2)}, u32[]{:S(2)}) async-start(bf16[16,2,1280]{2,1,0:T(2,128)(2,1)} %broadcast_in_dim.56), calls=%async_computation | async-start | bytes 163840 | tf_op jit(solution)/shard_map/all_to_all | solution.py:215
  30.6 24.4 %copy-start.3 = (bf16[128,5120]{1,0:T(8,128)(2,1)}, bf16[128,5120]{1,0:T(8,128)(2,1)S(1)}, u32[]{:S(2)}) copy-start(bf16[128,5120]{1,0:T(8,128)(2,1)S(1)} %collective-permute-done.1.xt_ref.refs_2_) | copy-start | bytes 3932164
  30.6 24.4 %copy-start.6 = (bf16[128,5120]{1,0:T(8,128)(2,1)}, bf16[128,5120]{1,0:T(8,128)(2,1)S(1)}, u32[]{:S(2)}) copy-start(bf16[128,5120]{1,0:T(8,128)(2,1)S(1)} %collective-permute-done.2.yt_ref.refs_4_) | copy-start | bytes 3932164
  31.4 22.3 %all-to-all-start.1 = ((bf16[8,160,128]{2,1,0:T(8,128)(2,1)}), bf16[8,160,128]{2,1,0:T(8,128)(2,1)S(1)}, u32[]{:S(2)}, u32[]{:S(2)}) async-start(bf16[8,160,128]{2,1,0:T(8,128)(2,1)} %broadcast_in_dim.57), calls=%async_computation.1 | async-start | bytes 655360 | tf_op jit(solution)/shard_map/all_to_all | solution.py:215
  55.0 4.2 %copy-start.20 = (bf16[512,64]{0,1:T(8,128)(2,1)S(1)}, bf16[512,64]{0,1:T(8,128)(2,1)}, u32[]{:S(2)}) copy-start(bf16[512,64]{0,1:T(8,128)(2,1)} %param.20) | copy-start | bytes 196612
  55.0 27.7 %all-to-all-start.2 = ((bf16[4,1280,128]{2,1,0:T(8,128)(2,1)}), bf16[4,1280,128]{2,1,0:T(8,128)(2,1)S(1)}, u32[]{:S(2)}, u32[]{:S(2)}) async-start(bf16[4,1280,128]{2,1,0:T(8,128)(2,1)} %broadcast_in_dim.59), calls=%async_computation.2 | async-start | bytes 2621440 | tf_op jit(solution)/shard_map/all_to_all | solution.py:215
  59.3 0.7 copy-start.17
  59.3 23.5 %copy-start = (bf16[1,128,5120]{2,1,0:T(8,128)(2,1)S(1)}, bf16[1,128,5120]{2,1,0:T(8,128)(2,1)}, u32[]{:S(2)}) copy-start(bf16[1,128,5120]{2,1,0:T(8,128)(2,1)} %param.11) | copy-start | bytes 3932164
  61.8 32.8 %collective-permute-start.4 = (bf16[256,512]{1,0:T(8,128)(2,1)S(1)}, bf16[256,512]{1,0:T(8,128)(2,1)S(1)}, u32[]{:S(2)}, u32[]{:S(2)}) collective-permute-start(bf16[256,512]{1,0:T(8,128)(2,1)S(1)} %bitcast.79), channel_id=1, source_target_pairs={{0,2},{2,4},{4,6},{6,8},{8,10},{10,12},{12,14},{14,16},{16,18},{18... | collective-permute-start | bytes 786440 | tf_op jit(solution)/shard_map/ppermute | solution.py:228
  63.9 31.3 %collective-permute-start.5 = (bf16[256,512]{1,0:T(8,128)(2,1)S(1)}, bf16[256,512]{1,0:T(8,128)(2,1)}, u32[]{:S(2)}, u32[]{:S(2)}) collective-permute-start(bf16[256,512]{1,0:T(8,128)(2,1)S(1)} %bitcast.80), channel_id=1, source_target_pairs={{2,0},{4,2},{6,4},{8,6},{10,8},{12,10},{14,12},{16,14},{18,16},{20... | collective-permute-start | bytes 786440 | tf_op jit(solution)/shard_map/ppermute | solution.py:228
  66.6 27.9 %collective-permute-start.3 = (bf16[128,512]{1,0:T(8,128)(2,1)}, bf16[128,512]{1,0:T(8,128)(2,1)}, u32[]{:S(2)}, u32[]{:S(2)}) collective-permute-start(bf16[128,512]{1,0:T(8,128)(2,1)} %get-tuple-element.94), channel_id=1, source_target_pairs={{0,4},{2,6},{4,8},{6,10},{8,12},{10,14},{12,16},{14,18},{16,20},{1... | collective-permute-start | bytes 393224 | tf_op jit(solution)/shard_map/ppermute | solution.py:228
  71.2 23.3 %collective-permute-start.6 = (bf16[128,512]{1,0:T(8,128)(2,1)}, bf16[128,512]{1,0:T(8,128)(2,1)}, u32[]{:S(2)}, u32[]{:S(2)}) collective-permute-start(bf16[128,512]{1,0:T(8,128)(2,1)} %get-tuple-element.93), channel_id=1, source_target_pairs={{4,0},{6,2},{8,4},{10,6},{12,8},{14,10},{16,12},{18,14},{20,16},{2... | collective-permute-start | bytes 393224 | tf_op jit(solution)/shard_map/ppermute | solution.py:228
  82.8 1.3 copy-start.1
  84.1 1.3 copy-start.4
  85.4 1.3 copy-start.7
  86.7 8.5 %copy-start.10 = (bf16[2,128,256]{2,1,0:T(8,128)(2,1)S(1)}, bf16[2,128,256]{2,1,0:T(8,128)(2,1)}, u32[]{:S(2)}) copy-start(bf16[2,128,256]{2,1,0:T(8,128)(2,1)} %get-tuple-element.76) | copy-start | bytes 393220
  86.7 8.5 %copy-start.11 = (f32[8,1024]{1,0:T(8,128)S(1)}, f32[8,1024]{1,0:T(8,128)}, u32[]{:S(2)}) copy-start(f32[8,1024]{1,0:T(8,128)} %reshape.88.bias_ref) | copy-start | bytes 98308
  94.5 0.7 copy-start.12
  95.2 1.0 copy-start.13
  96.2 13.2 %copy-start.19 = (bf16[3,64,512]{2,1,0:T(8,128)(2,1)S(1)}, bf16[3,64,512]{2,1,0:T(8,128)(2,1)}, u32[]{:S(2)}) copy-start(bf16[3,64,512]{2,1,0:T(8,128)(2,1)} %param.19) | copy-start | bytes 589828
  102.6 0.8 copy-start.9
  103.4 6.0 %copy-start.14 = (bf16[128,512]{1,0:T(8,128)(2,1)}, bf16[128,512]{1,0:T(8,128)(2,1)S(1)}, u32[]{:S(2)}) copy-start(bf16[128,512]{1,0:T(8,128)(2,1)S(1)} %get-tuple-element.28) | copy-start | bytes 393220
  103.4 19.0 %collective-permute-start.8 = (bf16[256,512]{1,0:T(8,128)(2,1)}, bf16[256,512]{1,0:T(8,128)(2,1)}, u32[]{:S(2)}, u32[]{:S(2)}) collective-permute-start(bf16[256,512]{1,0:T(8,128)(2,1)} %get-tuple-element.26), channel_id=1, source_target_pairs={{2,0},{4,2},{6,4},{8,6},{10,8},{12,10},{14,12},{16,14},{18,16},{20... | collective-permute-start | bytes 786440 | tf_op jit(solution)/shard_map/ppermute | solution.py:228
  104.6 17.8 %collective-permute-start.9 = (bf16[256,512]{1,0:T(8,128)(2,1)}, bf16[256,512]{1,0:T(8,128)(2,1)}, u32[]{:S(2)}, u32[]{:S(2)}) collective-permute-start(bf16[256,512]{1,0:T(8,128)(2,1)} %get-tuple-element.27), channel_id=1, source_target_pairs={{0,2},{2,4},{4,6},{6,8},{8,10},{10,12},{12,14},{14,16},{16,18},{18... | collective-permute-start | bytes 786440 | tf_op jit(solution)/shard_map/ppermute | solution.py:228
  109.4 18.1 %copy-start.8 = (bf16[128,5120]{1,0:T(8,128)(2,1)S(1)}, bf16[128,5120]{1,0:T(8,128)(2,1)}, u32[]{:S(2)}) copy-start(bf16[128,5120]{1,0:T(8,128)(2,1)} %copy-done.6) | copy-start | bytes 3932164
  111.0 8.6 %collective-permute-start.10 = (bf16[128,512]{1,0:T(8,128)(2,1)}, bf16[128,512]{1,0:T(8,128)(2,1)S(1)}, u32[]{:S(2)}, u32[]{:S(2)}) collective-permute-start(bf16[128,512]{1,0:T(8,128)(2,1)} %copy-done.14), channel_id=1, source_target_pairs={{0,4},{2,6},{4,8},{6,10},{8,12},{10,14},{12,16},{14,18},{16,20},{1... | collective-permute-start | bytes 393224 | tf_op jit(solution)/shard_map/ppermute | solution.py:228
  112.3 10.1 %collective-permute-start.11 = (bf16[128,512]{1,0:T(8,128)(2,1)S(1)}, bf16[128,512]{1,0:T(8,128)(2,1)S(1)}, u32[]{:S(2)}, u32[]{:S(2)}) collective-permute-start(bf16[128,512]{1,0:T(8,128)(2,1)S(1)} %get-tuple-element.29), channel_id=1, source_target_pairs={{4,0},{6,2},{8,4},{10,6},{12,8},{14,10},{16,12},{18,14},{20,16},{2... | collective-permute-start | bytes 393224 | tf_op jit(solution)/shard_map/ppermute | solution.py:228
  113.6 12.8 %copy-start.18 = (bf16[1,64,512]{1,2,0:T(8,128)(2,1)S(1)}, bf16[1,64,512]{1,2,0:T(8,128)(2,1)}, u32[]{:S(2)}) copy-start(bf16[1,64,512]{1,2,0:T(8,128)(2,1)} %copy.88) | copy-start | bytes 196612
  114.6 12.7 %collective-permute-start.7 = (bf16[384,256]{1,0:T(8,128)(2,1)}, bf16[384,256]{1,0:T(8,128)(2,1)S(1)}, u32[]{:S(2)}, u32[]{:S(2)}) collective-permute-start(bf16[384,256]{1,0:T(8,128)(2,1)} %get-tuple-element.24), channel_id=1, source_target_pairs={{0,1},{1,0},{2,3},{3,2},{4,5},{5,4},{6,7},{7,6},{8,9},{9,8},{10,11... | collective-permute-start | bytes 589832 | tf_op jit(solution)/shard_map/ppermute | solution.py:223
  122.4 5.0 %copy-start.2 = (bf16[1,128,5120]{2,1,0:T(8,128)(2,1)S(1)}, bf16[1,128,5120]{2,1,0:T(8,128)(2,1)}, u32[]{:S(2)}) copy-start(bf16[1,128,5120]{2,1,0:T(8,128)(2,1)} %param.16) | copy-start | bytes 3932164
  122.4 5.0 %copy-start.5 = (bf16[128,5120]{1,0:T(8,128)(2,1)S(1)}, bf16[128,5120]{1,0:T(8,128)(2,1)}, u32[]{:S(2)}) copy-start(bf16[128,5120]{1,0:T(8,128)(2,1)} %copy-done.3) | copy-start | bytes 3932164
  123.9 3.5 %copy-start.15 = (bf16[256,512]{1,0:T(8,128)(2,1)}, bf16[256,512]{1,0:T(8,128)(2,1)S(1)}, u32[]{:S(2)}) copy-start(bf16[256,512]{1,0:T(8,128)(2,1)S(1)} %add_convert_fusion) | copy-start | bytes 786436
  124.0 3.5 %collective-permute-start.12 = (bf16[384,256]{1,0:T(8,128)(2,1)S(1)}, bf16[384,256]{1,0:T(8,128)(2,1)S(1)}, u32[]{:S(2)}, u32[]{:S(2)}) collective-permute-start(bf16[384,256]{1,0:T(8,128)(2,1)S(1)} %pad_maximum_fusion.4), channel_id=1, source_target_pairs={{0,1},{1,0},{2,3},{3,2},{4,5},{5,4},{6,7},{7,6},{8,9},{9,8},{10,11... | collective-permute-start | bytes 589832 | tf_op jit(solution)/shard_map/ppermute | solution.py:223
  155.3 24.6 %copy-start.16 = (bf16[256,512]{1,0:T(8,128)(2,1)S(1)}, bf16[256,512]{1,0:T(8,128)(2,1)}, u32[]{:S(2)}) copy-start(bf16[256,512]{1,0:T(8,128)(2,1)} %copy-done.15) | copy-start | bytes 786436
  155.3 15.2 %all-to-all-start.4 = ((bf16[8,176,128]{2,1,0:T(8,128)(2,1)}), bf16[8,176,128]{2,1,0:T(8,128)(2,1)S(1)}, u32[]{:S(2)}, u32[]{:S(2)}) async-start(bf16[8,176,128]{2,1,0:T(8,128)(2,1)} %bitcast.31), calls=%async_computation.4 | async-start | bytes 720896 | tf_op jit(solution)/shard_map/all_to_all | solution.py:215
  171.3 17.8 %all-to-all-start.5 = ((bf16[16,26,128]{2,1,0:T(8,128)(2,1)}), bf16[16,26,128]{2,1,0:T(8,128)(2,1)S(1)}, u32[]{:S(2)}, u32[]{:S(2)}) async-start(bf16[16,26,128]{2,1,0:T(8,128)(2,1)} %pad_maximum_fusion.5), calls=%async_computation.5 | async-start | bytes 262144 | tf_op jit(solution)/shard_map/all_to_all | solution.py:215
  189.9 15.1 %all-to-all-start.6 = ((bf16[32,32,128]{2,1,0:T(8,128)(2,1)}), bf16[32,32,128]{2,1,0:T(8,128)(2,1)S(1)}, u32[]{:S(2)}, u32[]{:S(2)}) async-start(bf16[32,32,128]{2,1,0:T(8,128)(2,1)} %broadcast_in_dim.68), calls=%async_computation.6 | async-start | bytes 524288 | tf_op jit(solution)/shard_map/all_to_all | solution.py:215

commit v3 on v2

v3 whole, which is shorter than its diff:
```python
import math

import jax
import jax.numpy as jnp
from jax import lax
from jax.experimental import pallas as pl
from jax.experimental.pallas import tpu as pltpu
from jax.sharding import Mesh, PartitionSpec as P

HDIM = 128
BLK = 32
BLK_DEV = 4
NX, NY, NZ = 4, 8, 8
STRENGTH = 2.0
SCALING = HDIM**-0.5
MASKED = -1e30
BF = jnp.bfloat16
F32 = jnp.float32

PAIR = 4
REACH = 3


def dot(a, b, ca, cb):
    return lax.dot_general(a, b, (((ca,), (cb,)), ((), ())), preferred_element_type=F32)


def attention_kernel(
    q_ref, left_ref, own_ref, right_ref, fog_ref, low_ref, odp_ref, bias_ref,
    send_ref, to_left_ref, to_own_ref, to_right_ref, kv_ref, sum_ref, dq_ref, attn_ref,
):
    edge, tokens = left_ref.shape[0], own_ref.shape[0]
    rank = odp_ref.shape[1]
    kv_ref[:edge] = left_ref[...]
    kv_ref[edge : edge + tokens] = own_ref[...]
    kv_ref[edge + tokens :] = right_ref[...]
    sum_ref[...] = jnp.zeros_like(sum_ref)
    low_out = jnp.concatenate([low_ref[1][:, :rank], low_ref[3][:, :rank]], axis=0)
    dout = (fog_ref[...].astype(F32) + STRENGTH * dot(low_out, odp_ref[...], 1, 1)).astype(BF)
    block = tokens // 2
    wide = block + 2 * edge
    for j in range(2):
        rows = slice(j * block, (j + 1) * block)
        window = slice(j * block, j * block + wide)
        q, dout_j = q_ref[rows], dout[rows]
        k, v = kv_ref[window, :HDIM], kv_ref[window, HDIM:]
        s = (dot(q, k, 1, 1) * SCALING).reshape(8, BLK, wide)
        s = (s + bias_ref[8 * j : 8 * j + 8, window][:, None, :]).reshape(block, wide)
        weights = jnp.exp(s - s.max(axis=1, keepdims=True))
        probs = weights * (1.0 / weights.sum(axis=1, keepdims=True))
        probs_low = probs.astype(BF)
        attn = dot(probs_low, v, 1, 0).astype(BF)
        delta = (dout_j.astype(F32) * attn.astype(F32)).sum(axis=1, keepdims=True)
        dscore = (probs * (dot(dout_j, v, 1, 1) - delta)).astype(BF)
        attn_ref[rows] = attn
        dq_ref[rows] = (dot(dscore, k, 1, 0) * SCALING).astype(BF)
        sum_ref[window, :HDIM] += dot(dscore, q, 0, 0) * SCALING
        sum_ref[window, HDIM:] += dot(probs_low, dout_j, 0, 0)
    to_left_ref[...] = sum_ref[:edge].astype(BF)
    to_own_ref[...] = sum_ref[edge : edge + tokens]
    to_right_ref[...] = sum_ref[edge + tokens :].astype(BF)
    for yl in range(2):
        chip = slice(yl * block, (yl + 1) * block)
        later = slice(yl * block + block // 2, (yl + 1) * block)
        send_ref[2 * yl, :block] = dq_ref[chip]
        send_ref[2 * yl, block:] = dq_ref[later]
        send_ref[2 * yl + 1, :block] = attn_ref[chip]
        send_ref[2 * yl + 1, block:] = dq_ref[later]


def attention(q, left, own, right, fog, low, odp_head, bias):
    tokens, edge = q.shape[0], left.shape[0]
    shape = jax.ShapeDtypeStruct
    vmem = pl.BlockSpec(memory_space=pltpu.VMEM)
    return pl.pallas_call(
        attention_kernel,
        out_shape=[
            shape((PAIR, 3 * tokens // PAIR, HDIM), BF),
            shape((edge, 2 * HDIM), BF),
            shape((tokens, 2 * HDIM), F32),
            shape((edge, 2 * HDIM), BF),
        ],
        in_specs=[vmem] * 8,
        out_specs=[vmem] * 4,
        scratch_shapes=[
            pltpu.VMEM((tokens + 2 * edge, 2 * HDIM), BF),
            pltpu.VMEM((tokens + 2 * edge, 2 * HDIM), F32),
            pltpu.VMEM((tokens, HDIM), BF),
            pltpu.VMEM((tokens, HDIM), BF),
        ],
        compiler_params=pltpu.CompilerParams(vmem_limit_bytes=24 * 1024 * 1024),
        cost_estimate=pl.CostEstimate(flops=700_000_000, bytes_accessed=3_000_000, transcendentals=524288),
        name="attention",
    )(q, left, own, right, fog, low, odp_head, bias)


def merge_kernel(own_ref, from_left_ref, from_right_ref, send_ref, total_ref):
    tokens = own_ref.shape[0]
    frame = tokens // PAIR
    edge = from_left_ref.shape[0]
    head, tail = from_left_ref[...].astype(F32), from_right_ref[...].astype(F32)
    total_ref[:frame] = (own_ref[:frame] + head[:frame]).astype(BF)
    total_ref[frame:edge] = (own_ref[frame:edge] + head[frame:] + tail[: edge - frame]).astype(BF)
    total_ref[edge:] = (own_ref[edge:] + tail[edge - frame :]).astype(BF)
    for yl in range(2):
        chip = slice(2 * yl * frame, 2 * (yl + 1) * frame)
        for core in range(2):
            mine = slice((2 * yl + core) * frame, (2 * yl + core + 1) * frame)
            role = slice(core * HDIM, (core + 1) * HDIM)
            rest = slice((1 - core) * HDIM, (2 - core) * HDIM)
            send_ref[2 * yl + core, : 2 * frame] = total_ref[chip, role]
            send_ref[2 * yl + core, 2 * frame :] = total_ref[mine, rest]


def merge(own, from_left, from_right):
    tokens = own.shape[0]
    vmem = pl.BlockSpec(memory_space=pltpu.VMEM)
    return pl.pallas_call(
        merge_kernel,
        out_shape=jax.ShapeDtypeStruct((PAIR, 3 * tokens // PAIR, HDIM), BF),
        in_specs=[vmem] * 3,
        out_specs=vmem,
        scratch_shapes=[pltpu.VMEM((tokens, 2 * HDIM), BF)],
        compiler_params=pltpu.CompilerParams(vmem_limit_bytes=8 * 1024 * 1024),
        cost_estimate=pl.CostEstimate(flops=1_000_000, bytes_accessed=1_400_000, transcendentals=0),
        name="merge",
    )(own, from_left, from_right)


Z_STEP = 2


def low_kernel(core_ref, xo_ref, xt_ref, yo_ref, yt_ref, w_ref, low_ref, own_acc, other_acc):
    core = core_ref[0]
    step = pl.program_id(0)
    rows = xo_ref.shape[0]
    ranks = w_ref.shape[3]
    block = NX * w_ref.shape[2]

    @pl.when(step == 0)
    def _():
        own_acc[...] = jnp.zeros_like(own_acc)
        other_acc[...] = jnp.zeros_like(other_acc)

    lane = lax.broadcasted_iota(jnp.int32, (rows, ranks), 1)
    from_y = (lane < ranks // 2) & (core == 1)
    for zz in range(Z_STEP):
        cols = slice(zz * block, (zz + 1) * block)
        w = jnp.concatenate([w_ref[i, zz] for i in range(NX)], axis=0)
        for x_ref, y_ref, acc in ((xo_ref, yo_ref, own_acc), (xt_ref, yt_ref, other_acc)):
            acc[...] += jnp.where(from_y, dot(y_ref[:, cols], w, 1, 0), dot(x_ref[:, cols], w, 1, 0))

    @pl.when(step == pl.num_programs(0) - 1)
    def _():
        low_ref[pl.ds(pl.multiple_of(core * rows, rows), rows)] = own_acc[...].astype(BF)
        low_ref[pl.ds(pl.multiple_of((1 - core) * rows, rows), rows)] = other_acc[...].astype(BF)


def low_factors(core, x_own, x_other, y_own, y_other, weights):
    rows, width = x_own.shape
    pieces, ranks = weights.shape[2:]
    wide = pl.BlockSpec((rows, width * Z_STEP // NZ), lambda i: (0, i))
    return pl.pallas_call(
        low_kernel,
        grid=(NZ // Z_STEP,),
        out_shape=jax.ShapeDtypeStruct((2 * rows, ranks), BF),
        in_specs=[pl.BlockSpec(memory_space=pltpu.SMEM)] + [wide] * 4
        + [pl.BlockSpec((NX, Z_STEP, pieces, ranks), lambda i: (0, i, 0, 0))],
        out_specs=pl.BlockSpec((2 * rows, ranks), lambda i: (0, 0)),
        scratch_shapes=[pltpu.VMEM((rows, ranks), F32), pltpu.VMEM((rows, ranks), F32)],
        compiler_params=pltpu.CompilerParams(vmem_limit_bytes=10 * 1024 * 1024),
        cost_estimate=pl.CostEstimate(flops=700_000_000, bytes_accessed=6_600_000, transcendentals=0),
        name="low_factors",
    )(core, x_own, x_other, y_own, y_other, weights)


def grad_kernel(
    scale, core_ref, xo_ref, xt_ref, yo_ref, yt_ref, got_a_ref, got_b_ref, low_ref, m_a_ref, m_b_ref,
    g_ref, f_ref, u_ref,
):
    core = core_ref[0]
    step = pl.program_id(0)
    rows = xo_ref.shape[0]
    rank = m_a_ref.shape[1]
    block = xo_ref.shape[1] // Z_STEP
    piece = block // NX
    extra = g_ref.shape[2] - piece

    @pl.when(step == 0)
    def _():
        for i, (got_ref, m_ref) in enumerate(((got_a_ref, m_a_ref), (got_b_ref, m_b_ref))):
            ranks = slice(i * rank, (i + 1) * rank)
            low = low_ref[:, ranks]
            factor = None
            for head in range(PAIR):
                cols = slice(head * HDIM, (head + 1) * HDIM)
                got = got_ref[head, : 2 * rows]
                term = dot(got, m_ref[cols], 1, 0)
                factor = term if factor is None else factor + term
                u_ref[ranks, cols] = (dot(low, got, 0, 0) * scale).astype(BF)
            f_ref[:, ranks] = factor.astype(BF)

    f_own = f_ref[pl.ds(pl.multiple_of(core * rows, rows), rows)]
    f_other = f_ref[pl.ds(pl.multiple_of((1 - core) * rows, rows), rows)]
    line = lax.broadcasted_iota(jnp.int32, (2 * rank, block), 0)
    from_y = (line < rank) & (core == 1)
    for zz in range(Z_STEP):
        cols = slice(zz * block, (zz + 1) * block)
        gx = dot(f_own, xo_ref[:, cols], 0, 0) + dot(f_other, xt_ref[:, cols], 0, 0)
        gy = dot(f_own, yo_ref[:, cols], 0, 0) + dot(f_other, yt_ref[:, cols], 0, 0)
        g = (jnp.where(from_y, gy, gx) * scale).T.astype(BF)
        at = pl.ds(pl.multiple_of((step * Z_STEP + zz) * extra, extra), extra)
        for i in range(NX):
            g_ref[i, zz, :piece] = g[i * piece : (i + 1) * piece]
            g_ref[i, zz, piece:] = u_ref[at, i * 2 * rank : (i + 1) * 2 * rank]


def grad_partials(scale, core, x_own, x_other, y_own, y_other, got_a, got_b, low, m_a, m_b):
    rows, width = x_own.shape
    feats, rank = m_a.shape
    piece = width // (NX * NZ)
    extra = 2 * rank // NZ
    wide = pl.BlockSpec((rows, width * Z_STEP // NZ), lambda i: (0, i))
    whole = [pl.BlockSpec(a.shape, lambda i: (0, 0, 0)) for a in (got_a, got_b)]
    whole += [pl.BlockSpec(a.shape, lambda i: (0, 0)) for a in (low, m_a, m_b)]
    return pl.pallas_call(
        lambda *refs: grad_kernel(scale, *refs),
        grid=(NZ // Z_STEP,),
        out_shape=jax.ShapeDtypeStruct((NX, NZ, piece + extra, 2 * rank), BF),
        in_specs=[pl.BlockSpec(memory_space=pltpu.SMEM)] + [wide] * 4 + whole,
        out_specs=pl.BlockSpec((NX, Z_STEP, piece + extra, 2 * rank), lambda i: (0, i, 0, 0)),
        scratch_shapes=[pltpu.VMEM((2 * rows, 2 * rank), BF), pltpu.VMEM((2 * rank, feats), BF)],
        compiler_params=pltpu.CompilerParams(vmem_limit_bytes=16 * 1024 * 1024),
        cost_estimate=pl.CostEstimate(flops=800_000_000, bytes_accessed=7_500_000, transcendentals=0),
        name="grad_partials",
    )(core, x_own, x_other, y_own, y_other, got_a, got_b, low, m_a, m_b)


def exchange(parts, axes):
    return lax.all_to_all(parts, axes, split_axis=0, concat_axis=0, tiled=True)


def spread(block, axes, peers):
    return exchange(jnp.broadcast_to(block[None], (peers,) + block.shape), axes)


def across(block, by):
    return lax.ppermute(block, ("yl", "c"), [(i, i ^ by) for i in range(PAIR)])


def swap(block):
    return lax.ppermute(block, "c", [(0, 1), (1, 0)])


def pair_shift(block, by):
    pairs = NX * NY // 2
    return lax.ppermute(block, ("x", "yh"), [(i, i + by) for i in range(pairs) if 0 <= i + by < pairs])


def shards(
    inputs, queries, key_rows, values, frozen_output_gradient, out_grad, block_lists,
    down_qkv, up_qkv, output_down_projection, up_out,
):
    x_own, y_own = inputs[0], out_grad[0]
    rows, feats = queries.shape[1:]
    rank = output_down_projection.shape[1]
    own_cols = down_qkv.shape[1]
    slots = block_lists.shape[2]
    core = lax.axis_index("c")
    first = core == 0
    head = lax.axis_index(("yl", "c"))
    pair = lax.axis_index(("x", "yh"))
    line_axes = ("yh", "yl", "c")
    grad_scale = STRENGTH / math.sqrt(NX * NY * NZ * 2 * rows)
    core_id = core.astype(jnp.int32).reshape(1)

    stack = jnp.concatenate([queries[0], frozen_output_gradient[0], key_rows[0], values[0]], axis=0)
    lists = jnp.pad(block_lists[0].astype(BF), ((0, 12), (0, HDIM - slots)))
    shard = jnp.concatenate([down_qkv[0], down_qkv[1], up_out.T, down_qkv[2]], axis=1)
    copies = jnp.broadcast_to(shard.reshape(1, 2, -1), (2 * NY, 2, 2 * own_cols * rank))
    copies, stack = lax.optimization_barrier((copies, stack))
    line = exchange(copies, line_axes).reshape(2 * NY * own_cols, 4 * rank)
    line = lax.dynamic_slice_in_dim(line, core * 2 * rank, 2 * rank, 1)

    def for_head(h):
        return jnp.concatenate([lax.dynamic_slice_in_dim(stack, h * HDIM, HDIM, 1), lists], axis=0)

    got = [for_head(head)] + [across(for_head(head ^ by), by) for by in range(1, PAIR)]
    frames = [
        jnp.where(head == f, got[0], jnp.where(head ^ f == 1, got[1], jnp.where(head ^ f == 2, got[2], got[3])))
        for f in range(PAIR)
    ]
    frames = jnp.stack(frames)
    line, frames = lax.optimization_barrier((line, frames))
    q_pair, fog_pair, k_pair, v_pair = (
        frames[:, i * rows : (i + 1) * rows].reshape(PAIR * rows, HDIM) for i in range(4)
    )
    kv_pair = jnp.concatenate([k_pair, v_pair], axis=1)
    lists_pair = frames[:, 4 * rows : 4 * rows + BLK_DEV, :slots].reshape(PAIR * BLK_DEV, slots)
    left = pair_shift(kv_pair[rows:], 1)
    right = pair_shift(kv_pair[: REACH * rows], -1)
    window = (PAIR + 2 * REACH) * BLK_DEV
    ids = (PAIR * pair - REACH) * BLK_DEV + jnp.arange(window, dtype=jnp.int32)
    allowed = jnp.any(lists_pair[:, :, None] == ids.astype(F32)[None, None, :], axis=1) & (ids >= 0)[None]
    bias = jnp.repeat(jnp.where(allowed, 0.0, MASKED).astype(F32), BLK, axis=1)

    plane = spread(line, "z", NZ)
    plane, left, right, x_own, y_own = lax.optimization_barrier((plane, left, right, x_own, y_own))
    x_other = swap(x_own)
    y_other = lax.ppermute(y_own, "c", [(0, 1)])
    weights = spread(plane.reshape(-1, 2 * rank), "x", NX).reshape(NX, NZ, -1, 2 * rank)
    low = low_factors(core_id, x_own, x_other, y_own, y_other, weights)
    low_pair = lax.all_gather(low, ("yl", "c"))
    odp_head = lax.dynamic_slice_in_dim(output_down_projection, head * HDIM, HDIM, 0)

    send_a, to_left, to_own, to_right = attention(
        q_pair, left, kv_pair, right, fog_pair, low_pair, odp_head, bias
    )
    from_right = pair_shift(to_left, -1)
    from_left = pair_shift(to_right, 1)
    got_a = exchange(send_a, ("yl", "c"))
    m_a = jnp.where(first, up_qkv[0].T, output_down_projection)
    m_b = jnp.where(first, up_qkv[1].T, up_qkv[2].T)
    got_b = exchange(merge(to_own, from_left, from_right), ("yl", "c"))
    g = grad_partials(
        grad_scale, core_id, x_own, x_other, y_own, y_other, got_a, got_b, low, m_a, m_b
    )

    line_rows = 2 * NY * own_cols
    u_rows = g.shape[2] - line_rows
    step = exchange(g.reshape(NX, -1, 2 * rank), "x")
    step = step.astype(F32).sum(axis=0).astype(BF).reshape(NZ, -1, 2 * rank)
    step = exchange(step, "z")
    step = step.astype(F32).sum(axis=0).astype(BF)
    g_line = step[:line_rows].reshape(2 * NY, own_cols, 2 * rank)
    u_line = jnp.broadcast_to(step[line_rows:][None], (2 * NY, u_rows, 2 * rank))
    step = exchange(jnp.concatenate([g_line, u_line], axis=1), line_axes)
    step = step.reshape(NY, 2, own_cols + u_rows, 2 * rank).astype(F32).sum(axis=0)
    g_out = step[:, :own_cols]
    grad_down = jnp.stack([g_out[0, :, :rank], g_out[0, :, rank:], g_out[1, :, rank:]])
    grad_up_out = g_out[1, :, :rank].T
    u_mine = step[:, own_cols:].astype(BF).reshape(2 * u_rows, 2 * rank)
    u_all = spread(u_mine, ("x", "z"), NX * NZ).reshape(NX, NZ, 2, u_rows, 2 * rank)
    u_all = jnp.transpose(u_all, (2, 1, 3, 0, 4)).reshape(2, 2, rank, feats).astype(F32)
    grad_up = jnp.stack([u_all[0, 0], u_all[0, 1], u_all[1, 1]])
    grad_down_out = u_all[1, 0].T

    def own_frame(on_zero, on_one):
        return jnp.concatenate([jnp.where(first, on_zero[h], on_one[h]) for h in range(PAIR)], axis=1)[None]

    grad_q = own_frame(got_a[:, :rows], got_a[:, 2 * rows :])
    grad_k = own_frame(got_b[:, :rows], got_b[:, 2 * rows :])
    grad_v = own_frame(got_b[:, 2 * rows :], got_b[:, rows : 2 * rows])
    return grad_q, grad_k, grad_v, grad_down, grad_up, grad_down_out, grad_up_out


def solution(mesh):
    fine = Mesh(mesh.devices.reshape(NZ, NX, NY // 2, 2, 2), ("z", "x", "yh", "yl", "c"))
    ctx = ("x", "yh", "yl", "c")
    every = ("z",) + ctx
    tokens = P("z", ctx, None)
    return jax.shard_map(
        shards,
        mesh=fine,
        in_specs=(tokens,) * 7 + (P(None, every, None), P(), P(), P(None, every)),
        out_specs=(tokens,) * 3 + (P(None, every, None), P(), P(), P(None, every)),
        check_vma=False,
    )
```

time: 209 us -> 217 us (1.038)
  waiting for transfers between devices: 65.6 us -> 79.9 us
  local copies, waits for them, and re-layouts: 19.9 us -> 9.44 us
  blocking collectives: 27.2 us -> 32.4 us
  other arithmetic: 13.3 us -> 8.85 us
  starting transfers between devices: 67.6 us -> 70.7 us
    ppermute x8 -> x7, waiting for transfers between devices: 5.79 us -> 25.4 us  [the longest x4 24.3 us: pair_shift(): lax.ppermute(block, ('x', 'yh'), [(i, i + by) for i in range(pairs) if 0...]
    ppermute x4 -> x1, starting transfers between devices: 16.3 us -> 2.51 us  [swap(): return lax.ppermute(block, 'c', [(0, 1), (1, 0)])]
    all_to_all x6 -> x8, starting transfers between devices: 32.1 us -> 45.3 us  [exchange(): return lax.all_to_all(parts, axes, split_axis=0, concat_axis=0, tiled=True)]
    unnamed x56 -> x32, local copies, waits for them, and re-layouts: 10.1 us -> 2.44 us
    all_to_all x6 -> x8, waiting for transfers between devices: 59.7 us -> 54.5 us  [exchange(): return lax.all_to_all(parts, axes, split_axis=0, concat_axis=0, tiled=True)]
    all_gather x1, blocking collectives: 5.24 us -> 9.03 us  [shards(): low_pair = lax.all_gather(low, ('yl', 'c'))]
    ppermute x8 -> x7, starting transfers between devices: 17.9 us -> 21.6 us  [the longest x3 14.2 us: across(): return lax.ppermute(block, ('yl', 'c'), [(i, i ^ by) for i in range(PAIR)])]
    pallas_call x1 -> x2, Pallas kernels: 6.37 us -> 4.23 us  [the longest x1 3.36 us: attention(): pl.pallas_call(attention_kernel, out_shape=[shape((PAIR, 3 * tokens // PA...]
  transfers between devices with their start and end apart: 19 -> 17, of which waited for: 9 -> 11; matrix products, arithmetic and copies ran while one was open for 9% -> 4% of each run, Pallas kernels for 1% -> 0%
where the time goes in v3:
time: 217 us; the launch traced here: 216 us
  waiting for transfers between devices  79.9 us (37%)
  starting transfers between devices  70.7 us (33%)
  blocking collectives  32.4 us (15%)
  Pallas kernels  13.3 us (6%)
  local copies, waits for them, and re-layouts  9.44 us (4%)
  other arithmetic  8.85 us (4%)
    all_to_all x8, waiting for transfers between devices, exchange(): return lax.all_to_all(parts, axes, split_axis=0, concat_axis=0, tiled=True)  54.5 us
    all_to_all x8, starting transfers between devices, exchange(): return lax.all_to_all(parts, axes, split_axis=0, concat_axis=0, tiled=True)  45.3 us
    ppermute x4, waiting for transfers between devices, pair_shift(): lax.ppermute(block, ('x', 'yh'), [(i, i + by) for i in range(pairs) if 0...  24.3 us
    all_to_all x1, blocking collectives, exchange(): return lax.all_to_all(parts, axes, split_axis=0, concat_axis=0, tiled=True)  23.4 us
    ppermute x3, starting transfers between devices, across(): return lax.ppermute(block, ('yl', 'c'), [(i, i ^ by) for i in range(PAIR)])  14.2 us
    all_gather x1, blocking collectives, shards(): low_pair = lax.all_gather(low, ('yl', 'c'))  9.03 us
    ppermute x4, starting transfers between devices, pair_shift(): lax.ppermute(block, ('x', 'yh'), [(i, i + by) for i in range(pairs) if 0...  7.32 us
    pallas_call x1, Pallas kernels, grad_partials(): pl.pallas_call(lambda *refs: grad_kernel(scale, *refs), grid=(NZ // Z_STE...  4.96 us
  transfers between devices with their start and end apart: 17, of which 11 were waited for; matrix products, arithmetic and copies ran while one was open for 4% of the time, Pallas kernels for 0%

profile of v3, /device:TPU:1, one launch (start us, length us, event | category | flops | bytes accessed | tf_op | source)
XLA Modules:
  0.0 215.7 jit_solution(2573689069173163464)
XLA Ops:
  0.7 0.8 fusion.24
  1.5 0.8 pad_maximum_fusion.6
  2.3 1.1 pad_maximum_fusion.1
  3.4 0.7 broadcast_in_dim.56
  4.1 0.7 convert_bitcast_fusion.1
  4.9 8.8 %collective-permute-start = (bf16[528,128]{1,0:T(8,128)(2,1)S(1)}, bf16[528,128]{1,0:T(8,128)(2,1)S(1)}, u32[]{:S(2)}, u32[]{:S(2)}) collective-permute-start(bf16[528,128]{1,0:T(8,128)(2,1)S(1)} %get-tuple-element.113), channel_id=1, source_target_pairs={{0,1},{1,0},{2,3},{3,2},{4,5},{5,4},{6,7},{7,6},{8,9},{9,8},{10,11... | collective-permute-start | bytes 405512 | tf_op jit(solution)/shard_map/ppermute | solution.py:248
  13.7 1.9 collective-permute-start.1
  15.7 3.5 %collective-permute-start.2 = (bf16[528,128]{1,0:T(8,128)(2,1)S(1)}, bf16[528,128]{1,0:T(8,128)(2,1)S(1)}, u32[]{:S(2)}, u32[]{:S(2)}) collective-permute-start(bf16[528,128]{1,0:T(8,128)(2,1)S(1)} %get-tuple-element.112), channel_id=1, source_target_pairs={{0,3},{1,2},{2,1},{3,0},{4,7},{5,6},{6,5},{7,4},{8,11},{9,10},{10,... | collective-permute-start | bytes 405512 | tf_op jit(solution)/shard_map/ppermute | solution.py:248
  19.2 3.5 %all-to-all-start = ((bf16[16,2,1280]{2,1,0:T(2,128)(2,1)}), bf16[16,2,1280]{2,1,0:T(2,128)(2,1)S(1)}, u32[]{:S(2)}, u32[]{:S(2)}) async-start(bf16[16,2,1280]{2,1,0:T(2,128)(2,1)} %broadcast_in_dim.56), calls=%async_computation | async-start | bytes 163840 | tf_op jit(solution)/shard_map/all_to_all | solution.py:240
  22.7 1.1 collective-permute-done.2
  23.8 0.1 select_bitcast_fusion.3
  24.2 6.8 %all-to-all-done = bf16[16,2,1280]{2,1,0:T(2,128)(2,1)S(1)} async-done(((bf16[16,2,1280]{2,1,0:T(2,128)(2,1)}), bf16[16,2,1280]{2,1,0:T(2,128)(2,1)S(1)}, u32[]{:S(2)}, u32[]{:S(2)}) %all-to-all-start) | async-done | bytes 81952 | tf_op jit(solution)/shard_map/all_to_all | solution.py:240
  31.0 0.8 broadcast_in_dim.57
  31.8 8.4 %all-to-all-start.1 = ((bf16[8,160,128]{2,1,0:T(8,128)(2,1)}), bf16[8,160,128]{2,1,0:T(8,128)(2,1)S(1)}, u32[]{:S(2)}, u32[]{:S(2)}) async-start(bf16[8,160,128]{2,1,0:T(8,128)(2,1)} %broadcast_in_dim.57), calls=%async_computation.1 | async-start | bytes 655360 | tf_op jit(solution)/shard_map/all_to_all | solution.py:240
  40.3 2.2 %collective-permute-start.3 = (bf16[384,256]{1,0:T(8,128)(2,1)S(1)}, bf16[384,256]{1,0:T(8,128)(2,1)S(1)}, u32[]{:S(2)}, u32[]{:S(2)}) collective-permute-start(bf16[384,256]{1,0:T(8,128)(2,1)S(1)} %get-tuple-element.103), channel_id=1, source_target_pairs={{0,4},{4,8},{8,12},{12,16},{16,20},{20,24},{24,28},{28,32},{32,36}... | collective-permute-start | bytes 589832 | tf_op jit(solution)/shard_map/ppermute | solution.py:257
  42.5 1.3 collective-permute-start.4
  43.8 2.3 %collective-permute-done.3.left_ref = bf16[384,256]{1,0:T(8,128)(2,1)S(1)} collective-permute-done((bf16[384,256]{1,0:T(8,128)(2,1)S(1)}, bf16[384,256]{1,0:T(8,128)(2,1)S(1)}, u32[]{:S(2)}, u32[]{:S(2)}) %collective-permute-start.3) | collective-permute-done | bytes 196640 | tf_op jit(solution)/shard_map/ppermute | solution.py:257
  46.2 10.1 %collective-permute-done.4.right_ref = bf16[384,256]{1,0:T(8,128)(2,1)S(1)} collective-permute-done((bf16[384,256]{1,0:T(8,128)(2,1)S(1)}, bf16[384,256]{1,0:T(8,128)(2,1)S(1)}, u32[]{:S(2)}, u32[]{:S(2)}) %collective-permute-start.4) | collective-permute-done | bytes 196640 | tf_op jit(solution)/shard_map/ppermute | solution.py:257
  56.3 2.5 %collective-permute-start.5 = (bf16[128,5120]{1,0:T(8,128)(2,1)S(1)}, bf16[128,5120]{1,0:T(8,128)(2,1)}, u32[]{:S(2)}, u32[]{:S(2)}) collective-permute-start(bf16[128,5120]{1,0:T(8,128)(2,1)S(1)} %bitcast.98), channel_id=1, source_target_pairs={{0,1},{1,0},{2,3},{3,2},{4,5},{5,4},{6,7},{7,6},{8,9},{9,8},{10,11... | collective-permute-start | bytes 3932168 | tf_op jit(solution)/shard_map/ppermute | solution.py:252
  58.8 1.3 collective-permute-start.6
  60.1 1.2 broadcast_in_dim.59
  61.3 5.3 %all-to-all-start.2 = ((bf16[4,1280,128]{2,1,0:T(8,128)(2,1)}), bf16[4,1280,128]{2,1,0:T(8,128)(2,1)S(1)}, u32[]{:S(2)}, u32[]{:S(2)}) async-start(bf16[4,1280,128]{2,1,0:T(8,128)(2,1)} %broadcast_in_dim.59), calls=%async_computation.2 | async-start | bytes 2621440 | tf_op jit(solution)/shard_map/all_to_all | solution.py:240
  66.6 0.1 copy.73
  66.8 0.7 slice.176
  67.6 0.1 compare_reduce_fusion
  67.7 0.1 broadcast_in_dim.62
  67.9 0.1 reshape.115.bias_ref
  68.0 1.0 pad_maximum_fusion.3.own_ref
  69.0 13.1 %all-to-all-done.2 = bf16[4,1280,128]{2,1,0:T(8,128)(2,1)S(1)} async-done(((bf16[4,1280,128]{2,1,0:T(8,128)(2,1)}), bf16[4,1280,128]{2,1,0:T(8,128)(2,1)S(1)}, u32[]{:S(2)}, u32[]{:S(2)}) %all-to-all-start.2) | async-done | bytes 1310752 | tf_op jit(solution)/shard_map/all_to_all | solution.py:240
  82.1 4.1 %low_factors.1.refs_7_ = bf16[256,128]{1,0:T(8,128)(2,1)S(1)} custom-call(s32[1]{0:T(128)} %bitcast.19.core_ref.refs_0_, bf16[128,5120]{1,0:T(8,128)(2,1)S(1)} %bitcast.99, bf16[128,5120]{1,0:T(8,128)(2,1)} %collective-permute-done.5.xt_ref.refs_2_, bf16[128,5120]{1,0:T(8,128)(2,1)} %bitcast.17.yo_ref.refs_3_, ...), custom_call_target="tpu_custom_call" | custom-call | flops 700000000 | bytes 6600000 | tf_op jit(solution)/shard_map/low_factors/pallas_call | solution.py:163
  86.2 9.0 %all-gather = bf16[1024,128]{1,0:T(8,128)(2,1)S(1)} all-gather(bf16[256,128]{1,0:T(8,128)(2,1)S(1)} %low_factors.1.refs_7_), channel_id=2, replica_groups=mesh['z'=8,'x'=4,'yh'=4,'yl'=2,'c'=2] {'yl','c'}, dimensions={0}, use_global_device_ids=true | all-gather | bytes 327680 | tf_op jit(solution)/shard_map/all_gather | solution.py:313
  95.3 3.4 %attention.1 = (bf16[4,384,128]{2,1,0:T(8,128)(2,1)}, bf16[384,256]{1,0:T(8,128)(2,1)S(1)}, f32[512,256]{1,0:T(8,128)S(1)}, bf16[384,256]{1,0:T(8,128)(2,1)}) custom-call(bf16[512,128]{1,0:T(8,128)(2,1)S(1)} %bitcast.103, bf16[384,256]{1,0:T(8,128)(2,1)S(1)} %collective-permute-done.3.left_ref, bf16[512,256]{1,0:T(8,128)(2,1)S(1)} %pad_maximum_fusion.3.own_ref, ...), custom_call_target="tpu_custom_call" | custom-call | flops 700000000 | bytes 3000000 | tf_op jit(solution)/shard_map/attention/pallas_call | solution.py:75
  98.6 0.7 copy-done.3
  99.3 3.7 %all-to-all-start.3 = ((bf16[4,384,128]{2,1,0:T(8,128)(2,1)}), bf16[4,384,128]{2,1,0:T(8,128)(2,1)S(1)}, u32[]{:S(2)}, u32[]{:S(2)}) async-start(bf16[4,384,128]{2,1,0:T(8,128)(2,1)} %get-tuple-element.29), calls=%async_computation.3 | async-start | bytes 786432 | tf_op jit(solution)/shard_map/all_to_all | solution.py:240
  103.0 2.6 %collective-permute-start.7 = (bf16[384,256]{1,0:T(8,128)(2,1)}, bf16[384,256]{1,0:T(8,128)(2,1)S(1)}, u32[]{:S(2)}, u32[]{:S(2)}) collective-permute-start(bf16[384,256]{1,0:T(8,128)(2,1)} %get-tuple-element.31), channel_id=1, source_target_pairs={{0,4},{4,8},{8,12},{12,16},{16,20},{20,24},{24,28},{28,32},{32,36}... | collective-permute-start | bytes 589832 | tf_op jit(solution)/shard_map/ppermute | solution.py:257
  105.6 1.3 collective-permute-start.8
  106.9 7.9 %collective-permute-done.7.from_left_ref = bf16[384,256]{1,0:T(8,128)(2,1)S(1)} collective-permute-done((bf16[384,256]{1,0:T(8,128)(2,1)}, bf16[384,256]{1,0:T(8,128)(2,1)S(1)}, u32[]{:S(2)}, u32[]{:S(2)}) %collective-permute-start.7) | collective-permute-done | bytes 196640 | tf_op jit(solution)/shard_map/ppermute | solution.py:257
  114.8 4.0 %collective-permute-done.8.from_right_ref = bf16[384,256]{1,0:T(8,128)(2,1)S(1)} collective-permute-done((bf16[384,256]{1,0:T(8,128)(2,1)}, bf16[384,256]{1,0:T(8,128)(2,1)S(1)}, u32[]{:S(2)}, u32[]{:S(2)}) %collective-permute-start.8) | collective-permute-done | bytes 196640 | tf_op jit(solution)/shard_map/ppermute | solution.py:257
  118.8 0.9 merge.1
  119.6 4.8 %all-to-all-start.4 = ((bf16[4,384,128]{2,1,0:T(8,128)(2,1)}), bf16[4,384,128]{2,1,0:T(8,128)(2,1)S(1)}, u32[]{:S(2)}, u32[]{:S(2)}) async-start(bf16[4,384,128]{2,1,0:T(8,128)(2,1)} %merge.1), calls=%async_computation.4 | async-start | bytes 786432 | tf_op jit(solution)/shard_map/all_to_all | solution.py:240
  124.5 0.1 copy.88
  124.6 0.1 copy.89
  124.7 0.1 copy.87
  124.9 6.1 %all-to-all-done.4.refs_6_ = bf16[4,384,128]{2,1,0:T(8,128)(2,1)S(1)} async-done(((bf16[4,384,128]{2,1,0:T(8,128)(2,1)}), bf16[4,384,128]{2,1,0:T(8,128)(2,1)S(1)}, u32[]{:S(2)}, u32[]{:S(2)}) %all-to-all-start.4) | async-done | bytes 393248 | tf_op jit(solution)/shard_map/all_to_all | solution.py:240
  131.0 5.0 %grad_partials.1 = bf16[4,8,176,128]{3,2,1,0:T(8,128)(2,1)S(1)} custom-call(s32[1]{0:T(128)} %bitcast.19.core_ref.refs_0_, bf16[128,5120]{1,0:T(8,128)(2,1)S(1)} %bitcast.100, bf16[128,5120]{1,0:T(8,128)(2,1)} %collective-permute-done.5.xt_ref.refs_2_, bf16[128,5120]{1,0:T(8,128)(2,1)} %bitcast.17.yo_ref.refs_3_, ...), custom_call_target="tpu_custom_call" | custom-call | flops 800000000 | bytes 7500000 | tf_op jit(solution)/shard_map/grad_partials/pallas_call | solution.py:226
  136.0 23.4 %all_to_all.45 = bf16[4,1408,128]{2,1,0:T(8,128)(2,1)S(1)} all-to-all(bf16[4,1408,128]{2,1,0:T(8,128)(2,1)S(1)} %bitcast.96), channel_id=1, replica_groups=mesh['z'=8,'x'=4,'yh'=4,'yl'=2,'c'=2] {'x'}, dimensions={0} | all-to-all | bytes 2883584 | tf_op jit(solution)/shard_map/all_to_all | solution.py:240
  159.4 1.0 reduce_sum.33
  160.4 6.6 %all-to-all-start.6 = ((bf16[8,176,128]{2,1,0:T(8,128)(2,1)}), bf16[8,176,128]{2,1,0:T(8,128)(2,1)S(1)}, u32[]{:S(2)}, u32[]{:S(2)}) async-start(bf16[8,176,128]{2,1,0:T(8,128)(2,1)} %bitcast.44), calls=%async_computation.6 | async-start | bytes 720896 | tf_op jit(solution)/shard_map/all_to_all | solution.py:240
  167.1 0.7 maximum_bitcast_fusion
  167.7 10.7 %all-to-all-done.6 = bf16[8,176,128]{2,1,0:T(8,128)(2,1)S(1)} async-done(((bf16[8,176,128]{2,1,0:T(8,128)(2,1)}), bf16[8,176,128]{2,1,0:T(8,128)(2,1)S(1)}, u32[]{:S(2)}, u32[]{:S(2)}) %all-to-all-start.6) | async-done | bytes 360480 | tf_op jit(solution)/shard_map/all_to_all | solution.py:240
  178.5 0.7 pad_maximum_fusion.4
  179.2 9.0 %all-to-all-start.7 = ((bf16[16,26,128]{2,1,0:T(8,128)(2,1)}), bf16[16,26,128]{2,1,0:T(8,128)(2,1)S(1)}, u32[]{:S(2)}, u32[]{:S(2)}) async-start(bf16[16,26,128]{2,1,0:T(8,128)(2,1)} %pad_maximum_fusion.4), calls=%async_computation.7 | async-start | bytes 262144 | tf_op jit(solution)/shard_map/all_to_all | solution.py:240
  188.3 9.1 %all-to-all-done.7 = bf16[16,26,128]{2,1,0:T(8,128)(2,1)S(1)} async-done(((bf16[16,26,128]{2,1,0:T(8,128)(2,1)}), bf16[16,26,128]{2,1,0:T(8,128)(2,1)S(1)}, u32[]{:S(2)}, u32[]{:S(2)}) %all-to-all-start.7) | async-done | bytes 106528 | tf_op jit(solution)/shard_map/all_to_all | solution.py:240
  197.6 0.7 broadcast_in_dim.68
  198.3 3.9 %all-to-all-start.8 = ((bf16[32,32,128]{2,1,0:T(8,128)(2,1)}), bf16[32,32,128]{2,1,0:T(8,128)(2,1)S(1)}, u32[]{:S(2)}, u32[]{:S(2)}) async-start(bf16[32,32,128]{2,1,0:T(8,128)(2,1)} %broadcast_in_dim.68), calls=%async_computation.8 | async-start | bytes 524288 | tf_op jit(solution)/shard_map/all_to_all | solution.py:240
  202.2 0.7 maximum_bitcast_fusion.2
  202.9 0.7 maximum_bitcast_fusion.1
  203.7 0.6 copy.82
  204.3 0.6 copy.100
  204.9 8.8 %all-to-all-done.8 = bf16[32,32,128]{2,1,0:T(8,128)(2,1)S(1)} async-done(((bf16[32,32,128]{2,1,0:T(8,128)(2,1)}), bf16[32,32,128]{2,1,0:T(8,128)(2,1)S(1)}, u32[]{:S(2)}, u32[]{:S(2)}) %all-to-all-start.8) | async-done | bytes 262176 | tf_op jit(solution)/shard_map/all_to_all | solution.py:240
  213.7 0.3 copy.81
  214.1 0.2 reshape.121
  214.3 0.7 slice_bitcast_fusion
  215.0 0.8 pad_maximum_fusion.2
  (63 shorter events, 1.1 us)
Async XLA Ops:
  4.9 17.8 %collective-permute-start = (bf16[528,128]{1,0:T(8,128)(2,1)S(1)}, bf16[528,128]{1,0:T(8,128)(2,1)S(1)}, u32[]{:S(2)}, u32[]{:S(2)}) collective-permute-start(bf16[528,128]{1,0:T(8,128)(2,1)S(1)} %get-tuple-element.113), channel_id=1, source_target_pairs={{0,1},{1,0},{2,3},{3,2},{4,5},{5,4},{6,7},{7,6},{8,9},{9,8},{10,11... | collective-permute-start | bytes 405512 | tf_op jit(solution)/shard_map/ppermute | solution.py:248
  13.7 9.0 %collective-permute-start.1 = (bf16[528,128]{1,0:T(8,128)(2,1)S(1)}, bf16[528,128]{1,0:T(8,128)(2,1)S(1)}, u32[]{:S(2)}, u32[]{:S(2)}) collective-permute-start(bf16[528,128]{1,0:T(8,128)(2,1)S(1)} %get-tuple-element.114), channel_id=1, source_target_pairs={{0,2},{1,3},{2,0},{3,1},{4,6},{5,7},{6,4},{7,5},{8,10},{9,11},{10,... | collective-permute-start | bytes 405512 | tf_op jit(solution)/shard_map/ppermute | solution.py:248
  15.7 8.2 %collective-permute-start.2 = (bf16[528,128]{1,0:T(8,128)(2,1)S(1)}, bf16[528,128]{1,0:T(8,128)(2,1)S(1)}, u32[]{:S(2)}, u32[]{:S(2)}) collective-permute-start(bf16[528,128]{1,0:T(8,128)(2,1)S(1)} %get-tuple-element.112), channel_id=1, source_target_pairs={{0,3},{1,2},{2,1},{3,0},{4,7},{5,6},{6,5},{7,4},{8,11},{9,10},{10,... | collective-permute-start | bytes 405512 | tf_op jit(solution)/shard_map/ppermute | solution.py:248
  19.2 11.7 %all-to-all-start = ((bf16[16,2,1280]{2,1,0:T(2,128)(2,1)}), bf16[16,2,1280]{2,1,0:T(2,128)(2,1)S(1)}, u32[]{:S(2)}, u32[]{:S(2)}) async-start(bf16[16,2,1280]{2,1,0:T(2,128)(2,1)} %broadcast_in_dim.56), calls=%async_computation | async-start | bytes 163840 | tf_op jit(solution)/shard_map/all_to_all | solution.py:240
  24.1 37.2 %copy-start.4 = (bf16[4,528,128]{2,1,0:T(8,128)(2,1)}, bf16[4,528,128]{2,1,0:T(8,128)(2,1)S(1)}, u32[]{:S(2)}) copy-start(bf16[4,528,128]{2,1,0:T(8,128)(2,1)S(1)} %pad_maximum_fusion) | copy-start | bytes 1622020
  31.0 25.3 %copy-start = (bf16[1,128,5120]{2,1,0:T(8,128)(2,1)S(1)}, bf16[1,128,5120]{2,1,0:T(8,128)(2,1)}, u32[]{:S(2)}) copy-start(bf16[1,128,5120]{2,1,0:T(8,128)(2,1)} %param.11) | copy-start | bytes 3932164
  31.8 24.5 %all-to-all-start.1 = ((bf16[8,160,128]{2,1,0:T(8,128)(2,1)}), bf16[8,160,128]{2,1,0:T(8,128)(2,1)S(1)}, u32[]{:S(2)}, u32[]{:S(2)}) async-start(bf16[8,160,128]{2,1,0:T(8,128)(2,1)} %broadcast_in_dim.57), calls=%async_computation.1 | async-start | bytes 655360 | tf_op jit(solution)/shard_map/all_to_all | solution.py:240
  40.3 2.2 %copy-start.5 = (bf16[4,128,128]{2,1,0:T(8,128)(2,1)}, bf16[4,128,128]{2,1,0:T(8,128)(2,1)S(1)}, u32[]{:S(2)}) copy-start(bf16[4,128,128]{2,1,0:T(8,128)(2,1)S(1)} %get-tuple-element.76) | copy-start | bytes 393220
  40.3 2.2 %copy-start.6 = (bf16[4,128,128]{2,1,0:T(8,128)(2,1)}, bf16[4,128,128]{2,1,0:T(8,128)(2,1)S(1)}, u32[]{:S(2)}) copy-start(bf16[4,128,128]{2,1,0:T(8,128)(2,1)S(1)} %get-tuple-element.77) | copy-start | bytes 393220
  40.3 5.8 %collective-permute-start.3 = (bf16[384,256]{1,0:T(8,128)(2,1)S(1)}, bf16[384,256]{1,0:T(8,128)(2,1)S(1)}, u32[]{:S(2)}, u32[]{:S(2)}) collective-permute-start(bf16[384,256]{1,0:T(8,128)(2,1)S(1)} %get-tuple-element.103), channel_id=1, source_target_pairs={{0,4},{4,8},{8,12},{12,16},{16,20},{20,24},{24,28},{28,32},{32,36}... | collective-permute-start | bytes 589832 | tf_op jit(solution)/shard_map/ppermute | solution.py:257
  42.5 13.7 %collective-permute-start.4 = (bf16[384,256]{1,0:T(8,128)(2,1)S(1)}, bf16[384,256]{1,0:T(8,128)(2,1)S(1)}, u32[]{:S(2)}, u32[]{:S(2)}) collective-permute-start(bf16[384,256]{1,0:T(8,128)(2,1)S(1)} %get-tuple-element.102), channel_id=1, source_target_pairs={{4,0},{8,4},{12,8},{16,12},{20,16},{24,20},{28,24},{32,28},{36,32}... | collective-permute-start | bytes 589832 | tf_op jit(solution)/shard_map/ppermute | solution.py:257
  56.2 5.1 %copy-start.1 = (bf16[384,256]{1,0:T(8,128)(2,1)}, bf16[384,256]{1,0:T(8,128)(2,1)S(1)}, u32[]{:S(2)}) copy-start(bf16[384,256]{1,0:T(8,128)(2,1)S(1)} %collective-permute-done.4.right_ref) | copy-start | bytes 589828
  56.3 25.8 %collective-permute-start.5 = (bf16[128,5120]{1,0:T(8,128)(2,1)S(1)}, bf16[128,5120]{1,0:T(8,128)(2,1)}, u32[]{:S(2)}, u32[]{:S(2)}) collective-permute-start(bf16[128,5120]{1,0:T(8,128)(2,1)S(1)} %bitcast.98), channel_id=1, source_target_pairs={{0,1},{1,0},{2,3},{3,2},{4,5},{5,4},{6,7},{7,6},{8,9},{9,8},{10,11... | collective-permute-start | bytes 3932168 | tf_op jit(solution)/shard_map/ppermute | solution.py:252
  58.8 23.3 %collective-permute-start.6 = (bf16[128,5120]{1,0:T(8,128)(2,1)}, bf16[128,5120]{1,0:T(8,128)(2,1)}, u32[]{:S(2)}, u32[]{:S(2)}) collective-permute-start(bf16[128,5120]{1,0:T(8,128)(2,1)} %bitcast.17.yo_ref.refs_3_), channel_id=1, source_target_pairs={{0,1},{2,3},{4,5},{6,7},{8,9},{10,11},{12,13},{14,15},{16,17},{18,... | collective-permute-start | bytes 3932168 | tf_op jit(solution)/shard_map/ppermute | solution.py:310
  61.3 5.3 %copy-start.10 = (bf16[512,64]{0,1:T(8,128)(2,1)S(1)}, bf16[512,64]{0,1:T(8,128)(2,1)}, u32[]{:S(2)}) copy-start(bf16[512,64]{0,1:T(8,128)(2,1)} %param.20) | copy-start | bytes 196612
  61.3 20.7 %all-to-all-start.2 = ((bf16[4,1280,128]{2,1,0:T(8,128)(2,1)}), bf16[4,1280,128]{2,1,0:T(8,128)(2,1)S(1)}, u32[]{:S(2)}, u32[]{:S(2)}) async-start(bf16[4,1280,128]{2,1,0:T(8,128)(2,1)} %broadcast_in_dim.59), calls=%async_computation.2 | async-start | bytes 2621440 | tf_op jit(solution)/shard_map/all_to_all | solution.py:240
  66.7 1.0 copy-start.7
  82.1 13.2 %copy-start.2 = (bf16[384,256]{1,0:T(8,128)(2,1)S(1)}, bf16[384,256]{1,0:T(8,128)(2,1)}, u32[]{:S(2)}) copy-start(bf16[384,256]{1,0:T(8,128)(2,1)} %copy-done.1) | copy-start | bytes 589828
  98.6 0.7 copy-start.3
  99.3 25.2 %copy-start.9 = (bf16[3,64,512]{2,1,0:T(8,128)(2,1)S(1)}, bf16[3,64,512]{2,1,0:T(8,128)(2,1)}, u32[]{:S(2)}) copy-start(bf16[3,64,512]{2,1,0:T(8,128)(2,1)} %param.19) | copy-start | bytes 589828
  99.3 20.3 %all-to-all-start.3 = ((bf16[4,384,128]{2,1,0:T(8,128)(2,1)}), bf16[4,384,128]{2,1,0:T(8,128)(2,1)S(1)}, u32[]{:S(2)}, u32[]{:S(2)}) async-start(bf16[4,384,128]{2,1,0:T(8,128)(2,1)} %get-tuple-element.29), calls=%async_computation.3 | async-start | bytes 786432 | tf_op jit(solution)/shard_map/all_to_all | solution.py:240
  103.0 11.8 %collective-permute-start.7 = (bf16[384,256]{1,0:T(8,128)(2,1)}, bf16[384,256]{1,0:T(8,128)(2,1)S(1)}, u32[]{:S(2)}, u32[]{:S(2)}) collective-permute-start(bf16[384,256]{1,0:T(8,128)(2,1)} %get-tuple-element.31), channel_id=1, source_target_pairs={{0,4},{4,8},{8,12},{12,16},{16,20},{20,24},{24,28},{28,32},{32,36}... | collective-permute-start | bytes 589832 | tf_op jit(solution)/shard_map/ppermute | solution.py:257
  105.6 13.2 %collective-permute-start.8 = (bf16[384,256]{1,0:T(8,128)(2,1)}, bf16[384,256]{1,0:T(8,128)(2,1)S(1)}, u32[]{:S(2)}, u32[]{:S(2)}) collective-permute-start(bf16[384,256]{1,0:T(8,128)(2,1)} %copy-done.3), channel_id=1, source_target_pairs={{4,0},{8,4},{12,8},{16,12},{20,16},{24,20},{28,24},{32,28},{36,32}... | collective-permute-start | bytes 589832 | tf_op jit(solution)/shard_map/ppermute | solution.py:257
  118.8 6.1 %copy-start.8 = (bf16[512,64]{1,0:T(8,128)(2,1)S(1)}, bf16[512,64]{1,0:T(8,128)(2,1)}, u32[]{:S(2)}) copy-start(bf16[512,64]{1,0:T(8,128)(2,1)} %copy-done.7) | copy-start | bytes 196612
  119.6 11.4 %all-to-all-start.4 = ((bf16[4,384,128]{2,1,0:T(8,128)(2,1)}), bf16[4,384,128]{2,1,0:T(8,128)(2,1)S(1)}, u32[]{:S(2)}, u32[]{:S(2)}) async-start(bf16[4,384,128]{2,1,0:T(8,128)(2,1)} %merge.1), calls=%async_computation.4 | async-start | bytes 786432 | tf_op jit(solution)/shard_map/all_to_all | solution.py:240
  160.4 18.0 %all-to-all-start.6 = ((bf16[8,176,128]{2,1,0:T(8,128)(2,1)}), bf16[8,176,128]{2,1,0:T(8,128)(2,1)S(1)}, u32[]{:S(2)}, u32[]{:S(2)}) async-start(bf16[8,176,128]{2,1,0:T(8,128)(2,1)} %bitcast.44), calls=%async_computation.6 | async-start | bytes 720896 | tf_op jit(solution)/shard_map/all_to_all | solution.py:240
  179.2 18.2 %all-to-all-start.7 = ((bf16[16,26,128]{2,1,0:T(8,128)(2,1)}), bf16[16,26,128]{2,1,0:T(8,128)(2,1)S(1)}, u32[]{:S(2)}, u32[]{:S(2)}) async-start(bf16[16,26,128]{2,1,0:T(8,128)(2,1)} %pad_maximum_fusion.4), calls=%async_computation.7 | async-start | bytes 262144 | tf_op jit(solution)/shard_map/all_to_all | solution.py:240
  198.3 15.3 %all-to-all-start.8 = ((bf16[32,32,128]{2,1,0:T(8,128)(2,1)}), bf16[32,32,128]{2,1,0:T(8,128)(2,1)S(1)}, u32[]{:S(2)}, u32[]{:S(2)}) async-start(bf16[32,32,128]{2,1,0:T(8,128)(2,1)} %broadcast_in_dim.68), calls=%async_computation.8 | async-start | bytes 524288 | tf_op jit(solution)/shard_map/all_to_all | solution.py:240

commit v4 on v2

--- a/solution.py
+++ b/solution.py
@@ -26,50 +26,35 @@
 
 def attention_kernel(
     core_ref, q_ref, l2_ref, l1_ref, own_ref, r1_ref, r2_ref, fog_ref, low_ref, odp_ref, bias_ref,
-    kept_ref, send_ref, dq_ref, pl2_ref, pl1_ref, pown_ref, pr1_ref, pr2_ref, attn_ref,
+    kept_ref, send_ref, dq_ref, pl2_ref, pl1_ref, pown_ref, pr1_ref, pr2_ref, attn_ref, kv_ref,
 ):
-    kv_refs = (l2_ref, l1_ref, own_ref, r1_ref, r2_ref)
     part_refs = (pl2_ref, pl1_ref, pown_ref, pr1_ref, pr2_ref)
     rows, half = q_ref.shape
-    low_out = low_ref[1][:, : odp_ref.shape[1]]
-    dout = (fog_ref[...].astype(F32) + STRENGTH * dot(low_out, odp_ref[...], 1, 1)).astype(BF)
+    for ref, (a, b) in zip((l2_ref, l1_ref, own_ref, r1_ref, r2_ref), SEGMENTS):
+        kv_ref[a:b] = ref[...]
+    window = kv_ref.shape[0]
+    dout = (fog_ref[...].astype(F32) + STRENGTH * dot(low_ref[1][:, : odp_ref.shape[1]], odp_ref[...], 1, 1)).astype(BF)
     bias = bias_ref[...]
     for head in range(half // HDIM):
         cols = slice(head * HDIM, (head + 1) * HDIM)
         vcols = slice(half + head * HDIM, half + (head + 1) * HDIM)
-        q = q_ref[:, cols]
-        dout_h = dout[:, cols]
-        keys = [ref[:, cols] for ref in kv_refs]
-        vals = [ref[:, vcols] for ref in kv_refs]
-        scores = []
-        for k, (a, b) in zip(keys, SEGMENTS):
-            s = dot(q, k, 1, 1) * SCALING
-            s = s.reshape(8, BLK, b - a) + bias[:, None, a:b]
-            scores.append(s.reshape(8 * BLK, b - a))
-        top = scores[0].max(axis=1, keepdims=True)
-        for s in scores[1:]:
-            top = jnp.maximum(top, s.max(axis=1, keepdims=True))
-        weights = [jnp.exp(s - top) for s in scores]
-        total = weights[0].sum(axis=1, keepdims=True)
-        for w in weights[1:]:
-            total = total + w.sum(axis=1, keepdims=True)
-        inverse = 1.0 / total
-        probs = [w * inverse for w in weights]
-        probs_low = [p.astype(BF) for p in probs]
-        attn = dot(probs_low[0], vals[0], 1, 0)
-        for p, v in zip(probs_low[1:], vals[1:]):
-            attn = attn + dot(p, v, 1, 0)
-        attn = attn.astype(BF)
+        q, dout_h = q_ref[:, cols], dout[:, cols]
+        k, v = kv_ref[:, cols], kv_ref[:, vcols]
+        s = (dot(q, k, 1, 1) * SCALING).reshape(8, BLK, window)
+        s = (s + bias[:, None, :]).reshape(rows, window)
+        weights = jnp.exp(s - s.max(axis=1, keepdims=True))
+        probs = weights * (1.0 / weights.sum(axis=1, keepdims=True))
+        probs_low = probs.astype(BF)
+        attn = dot(probs_low, v, 1, 0).astype(BF)
         attn_ref[:, cols] = attn
         delta = (dout_h.astype(F32) * attn.astype(F32)).sum(axis=1, keepdims=True)
-        dq = None
-        for k, v, p, p_low, out in zip(keys, vals, probs, probs_low, part_refs):
-            dscore = (p * (dot(dout_h, v, 1, 1) - delta)).astype(BF)
-            term = dot(dscore, k, 1, 0)
-            dq = term if dq is None else dq + term
-            out[:, cols] = (dot(dscore, q, 0, 0) * SCALING).astype(out.dtype)
-            out[:, vcols] = dot(p_low, dout_h, 0, 0).astype(out.dtype)
-        dq_ref[:, cols] = (dq * SCALING).astype(BF)
+        dscore = (probs * (dot(dout_h, v, 1, 1) - delta)).astype(BF)
+        dq_ref[:, cols] = (dot(dscore, k, 1, 0) * SCALING).astype(BF)
+        dk = dot(dscore, q, 0, 0) * SCALING
+        dv = dot(probs_low, dout_h, 0, 0)
+        for ref, (a, b) in zip(part_refs, SEGMENTS):
+            ref[:, cols] = dk[a:b].astype(ref.dtype)
+            ref[:, vcols] = dv[a:b].astype(ref.dtype)
 
     @pl.when(core_ref[0] == 0)
     def _():
@@ -95,9 +80,9 @@
         out_shape=outs,
         in_specs=[pl.BlockSpec(memory_space=pltpu.SMEM)] + [vmem] * 10,
         out_specs=[vmem] * 8,
-        scratch_shapes=[pltpu.VMEM((rows, half), BF)],
+        scratch_shapes=[pltpu.VMEM((rows, half), BF), pltpu.VMEM((SEGMENTS[-1][1], 2 * half), BF)],
         compiler_params=pltpu.CompilerParams(vmem_limit_bytes=40 * 1024 * 1024),
-        cost_estimate=pl.CostEstimate(flops=1_400_000_000, bytes_accessed=4_000_000, transcendentals=524288),
+        cost_estimate=pl.CostEstimate(flops=700_000_000, bytes_accessed=4_000_000, transcendentals=524288),
         name="attention",
     )(core, q, *windows, fog, low, odp_half, bias)
 
@@ -245,18 +230,21 @@
 
     core_id = core.astype(jnp.int32).reshape(1)
 
+    stack = jnp.concatenate([queries[0], frozen_output_gradient[0], key_rows[0], values[0]], axis=0)
+
     shard = jnp.concatenate([down_qkv[0], down_qkv[1], up_out.T, down_qkv[2]], axis=1)
-    line = spread(shard.reshape(2, -1), ("y", "c"), 2 * NY).reshape(2 * NY * own_cols, 4 * rank)
+    copies = jnp.broadcast_to(shard.reshape(1, 2, -1), (2 * NY, 2, 2 * own_cols * rank))
+    copies, stack = lax.optimization_barrier((copies, stack))
+    line = exchange(copies, ("y", "c")).reshape(2 * NY * own_cols, 4 * rank)
     line = lax.dynamic_slice_in_dim(line, core * 2 * rank, 2 * rank, 1)
 
     lists = jnp.pad(block_lists[0].astype(BF), ((0, 12), (0, half - block_lists.shape[2])))
-    stack = jnp.concatenate([queries[0], frozen_output_gradient[0], key_rows[0], values[0]], axis=0)
     kept = jnp.concatenate([jnp.where(first, stack[:, :half], stack[:, half:]), lists], axis=0)
     got = swap(jnp.concatenate([jnp.where(first, stack[:, half:], stack[:, :half]), lists], axis=0))
     chip_stack = jnp.stack([jnp.where(first, kept, got), jnp.where(first, got, kept)])
     x_other = swap(x_own)
     y_other = lax.ppermute(y_own, "c", [(0, 1)])
-    line, chip_stack, x_other, y_other = lax.optimization_barrier((line, chip_stack, x_other, y_other))
+    line, chip_stack = lax.optimization_barrier((line, chip_stack))
 
     q_chip = chip_stack[:, :rows].reshape(2 * rows, half)
     fog_chip = chip_stack[:, rows : 2 * rows].reshape(2 * rows, half)
@@ -266,19 +254,16 @@
     lists_chip = chip_stack[:, 4 * rows : 4 * rows + BLK_DEV, : block_lists.shape[2]].reshape(
         2 * BLK_DEV, -1
     )
-    windows = (
-        chip_shift(kv_chip[rows:], 2),
-        chip_shift(kv_chip, 1),
-        kv_chip,
-        chip_shift(kv_chip, -1),
-        chip_shift(kv_chip[:rows], -2),
-    )
+    l1, r1 = chip_shift(kv_chip, 1), chip_shift(kv_chip, -1)
     ids = (2 * chip - 3) * BLK_DEV + jnp.arange(8 * BLK_DEV, dtype=jnp.int32)
     allowed = jnp.any(lists_chip[:, :, None] == ids.astype(F32)[None, None, :], axis=1) & (ids >= 0)[None]
     bias = jnp.repeat(jnp.where(allowed, 0.0, MASKED).astype(F32), BLK, axis=1)
 
     plane = spread(line, "z", NZ)
-    weights = spread(plane.reshape(-1, 2 * rank), "x", NX).reshape(NX, NZ, -1, 2 * rank)
+    copies = jnp.broadcast_to(plane.reshape(1, -1, 2 * rank), (NX, NZ * plane.shape[1], 2 * rank))
+    copies, l1, r1, kv_late = lax.optimization_barrier((copies, l1, r1, kv_chip))
+    windows = (chip_shift(kv_late[rows:], 2), l1, kv_chip, r1, chip_shift(kv_late[:rows], -2))
+    weights = exchange(copies, "x").reshape(NX, NZ, -1, 2 * rank)
     low = low_factors(core_id, x_own, x_other, y_own, y_other, weights)
     low_both = lax.all_gather(low, "c")
     odp_half = lax.dynamic_slice_in_dim(output_down_projection, core * half, half, 0)

time: 209 us -> 200 us (0.957)
  waiting for transfers between devices: 65.6 us -> 60.7 us
  other arithmetic: 13.3 us -> 9.96 us
  blocking collectives: 27.2 us -> 30.5 us
  local copies, waits for them, and re-layouts: 19.9 us -> 17.1 us
    all_to_all x6, waiting for transfers between devices: 59.7 us -> 47.7 us  [exchange(): return lax.all_to_all(parts, axes, split_axis=0, concat_axis=0, tiled=True)]
    ppermute x8, waiting for transfers between devices: 5.79 us -> 12 us  [chip_shift(): lax.ppermute(block, ('x', 'y'), [(i, i + by) for i in range(chips) if 0 <...]
    all_to_all x1, blocking collectives: 22 us -> 26.7 us  [exchange(): return lax.all_to_all(parts, axes, split_axis=0, concat_axis=0, tiled=True)]
    pallas_call x1, Pallas kernels: 6.37 us -> 3.54 us  [attention(): pl.pallas_call(attention_kernel, out_shape=outs, in_specs=[pl.BlockSpec(m...]
    all_to_all x6, starting transfers between devices: 32.1 us -> 34.8 us  [exchange(): return lax.all_to_all(parts, axes, split_axis=0, concat_axis=0, tiled=True)]
    ppermute x8, starting transfers between devices: 17.9 us -> 15.4 us  [chip_shift(): lax.ppermute(block, ('x', 'y'), [(i, i + by) for i in range(chips) if 0 <...]
    unnamed x56 -> x42, local copies, waits for them, and re-layouts: 10.1 us -> 7.98 us
  transfers between devices with their start and end apart: 19 -> 19, of which waited for: 9 -> 10; matrix products, arithmetic and copies ran while one was open for 9% -> 7% of each run, Pallas kernels for 1% -> 2%
where the time goes in v4:
time: 200 us; the launch traced here: 199 us
  starting transfers between devices  67 us (34%)
  waiting for transfers between devices  60.7 us (30%)
  blocking collectives  30.5 us (15%)
  local copies, waits for them, and re-layouts  17.1 us (9%)
  Pallas kernels  12.6 us (6%)
  other arithmetic  9.96 us (5%)
    all_to_all x6, waiting for transfers between devices, exchange(): return lax.all_to_all(parts, axes, split_axis=0, concat_axis=0, tiled=True)  47.7 us
    all_to_all x6, starting transfers between devices, exchange(): return lax.all_to_all(parts, axes, split_axis=0, concat_axis=0, tiled=True)  34.8 us
    all_to_all x1, blocking collectives, exchange(): return lax.all_to_all(parts, axes, split_axis=0, concat_axis=0, tiled=True)  26.7 us
    ppermute x4, starting transfers between devices, swap(): return lax.ppermute(block, 'c', [(0, 1), (1, 0)])  15.6 us
    ppermute x8, starting transfers between devices, chip_shift(): lax.ppermute(block, ('x', 'y'), [(i, i + by) for i in range(chips) if 0 <...  15.4 us
    ppermute x8, waiting for transfers between devices, chip_shift(): lax.ppermute(block, ('x', 'y'), [(i, i + by) for i in range(chips) if 0 <...  12 us
    unnamed x42, local copies, waits for them, and re-layouts  7.98 us
    pallas_call x1, Pallas kernels, grad_partials(): pl.pallas_call(lambda *refs: grad_kernel(scale, *refs), grid=(NZ // Z_STE...  4.84 us
  transfers between devices with their start and end apart: 19, of which 10 were waited for; matrix products, arithmetic and copies ran while one was open for 7% of the time, Pallas kernels for 2%

profile of v4, /device:TPU:1, one launch (start us, length us, event | category | flops | bytes accessed | tf_op | source)
XLA Modules:
  0.0 199.1 jit_solution(1668710438016815804)
XLA Ops:
  0.6 0.8 fusion.9
  1.5 0.8 pad_maximum_fusion.7
  2.3 1.2 pad_maximum_fusion.1
  3.5 0.7 broadcast_in_dim.56
  4.2 0.7 convert_bitcast_fusion.1
  5.0 8.8 %collective-permute-start = (bf16[528,256]{1,0:T(8,128)(2,1)S(1)}, bf16[528,256]{1,0:T(8,128)(2,1)S(1)}, u32[]{:S(2)}, u32[]{:S(2)}) collective-permute-start(bf16[528,256]{1,0:T(8,128)(2,1)S(1)} %fusion.2), channel_id=1, source_target_pairs={{0,1},{1,0},{2,3},{3,2},{4,5},{5,4},{6,7},{7,6},{8,9},{9,8},{10,11... | collective-permute-start | bytes 811016 | tf_op jit(solution)/shard_map/ppermute | solution.py:208
  13.8 3.4 %all-to-all-start = ((bf16[16,2,1280]{2,1,0:T(2,128)(2,1)}), bf16[16,2,1280]{2,1,0:T(2,128)(2,1)S(1)}, u32[]{:S(2)}, u32[]{:S(2)}) async-start(bf16[16,2,1280]{2,1,0:T(2,128)(2,1)} %broadcast_in_dim.56), calls=%async_computation | async-start | bytes 163840 | tf_op jit(solution)/shard_map/all_to_all | solution.py:200
  17.2 2.0 %collective-permute-start.5 = (bf16[128,5120]{1,0:T(8,128)(2,1)S(1)}, bf16[128,5120]{1,0:T(8,128)(2,1)}, u32[]{:S(2)}, u32[]{:S(2)}) collective-permute-start(bf16[128,5120]{1,0:T(8,128)(2,1)S(1)} %bitcast.69), channel_id=1, source_target_pairs={{0,1},{1,0},{2,3},{3,2},{4,5},{5,4},{6,7},{7,6},{8,9},{9,8},{10,11... | collective-permute-start | bytes 3932168 | tf_op jit(solution)/shard_map/ppermute | solution.py:208
  19.2 1.3 collective-permute-start.6
  20.5 4.7 %all-to-all-done = bf16[16,2,1280]{2,1,0:T(2,128)(2,1)S(1)} async-done(((bf16[16,2,1280]{2,1,0:T(2,128)(2,1)}), bf16[16,2,1280]{2,1,0:T(2,128)(2,1)S(1)}, u32[]{:S(2)}, u32[]{:S(2)}) %all-to-all-start) | async-done | bytes 81952 | tf_op jit(solution)/shard_map/all_to_all | solution.py:200
  25.5 0.9 broadcast_in_dim.57
  26.4 8.6 %all-to-all-start.1 = ((bf16[8,160,128]{2,1,0:T(8,128)(2,1)}), bf16[8,160,128]{2,1,0:T(8,128)(2,1)S(1)}, u32[]{:S(2)}, u32[]{:S(2)}) async-start(bf16[8,160,128]{2,1,0:T(8,128)(2,1)} %broadcast_in_dim.57), calls=%async_computation.1 | async-start | bytes 655360 | tf_op jit(solution)/shard_map/all_to_all | solution.py:200
  35.0 2.1 %collective-permute-start.1 = (bf16[256,512]{1,0:T(8,128)(2,1)S(1)}, bf16[256,512]{1,0:T(8,128)(2,1)S(1)}, u32[]{:S(2)}, u32[]{:S(2)}) collective-permute-start(bf16[256,512]{1,0:T(8,128)(2,1)S(1)} %bitcast.72), channel_id=1, source_target_pairs={{0,2},{2,4},{4,6},{6,8},{8,10},{10,12},{12,14},{14,16},{16,18},{18... | collective-permute-start | bytes 786440 | tf_op jit(solution)/shard_map/ppermute | solution.py:213
  37.1 1.3 collective-permute-start.2
  38.4 4.1 %collective-permute-done.1.l1_ref = bf16[256,512]{1,0:T(8,128)(2,1)S(1)} collective-permute-done((bf16[256,512]{1,0:T(8,128)(2,1)S(1)}, bf16[256,512]{1,0:T(8,128)(2,1)S(1)}, u32[]{:S(2)}, u32[]{:S(2)}) %collective-permute-start.1) | collective-permute-done | bytes 262176 | tf_op jit(solution)/shard_map/ppermute | solution.py:213
  42.5 0.7 copy-done.1
  43.2 3.1 %collective-permute-done.2.r1_ref = bf16[256,512]{1,0:T(8,128)(2,1)S(1)} collective-permute-done((bf16[256,512]{1,0:T(8,128)(2,1)S(1)}, bf16[256,512]{1,0:T(8,128)(2,1)S(1)}, u32[]{:S(2)}, u32[]{:S(2)}) %collective-permute-start.2) | collective-permute-done | bytes 262176 | tf_op jit(solution)/shard_map/ppermute | solution.py:213
  46.4 0.7 copy-done.3
  47.1 1.6 all-to-all-done.1
  48.7 1.2 broadcast_in_dim.59
  49.9 4.1 %all-to-all-start.2 = ((bf16[4,1280,128]{2,1,0:T(8,128)(2,1)}), bf16[4,1280,128]{2,1,0:T(8,128)(2,1)S(1)}, u32[]{:S(2)}, u32[]{:S(2)}) async-start(bf16[4,1280,128]{2,1,0:T(8,128)(2,1)} %broadcast_in_dim.59), calls=%async_computation.2 | async-start | bytes 2621440 | tf_op jit(solution)/shard_map/all_to_all | solution.py:200
  54.3 0.7 slice.142
  55.1 0.7 fusion.6
  55.9 2.1 %collective-permute-start.3 = (bf16[128,512]{1,0:T(8,128)(2,1)}, bf16[128,512]{1,0:T(8,128)(2,1)S(1)}, u32[]{:S(2)}, u32[]{:S(2)}) collective-permute-start(bf16[128,512]{1,0:T(8,128)(2,1)} %get-tuple-element.102), channel_id=1, source_target_pairs={{0,4},{2,6},{4,8},{6,10},{8,12},{10,14},{12,16},{14,18},{16,20},{1... | collective-permute-start | bytes 393224 | tf_op jit(solution)/shard_map/ppermute | solution.py:213
  58.0 1.3 collective-permute-start.4
  59.3 0.8 broadcast_in_dim.62
  60.1 1.0 reshape.88.bias_ref
  61.1 12.5 %all-to-all-done.2 = bf16[4,1280,128]{2,1,0:T(8,128)(2,1)S(1)} async-done(((bf16[4,1280,128]{2,1,0:T(8,128)(2,1)}), bf16[4,1280,128]{2,1,0:T(8,128)(2,1)S(1)}, u32[]{:S(2)}, u32[]{:S(2)}) %all-to-all-start.2) | async-done | bytes 1310752 | tf_op jit(solution)/shard_map/all_to_all | solution.py:200
  73.6 4.2 %low_factors.1.refs_9_ = bf16[256,128]{1,0:T(8,128)(2,1)S(1)} custom-call(s32[1]{0:T(128)} %bitcast.core_ref.refs_0_, bf16[128,5120]{1,0:T(8,128)(2,1)S(1)} %bitcast.70, bf16[128,5120]{1,0:T(8,128)(2,1)} %collective-permute-done.5.xt_ref.refs_2_, bf16[128,5120]{1,0:T(8,128)(2,1)} %bitcast.17.yo_ref.refs_3_, ...), custom_call_target="tpu_custom_call" | custom-call | flops 700000000 | bytes 6600000 | tf_op jit(solution)/shard_map/low_factors/pallas_call | solution.py:123
  77.9 3.8 %all-gather = bf16[512,128]{1,0:T(8,128)(2,1)S(1)} all-gather(bf16[256,128]{1,0:T(8,128)(2,1)S(1)} %low_factors.1.refs_9_), channel_id=2, replica_groups=mesh['z'=8,'x'=4,'y'=8,'c'=2] {'c'}, dimensions={0}, use_global_device_ids=true | all-gather | bytes 196608 | tf_op jit(solution)/shard_map/all_gather | solution.py:268
  81.7 0.7 copy-done.7
  82.3 0.9 copy-done.8
  83.2 3.5 %attention.1 = (bf16[256,256]{1,0:T(8,128)(2,1)S(1)}, bf16[384,256]{1,0:T(8,128)(2,1)S(1)}, bf16[256,256]{1,0:T(8,128)(2,1)S(1)}, bf16[128,512]{1,0:T(8,128)(2,1...) custom-call(s32[1]{0:T(128)} %bitcast.core_ref.refs_0_, ...), custom_call_target="tpu_custom_call" | custom-call | flops 700000000 | bytes 4000000 | tf_op jit(solution)/shard_map/attention/pallas_call | solution.py:78
  86.8 0.6 copy-done.5
  87.4 0.7 copy-done.6
  88.1 1.3 collective-permute-start.8
  89.4 4.7 %collective-permute-start.9 = (bf16[256,512]{1,0:T(8,128)(2,1)S(1)}, bf16[256,512]{1,0:T(8,128)(2,1)}, u32[]{:S(2)}, u32[]{:S(2)}) collective-permute-start(bf16[256,512]{1,0:T(8,128)(2,1)S(1)} %get-tuple-element.35), channel_id=1, source_target_pairs={{0,2},{2,4},{4,6},{6,8},{8,10},{10,12},{12,14},{14,16},{16,18},{18... | collective-permute-start | bytes 786440 | tf_op jit(solution)/shard_map/ppermute | solution.py:213
  94.1 0.8 copy.88
  94.9 0.8 copy.89
  95.7 1.3 collective-permute-start.10
  97.0 1.3 collective-permute-start.11
  98.3 0.9 bitcast_select_fusion.refs_10_
  99.3 1.9 collective-permute-start.7
  101.2 4.7 %collective-permute-done.11 = bf16[128,512]{1,0:T(8,128)(2,1)S(1)} collective-permute-done((bf16[128,512]{1,0:T(8,128)(2,1)}, bf16[128,512]{1,0:T(8,128)(2,1)S(1)}, u32[]{:S(2)}, u32[]{:S(2)}) %collective-permute-start.11) | collective-permute-done | bytes 131104 | tf_op jit(solution)/shard_map/ppermute | solution.py:213
  105.9 0.7 copy-done.13
  106.6 1.2 add_convert_fusion
  107.9 2.8 %collective-permute-start.12 = (bf16[384,256]{1,0:T(8,128)(2,1)S(1)}, bf16[384,256]{1,0:T(8,128)(2,1)S(1)}, u32[]{:S(2)}, u32[]{:S(2)}) collective-permute-start(bf16[384,256]{1,0:T(8,128)(2,1)S(1)} %pad_maximum_fusion.4), channel_id=1, source_target_pairs={{0,1},{1,0},{2,3},{3,2},{4,5},{5,4},{6,7},{7,6},{8,9},{9,8},{10,11... | collective-permute-start | bytes 589832 | tf_op jit(solution)/shard_map/ppermute | solution.py:208
  110.8 1.0 collective-permute-done.12.refs_8_
  111.8 4.8 %grad_partials.1 = bf16[4,8,176,128]{3,2,1,0:T(8,128)(2,1)S(1)} custom-call(s32[1]{0:T(128)} %bitcast.core_ref.refs_0_, bf16[128,5120]{1,0:T(8,128)(2,1)S(1)} %bitcast.71, bf16[128,5120]{1,0:T(8,128)(2,1)} %collective-permute-done.5.xt_ref.refs_2_, bf16[128,5120]{1,0:T(8,128)(2,1)} %bitcast.17.yo_ref.refs_3_, ...), custom_call_target="tpu_custom_call" | custom-call | flops 800000000 | bytes 7500000 | tf_op jit(solution)/shard_map/grad_partials/pallas_call | solution.py:186
  116.6 26.7 %all_to_all.35 = bf16[4,1408,128]{2,1,0:T(8,128)(2,1)S(1)} all-to-all(bf16[4,1408,128]{2,1,0:T(8,128)(2,1)S(1)} %bitcast.67), channel_id=1, replica_groups=mesh['z'=8,'x'=4,'y'=8,'c'=2] {'x'}, dimensions={0} | all-to-all | bytes 2883584 | tf_op jit(solution)/shard_map/all_to_all | solution.py:200
  143.4 1.0 reduce_sum.33
  144.4 6.3 %all-to-all-start.4 = ((bf16[8,176,128]{2,1,0:T(8,128)(2,1)}), bf16[8,176,128]{2,1,0:T(8,128)(2,1)S(1)}, u32[]{:S(2)}, u32[]{:S(2)}) async-start(bf16[8,176,128]{2,1,0:T(8,128)(2,1)} %bitcast.29), calls=%async_computation.4 | async-start | bytes 720896 | tf_op jit(solution)/shard_map/all_to_all | solution.py:200
  150.7 0.7 maximum_bitcast_fusion
  151.4 10.9 %all-to-all-done.4 = bf16[8,176,128]{2,1,0:T(8,128)(2,1)S(1)} async-done(((bf16[8,176,128]{2,1,0:T(8,128)(2,1)}), bf16[8,176,128]{2,1,0:T(8,128)(2,1)S(1)}, u32[]{:S(2)}, u32[]{:S(2)}) %all-to-all-start.4) | async-done | bytes 360480 | tf_op jit(solution)/shard_map/all_to_all | solution.py:200
  162.4 0.7 pad_maximum_fusion.5
  163.1 8.5 %all-to-all-start.5 = ((bf16[16,26,128]{2,1,0:T(8,128)(2,1)}), bf16[16,26,128]{2,1,0:T(8,128)(2,1)S(1)}, u32[]{:S(2)}, u32[]{:S(2)}) async-start(bf16[16,26,128]{2,1,0:T(8,128)(2,1)} %pad_maximum_fusion.5), calls=%async_computation.5 | async-start | bytes 262144 | tf_op jit(solution)/shard_map/all_to_all | solution.py:200
  171.6 9.1 %all-to-all-done.5 = bf16[16,26,128]{2,1,0:T(8,128)(2,1)S(1)} async-done(((bf16[16,26,128]{2,1,0:T(8,128)(2,1)}), bf16[16,26,128]{2,1,0:T(8,128)(2,1)S(1)}, u32[]{:S(2)}, u32[]{:S(2)}) %all-to-all-start.5) | async-done | bytes 106528 | tf_op jit(solution)/shard_map/all_to_all | solution.py:200
  180.9 0.7 broadcast_in_dim.68
  181.7 3.9 %all-to-all-start.6 = ((bf16[32,32,128]{2,1,0:T(8,128)(2,1)}), bf16[32,32,128]{2,1,0:T(8,128)(2,1)S(1)}, u32[]{:S(2)}, u32[]{:S(2)}) async-start(bf16[32,32,128]{2,1,0:T(8,128)(2,1)} %broadcast_in_dim.68), calls=%async_computation.6 | async-start | bytes 524288 | tf_op jit(solution)/shard_map/all_to_all | solution.py:200
  185.6 0.7 maximum_bitcast_fusion.2
  186.2 0.7 maximum_bitcast_fusion.1
  188.2 8.8 %all-to-all-done.6 = bf16[32,32,128]{2,1,0:T(8,128)(2,1)S(1)} async-done(((bf16[32,32,128]{2,1,0:T(8,128)(2,1)}), bf16[32,32,128]{2,1,0:T(8,128)(2,1)S(1)}, u32[]{:S(2)}, u32[]{:S(2)}) %all-to-all-start.6) | async-done | bytes 262176 | tf_op jit(solution)/shard_map/all_to_all | solution.py:200
  197.6 0.7 slice_bitcast_fusion
  198.3 0.8 pad_maximum_fusion.2
  (79 shorter events, 3.2 us)
Async XLA Ops:
  2.3 14.9 %copy-start = (bf16[1,128,5120]{2,1,0:T(8,128)(2,1)S(1)}, bf16[1,128,5120]{2,1,0:T(8,128)(2,1)}, u32[]{:S(2)}) copy-start(bf16[1,128,5120]{2,1,0:T(8,128)(2,1)} %param.11) | copy-start | bytes 3932164
  5.0 20.4 %collective-permute-start = (bf16[528,256]{1,0:T(8,128)(2,1)S(1)}, bf16[528,256]{1,0:T(8,128)(2,1)S(1)}, u32[]{:S(2)}, u32[]{:S(2)}) collective-permute-start(bf16[528,256]{1,0:T(8,128)(2,1)S(1)} %fusion.2), channel_id=1, source_target_pairs={{0,1},{1,0},{2,3},{3,2},{4,5},{5,4},{6,7},{7,6},{8,9},{9,8},{10,11... | collective-permute-start | bytes 811016 | tf_op jit(solution)/shard_map/ppermute | solution.py:208
  13.8 11.5 %all-to-all-start = ((bf16[16,2,1280]{2,1,0:T(2,128)(2,1)}), bf16[16,2,1280]{2,1,0:T(2,128)(2,1)S(1)}, u32[]{:S(2)}, u32[]{:S(2)}) async-start(bf16[16,2,1280]{2,1,0:T(2,128)(2,1)} %broadcast_in_dim.56), calls=%async_computation | async-start | bytes 163840 | tf_op jit(solution)/shard_map/all_to_all | solution.py:200
  17.2 43.9 %collective-permute-start.5 = (bf16[128,5120]{1,0:T(8,128)(2,1)S(1)}, bf16[128,5120]{1,0:T(8,128)(2,1)}, u32[]{:S(2)}, u32[]{:S(2)}) collective-permute-start(bf16[128,5120]{1,0:T(8,128)(2,1)S(1)} %bitcast.69), channel_id=1, source_target_pairs={{0,1},{1,0},{2,3},{3,2},{4,5},{5,4},{6,7},{7,6},{8,9},{9,8},{10,11... | collective-permute-start | bytes 3932168 | tf_op jit(solution)/shard_map/ppermute | solution.py:208
  19.2 41.8 %collective-permute-start.6 = (bf16[128,5120]{1,0:T(8,128)(2,1)}, bf16[128,5120]{1,0:T(8,128)(2,1)}, u32[]{:S(2)}, u32[]{:S(2)}) collective-permute-start(bf16[128,5120]{1,0:T(8,128)(2,1)} %bitcast.17.yo_ref.refs_3_), channel_id=1, source_target_pairs={{0,1},{2,3},{4,5},{6,7},{8,9},{10,11},{12,13},{14,15},{16,17},{18,... | collective-permute-start | bytes 3932168 | tf_op jit(solution)/shard_map/ppermute | solution.py:246
  25.5 24.4 %copy-start.9 = (bf16[2,528,256]{2,1,0:T(8,128)(2,1)}, bf16[2,528,256]{2,1,0:T(8,128)(2,1)S(1)}, u32[]{:S(2)}) copy-start(bf16[2,528,256]{2,1,0:T(8,128)(2,1)S(1)} %pad_maximum_fusion) | copy-start | bytes 1622020
  26.4 22.3 %all-to-all-start.1 = ((bf16[8,160,128]{2,1,0:T(8,128)(2,1)}), bf16[8,160,128]{2,1,0:T(8,128)(2,1)S(1)}, u32[]{:S(2)}, u32[]{:S(2)}) async-start(bf16[8,160,128]{2,1,0:T(8,128)(2,1)} %broadcast_in_dim.57), calls=%async_computation.1 | async-start | bytes 655360 | tf_op jit(solution)/shard_map/all_to_all | solution.py:200
  35.0 7.5 %collective-permute-start.1 = (bf16[256,512]{1,0:T(8,128)(2,1)S(1)}, bf16[256,512]{1,0:T(8,128)(2,1)S(1)}, u32[]{:S(2)}, u32[]{:S(2)}) collective-permute-start(bf16[256,512]{1,0:T(8,128)(2,1)S(1)} %bitcast.72), channel_id=1, source_target_pairs={{0,2},{2,4},{4,6},{6,8},{8,10},{10,12},{12,14},{14,16},{16,18},{18... | collective-permute-start | bytes 786440 | tf_op jit(solution)/shard_map/ppermute | solution.py:213
  37.1 9.2 %collective-permute-start.2 = (bf16[256,512]{1,0:T(8,128)(2,1)S(1)}, bf16[256,512]{1,0:T(8,128)(2,1)S(1)}, u32[]{:S(2)}, u32[]{:S(2)}) collective-permute-start(bf16[256,512]{1,0:T(8,128)(2,1)S(1)} %bitcast.73), channel_id=1, source_target_pairs={{2,0},{4,2},{6,4},{8,6},{10,8},{12,10},{14,12},{16,14},{18,16},{20... | collective-permute-start | bytes 786440 | tf_op jit(solution)/shard_map/ppermute | solution.py:213
  42.5 0.7 copy-start.1
  46.4 0.7 copy-start.3
  49.9 4.2 %copy-start.15 = (bf16[512,64]{0,1:T(8,128)(2,1)S(1)}, bf16[512,64]{0,1:T(8,128)(2,1)}, u32[]{:S(2)}) copy-start(bf16[512,64]{0,1:T(8,128)(2,1)} %param.20) | copy-start | bytes 196612
  49.9 23.7 %all-to-all-start.2 = ((bf16[4,1280,128]{2,1,0:T(8,128)(2,1)}), bf16[4,1280,128]{2,1,0:T(8,128)(2,1)S(1)}, u32[]{:S(2)}, u32[]{:S(2)}) async-start(bf16[4,1280,128]{2,1,0:T(8,128)(2,1)} %broadcast_in_dim.59), calls=%async_computation.2 | async-start | bytes 2621440 | tf_op jit(solution)/shard_map/all_to_all | solution.py:200
  54.2 1.6 copy-start.10
  55.9 25.8 %collective-permute-start.3 = (bf16[128,512]{1,0:T(8,128)(2,1)}, bf16[128,512]{1,0:T(8,128)(2,1)S(1)}, u32[]{:S(2)}, u32[]{:S(2)}) collective-permute-start(bf16[128,512]{1,0:T(8,128)(2,1)} %get-tuple-element.102), channel_id=1, source_target_pairs={{0,4},{2,6},{4,8},{6,10},{8,12},{10,14},{12,16},{14,18},{16,20},{1... | collective-permute-start | bytes 393224 | tf_op jit(solution)/shard_map/ppermute | solution.py:213
  58.0 24.3 %collective-permute-start.4 = (bf16[128,512]{1,0:T(8,128)(2,1)}, bf16[128,512]{1,0:T(8,128)(2,1)}, u32[]{:S(2)}, u32[]{:S(2)}) collective-permute-start(bf16[128,512]{1,0:T(8,128)(2,1)} %get-tuple-element.101), channel_id=1, source_target_pairs={{4,0},{6,2},{8,4},{10,6},{12,8},{14,10},{16,12},{18,14},{20,16},{2... | collective-permute-start | bytes 393224 | tf_op jit(solution)/shard_map/ppermute | solution.py:213
  73.6 8.7 %copy-start.2 = (bf16[256,512]{1,0:T(8,128)(2,1)S(1)}, bf16[256,512]{1,0:T(8,128)(2,1)}, u32[]{:S(2)}) copy-start(bf16[256,512]{1,0:T(8,128)(2,1)} %copy-done.1) | copy-start | bytes 786436
  73.6 8.7 %copy-start.4 = (bf16[256,512]{1,0:T(8,128)(2,1)S(1)}, bf16[256,512]{1,0:T(8,128)(2,1)}, u32[]{:S(2)}) copy-start(bf16[256,512]{1,0:T(8,128)(2,1)} %copy-done.3) | copy-start | bytes 786436
  77.8 16.2 %copy-start.14 = (bf16[3,64,512]{2,1,0:T(8,128)(2,1)S(1)}, bf16[3,64,512]{2,1,0:T(8,128)(2,1)}, u32[]{:S(2)}) copy-start(bf16[3,64,512]{2,1,0:T(8,128)(2,1)} %param.19) | copy-start | bytes 589828
  81.7 0.7 copy-start.7
  82.3 0.9 copy-start.8
  86.8 0.7 copy-start.5
  87.4 0.7 copy-start.6
  88.1 17.8 %collective-permute-start.8 = (bf16[256,512]{1,0:T(8,128)(2,1)S(1)}, bf16[256,512]{1,0:T(8,128)(2,1)S(1)}, u32[]{:S(2)}, u32[]{:S(2)}) collective-permute-start(bf16[256,512]{1,0:T(8,128)(2,1)S(1)} %get-tuple-element.34), channel_id=1, source_target_pairs={{2,0},{4,2},{6,4},{8,6},{10,8},{12,10},{14,12},{16,14},{18,16},{20... | collective-permute-start | bytes 786440 | tf_op jit(solution)/shard_map/ppermute | solution.py:213
  89.4 16.5 %collective-permute-start.9 = (bf16[256,512]{1,0:T(8,128)(2,1)S(1)}, bf16[256,512]{1,0:T(8,128)(2,1)}, u32[]{:S(2)}, u32[]{:S(2)}) collective-permute-start(bf16[256,512]{1,0:T(8,128)(2,1)S(1)} %get-tuple-element.35), channel_id=1, source_target_pairs={{0,2},{2,4},{4,6},{6,8},{8,10},{10,12},{12,14},{14,16},{16,18},{18... | collective-permute-start | bytes 786440 | tf_op jit(solution)/shard_map/ppermute | solution.py:213
  95.7 5.5 %collective-permute-start.10 = (bf16[128,512]{1,0:T(8,128)(2,1)}, bf16[128,512]{1,0:T(8,128)(2,1)S(1)}, u32[]{:S(2)}, u32[]{:S(2)}) collective-permute-start(bf16[128,512]{1,0:T(8,128)(2,1)} %copy-done.6), channel_id=1, source_target_pairs={{0,4},{2,6},{4,8},{6,10},{8,12},{10,14},{12,16},{14,18},{16,20},{1... | collective-permute-start | bytes 393224 | tf_op jit(solution)/shard_map/ppermute | solution.py:213
  97.0 8.9 %collective-permute-start.11 = (bf16[128,512]{1,0:T(8,128)(2,1)}, bf16[128,512]{1,0:T(8,128)(2,1)S(1)}, u32[]{:S(2)}, u32[]{:S(2)}) collective-permute-start(bf16[128,512]{1,0:T(8,128)(2,1)} %copy-done.5), channel_id=1, source_target_pairs={{4,0},{6,2},{8,4},{10,6},{12,8},{14,10},{16,12},{18,14},{20,16},{2... | collective-permute-start | bytes 393224 | tf_op jit(solution)/shard_map/ppermute | solution.py:213
  99.3 11.5 %collective-permute-start.7 = (bf16[384,256]{1,0:T(8,128)(2,1)S(1)}, bf16[384,256]{1,0:T(8,128)(2,1)S(1)}, u32[]{:S(2)}, u32[]{:S(2)}) collective-permute-start(bf16[384,256]{1,0:T(8,128)(2,1)S(1)} %get-tuple-element.32), channel_id=1, source_target_pairs={{0,1},{1,0},{2,3},{3,2},{4,5},{5,4},{6,7},{7,6},{8,9},{9,8},{10,11... | collective-permute-start | bytes 589832 | tf_op jit(solution)/shard_map/ppermute | solution.py:208
  105.9 0.7 copy-start.13
  106.6 4.1 %copy-start.11 = (bf16[1,64,512]{1,2,0:T(8,128)(2,1)S(1)}, bf16[1,64,512]{1,2,0:T(8,128)(2,1)}, u32[]{:S(2)}) copy-start(bf16[1,64,512]{1,2,0:T(8,128)(2,1)} %copy.88) | copy-start | bytes 196612
  106.6 4.1 %copy-start.12 = (bf16[1,64,512]{1,2,0:T(8,128)(2,1)S(1)}, bf16[1,64,512]{1,2,0:T(8,128)(2,1)}, u32[]{:S(2)}) copy-start(bf16[1,64,512]{1,2,0:T(8,128)(2,1)} %copy.89) | copy-start | bytes 196612
  107.9 3.9 %collective-permute-start.12 = (bf16[384,256]{1,0:T(8,128)(2,1)S(1)}, bf16[384,256]{1,0:T(8,128)(2,1)S(1)}, u32[]{:S(2)}, u32[]{:S(2)}) collective-permute-start(bf16[384,256]{1,0:T(8,128)(2,1)S(1)} %pad_maximum_fusion.4), channel_id=1, source_target_pairs={{0,1},{1,0},{2,3},{3,2},{4,5},{5,4},{6,7},{7,6},{8,9},{9,8},{10,11... | collective-permute-start | bytes 589832 | tf_op jit(solution)/shard_map/ppermute | solution.py:208
  144.4 17.9 %all-to-all-start.4 = ((bf16[8,176,128]{2,1,0:T(8,128)(2,1)}), bf16[8,176,128]{2,1,0:T(8,128)(2,1)S(1)}, u32[]{:S(2)}, u32[]{:S(2)}) async-start(bf16[8,176,128]{2,1,0:T(8,128)(2,1)} %bitcast.29), calls=%async_computation.4 | async-start | bytes 720896 | tf_op jit(solution)/shard_map/all_to_all | solution.py:200
  163.1 17.7 %all-to-all-start.5 = ((bf16[16,26,128]{2,1,0:T(8,128)(2,1)}), bf16[16,26,128]{2,1,0:T(8,128)(2,1)S(1)}, u32[]{:S(2)}, u32[]{:S(2)}) async-start(bf16[16,26,128]{2,1,0:T(8,128)(2,1)} %pad_maximum_fusion.5), calls=%async_computation.5 | async-start | bytes 262144 | tf_op jit(solution)/shard_map/all_to_all | solution.py:200
  181.7 15.3 %all-to-all-start.6 = ((bf16[32,32,128]{2,1,0:T(8,128)(2,1)}), bf16[32,32,128]{2,1,0:T(8,128)(2,1)S(1)}, u32[]{:S(2)}, u32[]{:S(2)}) async-start(bf16[32,32,128]{2,1,0:T(8,128)(2,1)} %broadcast_in_dim.68), calls=%async_computation.6 | async-start | bytes 524288 | tf_op jit(solution)/shard_map/all_to_all | solution.py:200

commit v5 on v4

--- a/solution.py
+++ b/solution.py
@@ -230,11 +230,11 @@
 
     core_id = core.astype(jnp.int32).reshape(1)
 
-    stack = jnp.concatenate([queries[0], frozen_output_gradient[0], key_rows[0], values[0]], axis=0)
-
     shard = jnp.concatenate([down_qkv[0], down_qkv[1], up_out.T, down_qkv[2]], axis=1)
     copies = jnp.broadcast_to(shard.reshape(1, 2, -1), (2 * NY, 2, 2 * own_cols * rank))
-    copies, stack = lax.optimization_barrier((copies, stack))
+    saved = (queries[0], frozen_output_gradient[0], key_rows[0], values[0])
+    copies, saved = lax.optimization_barrier((copies, saved))
+    stack = jnp.concatenate(saved, axis=0)
     line = exchange(copies, ("y", "c")).reshape(2 * NY * own_cols, 4 * rank)
     line = lax.dynamic_slice_in_dim(line, core * 2 * rank, 2 * rank, 1)
 
@@ -261,10 +261,13 @@
 
     plane = spread(line, "z", NZ)
     copies = jnp.broadcast_to(plane.reshape(1, -1, 2 * rank), (NX, NZ * plane.shape[1], 2 * rank))
-    copies, l1, r1, kv_late = lax.optimization_barrier((copies, l1, r1, kv_chip))
+    copies, kv_late = lax.optimization_barrier((copies, kv_chip))
     windows = (chip_shift(kv_late[rows:], 2), l1, kv_chip, r1, chip_shift(kv_late[:rows], -2))
     weights = exchange(copies, "x").reshape(NX, NZ, -1, 2 * rank)
     low = low_factors(core_id, x_own, x_other, y_own, y_other, weights)
+    m_a = jnp.where(first, up_qkv[0].T, output_down_projection)
+    m_b = jnp.where(first, up_qkv[1].T, up_qkv[2].T)
+    low, m_a, m_b = lax.optimization_barrier((low, m_a, m_b))
     low_both = lax.all_gather(low, "c")
     odp_half = lax.dynamic_slice_in_dim(output_down_projection, core * half, half, 0)
 
@@ -276,8 +279,6 @@
     from_r2 = chip_shift(p_l2, -2)
     from_l2 = chip_shift(p_r2, 2)
     got_a = swap(send_a)
-    m_a = jnp.where(first, up_qkv[0].T, output_down_projection)
-    m_b = jnp.where(first, up_qkv[1].T, up_qkv[2].T)
 
     total = p_own + from_r1.astype(F32) + from_l1.astype(F32)
     total = total + jnp.concatenate([from_l2, from_r2], axis=0).astype(F32)

time: 200 us -> 192 us (0.960)
  waiting for transfers between devices: 60.7 us -> 40.2 us
  starting transfers between devices: 67 us -> 77.5 us
  blocking collectives: 30.5 us -> 34.1 us
    all_to_all x6, waiting for transfers between devices: 47.7 us -> 36.3 us  [exchange(): return lax.all_to_all(parts, axes, split_axis=0, concat_axis=0, tiled=True)]
    ppermute x8, waiting for transfers between devices: 12 us -> 2.87 us  [chip_shift(): lax.ppermute(block, ('x', 'y'), [(i, i + by) for i in range(chips) if 0 <...]
    ppermute x8, starting transfers between devices: 15.4 us -> 24.4 us  [chip_shift(): lax.ppermute(block, ('x', 'y'), [(i, i + by) for i in range(chips) if 0 <...]
    all_to_all x6, starting transfers between devices: 34.8 us -> 40 us  [exchange(): return lax.all_to_all(parts, axes, split_axis=0, concat_axis=0, tiled=True)]
    ppermute x4, starting transfers between devices: 15.6 us -> 11.8 us  [swap(): return lax.ppermute(block, 'c', [(0, 1), (1, 0)])]
    all_gather x1, blocking collectives: 3.8 us -> 7.23 us  [shards(): low_both = lax.all_gather(low, 'c')]
    unnamed x42 -> x21, local copies, waits for them, and re-layouts: 7.98 us -> 6.51 us
  transfers between devices with their start and end apart: 19 -> 19, of which waited for: 10 -> 6; matrix products, arithmetic and copies ran while one was open for 7% -> 9% of each run, Pallas kernels for 2% -> 2%
where the time goes in v5:
time: 192 us; the launch traced here: 191 us
  starting transfers between devices  77.5 us (40%)
  waiting for transfers between devices  40.2 us (21%)
  blocking collectives  34.1 us (18%)
  local copies, waits for them, and re-layouts  16.6 us (9%)
  Pallas kernels  12.7 us (7%)
  other arithmetic  8.56 us (4%)
    all_to_all x6, starting transfers between devices, exchange(): return lax.all_to_all(parts, axes, split_axis=0, concat_axis=0, tiled=True)  40 us
    all_to_all x6, waiting for transfers between devices, exchange(): return lax.all_to_all(parts, axes, split_axis=0, concat_axis=0, tiled=True)  36.3 us
    all_to_all x1, blocking collectives, exchange(): return lax.all_to_all(parts, axes, split_axis=0, concat_axis=0, tiled=True)  26.9 us
    ppermute x8, starting transfers between devices, chip_shift(): lax.ppermute(block, ('x', 'y'), [(i, i + by) for i in range(chips) if 0 <...  24.4 us
    ppermute x4, starting transfers between devices, swap(): return lax.ppermute(block, 'c', [(0, 1), (1, 0)])  11.8 us
    all_gather x1, blocking collectives, shards(): low_both = lax.all_gather(low, 'c')  7.23 us
    unnamed x21, local copies, waits for them, and re-layouts  6.51 us
    pallas_call x1, Pallas kernels, grad_partials(): pl.pallas_call(lambda *refs: grad_kernel(scale, *refs), grid=(NZ // Z_STE...  4.85 us
  transfers between devices with their start and end apart: 19, of which 6 were waited for; matrix products, arithmetic and copies ran while one was open for 9% of the time, Pallas kernels for 2%

profile of v5, /device:TPU:1, one launch (start us, length us, event | category | flops | bytes accessed | tf_op | source)
XLA Modules:
  0.0 190.8 jit_solution(9792449450419052854)
XLA Ops:
  0.6 0.8 fusion.9
  1.5 0.8 pad_maximum_fusion.6
  2.3 0.7 broadcast_in_dim.56
  3.0 10.2 %all-to-all-start = ((bf16[16,2,1280]{2,1,0:T(2,128)(2,1)}), bf16[16,2,1280]{2,1,0:T(2,128)(2,1)S(1)}, u32[]{:S(2)}, u32[]{:S(2)}) async-start(bf16[16,2,1280]{2,1,0:T(2,128)(2,1)} %broadcast_in_dim.56), calls=%async_computation | async-start | bytes 163840 | tf_op jit(solution)/shard_map/all_to_all | solution.py:200
  13.1 0.7 convert_bitcast_fusion.1
  13.8 1.0 constant_dynamic-update-slice_fusion.3
  14.9 0.9 constant_dynamic-update-slice_fusion.2
  15.8 0.9 constant_dynamic-update-slice_fusion.1
  16.7 0.9 constant_dynamic-update-slice_fusion
  17.7 2.1 %collective-permute-start = (bf16[528,256]{1,0:T(8,128)(2,1)S(1)}, bf16[528,256]{1,0:T(8,128)(2,1)S(1)}, u32[]{:S(2)}, u32[]{:S(2)}) collective-permute-start(bf16[528,256]{1,0:T(8,128)(2,1)S(1)} %fusion.2), channel_id=1, source_target_pairs={{0,1},{1,0},{2,3},{3,2},{4,5},{5,4},{6,7},{7,6},{8,9},{9,8},{10,11... | collective-permute-start | bytes 811016 | tf_op jit(solution)/shard_map/ppermute | solution.py:208
  19.8 2.2 %collective-permute-start.5 = (bf16[128,5120]{1,0:T(8,128)(2,1)S(1)}, bf16[128,5120]{1,0:T(8,128)(2,1)}, u32[]{:S(2)}, u32[]{:S(2)}) collective-permute-start(bf16[128,5120]{1,0:T(8,128)(2,1)S(1)} %bitcast.69), channel_id=1, source_target_pairs={{0,1},{1,0},{2,3},{3,2},{4,5},{5,4},{6,7},{7,6},{8,9},{9,8},{10,11... | collective-permute-start | bytes 3932168 | tf_op jit(solution)/shard_map/ppermute | solution.py:208
  22.0 1.3 collective-permute-start.6
  23.5 0.1 select_bitcast_fusion.1
  23.7 0.8 broadcast_in_dim.57
  24.5 8.5 %all-to-all-start.1 = ((bf16[8,160,128]{2,1,0:T(8,128)(2,1)}), bf16[8,160,128]{2,1,0:T(8,128)(2,1)S(1)}, u32[]{:S(2)}, u32[]{:S(2)}) async-start(bf16[8,160,128]{2,1,0:T(8,128)(2,1)} %broadcast_in_dim.57), calls=%async_computation.1 | async-start | bytes 655360 | tf_op jit(solution)/shard_map/all_to_all | solution.py:200
  33.0 0.1 copy.74
  33.2 0.8 copy.89
  33.9 0.8 copy.88
  34.7 0.8 copy.87
  35.5 7.5 %all-to-all-done.1 = bf16[8,160,128]{2,1,0:T(8,128)(2,1)S(1)} async-done(((bf16[8,160,128]{2,1,0:T(8,128)(2,1)}), bf16[8,160,128]{2,1,0:T(8,128)(2,1)S(1)}, u32[]{:S(2)}, u32[]{:S(2)}) %all-to-all-start.1) | async-done | bytes 327712 | tf_op jit(solution)/shard_map/all_to_all | solution.py:200
  43.0 1.3 broadcast_in_dim.59
  44.2 4.0 %all-to-all-start.2 = ((bf16[4,1280,128]{2,1,0:T(8,128)(2,1)}), bf16[4,1280,128]{2,1,0:T(8,128)(2,1)S(1)}, u32[]{:S(2)}, u32[]{:S(2)}) async-start(bf16[4,1280,128]{2,1,0:T(8,128)(2,1)} %broadcast_in_dim.59), calls=%async_computation.2 | async-start | bytes 2621440 | tf_op jit(solution)/shard_map/all_to_all | solution.py:200
  48.3 0.9 bitcast_select_fusion.refs_10_
  49.2 0.9 select_bitcast_fusion.2.refs_11_
  50.1 0.7 slice.145
  50.8 1.3 collective-permute-start.3
  52.1 4.7 %collective-permute-start.2 = (bf16[256,512]{1,0:T(8,128)(2,1)S(1)}, bf16[256,512]{1,0:T(8,128)(2,1)}, u32[]{:S(2)}, u32[]{:S(2)}) collective-permute-start(bf16[256,512]{1,0:T(8,128)(2,1)S(1)} %bitcast.73), channel_id=1, source_target_pairs={{0,2},{2,4},{4,6},{6,8},{8,10},{10,12},{12,14},{14,16},{16,18},{18... | collective-permute-start | bytes 786440 | tf_op jit(solution)/shard_map/ppermute | solution.py:213
  57.0 0.7 fusion.6
  57.7 1.3 collective-permute-start.4
  59.0 5.6 %collective-permute-start.1 = (bf16[128,512]{1,0:T(8,128)(2,1)}, bf16[128,512]{1,0:T(8,128)(2,1)}, u32[]{:S(2)}, u32[]{:S(2)}) collective-permute-start(bf16[128,512]{1,0:T(8,128)(2,1)} %get-tuple-element.110), channel_id=1, source_target_pairs={{0,4},{2,6},{4,8},{6,10},{8,12},{10,14},{12,16},{14,18},{16,20},{1... | collective-permute-start | bytes 393224 | tf_op jit(solution)/shard_map/ppermute | solution.py:213
  64.6 0.8 broadcast_in_dim.62
  65.3 1.0 reshape.88.bias_ref
  66.3 4.1 %low_factors.1.refs_9_ = bf16[256,128]{1,0:T(8,128)(2,1)S(1)} custom-call(s32[1]{0:T(128)} %bitcast.core_ref.refs_0_, bf16[128,5120]{1,0:T(8,128)(2,1)S(1)} %bitcast.70, bf16[128,5120]{1,0:T(8,128)(2,1)} %collective-permute-done.5.xt_ref.refs_2_, bf16[128,5120]{1,0:T(8,128)(2,1)} %bitcast.17.yo_ref.refs_3_, ...), custom_call_target="tpu_custom_call" | custom-call | flops 700000000 | bytes 6600000 | tf_op jit(solution)/shard_map/low_factors/pallas_call | solution.py:123
  70.4 7.2 %all-gather = bf16[512,128]{1,0:T(8,128)(2,1)S(1)} all-gather(bf16[256,128]{1,0:T(8,128)(2,1)S(1)} %low_factors.1.refs_9_), channel_id=2, replica_groups=mesh['z'=8,'x'=4,'y'=8,'c'=2] {'c'}, dimensions={0}, use_global_device_ids=true | all-gather | bytes 196608 | tf_op jit(solution)/shard_map/all_gather | solution.py:271
  77.7 3.7 %attention.1 = (bf16[256,256]{1,0:T(8,128)(2,1)S(1)}, bf16[384,256]{1,0:T(8,128)(2,1)S(1)}, bf16[256,256]{1,0:T(8,128)(2,1)S(1)}, bf16[128,512]{1,0:T(8,128)(2,1...) custom-call(s32[1]{0:T(128)} %bitcast.core_ref.refs_0_, ...), custom_call_target="tpu_custom_call" | custom-call | flops 700000000 | bytes 4000000 | tf_op jit(solution)/shard_map/attention/pallas_call | solution.py:78
  81.5 1.3 collective-permute-start.8
  82.8 4.0 %collective-permute-start.9 = (bf16[256,512]{1,0:T(8,128)(2,1)S(1)}, bf16[256,512]{1,0:T(8,128)(2,1)S(1)}, u32[]{:S(2)}, u32[]{:S(2)}) collective-permute-start(bf16[256,512]{1,0:T(8,128)(2,1)S(1)} %get-tuple-element.41), channel_id=1, source_target_pairs={{0,2},{2,4},{4,6},{6,8},{8,10},{10,12},{12,14},{14,16},{16,18},{18... | collective-permute-start | bytes 786440 | tf_op jit(solution)/shard_map/ppermute | solution.py:213
  86.8 5.0 %collective-permute-start.10 = (bf16[128,512]{1,0:T(8,128)(2,1)S(1)}, bf16[128,512]{1,0:T(8,128)(2,1)S(1)}, u32[]{:S(2)}, u32[]{:S(2)}) collective-permute-start(bf16[128,512]{1,0:T(8,128)(2,1)S(1)} %get-tuple-element.42), channel_id=1, source_target_pairs={{0,4},{2,6},{4,8},{6,10},{8,12},{10,14},{12,16},{14,18},{16,20},{1... | collective-permute-start | bytes 393224 | tf_op jit(solution)/shard_map/ppermute | solution.py:213
  91.7 1.3 collective-permute-start.11
  93.0 2.8 %collective-permute-start.7 = (bf16[384,256]{1,0:T(8,128)(2,1)S(1)}, bf16[384,256]{1,0:T(8,128)(2,1)S(1)}, u32[]{:S(2)}, u32[]{:S(2)}) collective-permute-start(bf16[384,256]{1,0:T(8,128)(2,1)S(1)} %get-tuple-element.38), channel_id=1, source_target_pairs={{0,1},{1,0},{2,3},{3,2},{4,5},{5,4},{6,7},{7,6},{8,9},{9,8},{10,11... | collective-permute-start | bytes 589832 | tf_op jit(solution)/shard_map/ppermute | solution.py:208
  95.9 2.8 %collective-permute-done.11 = bf16[128,512]{1,0:T(8,128)(2,1)S(1)} collective-permute-done((bf16[128,512]{1,0:T(8,128)(2,1)S(1)}, bf16[128,512]{1,0:T(8,128)(2,1)S(1)}, u32[]{:S(2)}, u32[]{:S(2)}) %collective-permute-start.11) | collective-permute-done | bytes 131104 | tf_op jit(solution)/shard_map/ppermute | solution.py:213
  98.7 0.1 add_convert_fusion
  98.9 4.7 %collective-permute-start.12 = (bf16[384,256]{1,0:T(8,128)(2,1)S(1)}, bf16[384,256]{1,0:T(8,128)(2,1)S(1)}, u32[]{:S(2)}, u32[]{:S(2)}) collective-permute-start(bf16[384,256]{1,0:T(8,128)(2,1)S(1)} %pad_maximum_fusion.3), channel_id=1, source_target_pairs={{0,1},{1,0},{2,3},{3,2},{4,5},{5,4},{6,7},{7,6},{8,9},{9,8},{10,11... | collective-permute-start | bytes 589832 | tf_op jit(solution)/shard_map/ppermute | solution.py:208
  103.7 1.0 collective-permute-done.12.refs_8_
  104.7 4.8 %grad_partials.1 = bf16[4,8,176,128]{3,2,1,0:T(8,128)(2,1)S(1)} custom-call(s32[1]{0:T(128)} %bitcast.core_ref.refs_0_, bf16[128,5120]{1,0:T(8,128)(2,1)S(1)} %bitcast.71, bf16[128,5120]{1,0:T(8,128)(2,1)} %collective-permute-done.5.xt_ref.refs_2_, bf16[128,5120]{1,0:T(8,128)(2,1)} %bitcast.17.yo_ref.refs_3_, ...), custom_call_target="tpu_custom_call" | custom-call | flops 800000000 | bytes 7500000 | tf_op jit(solution)/shard_map/grad_partials/pallas_call | solution.py:186
  109.6 26.9 %all_to_all.35 = bf16[4,1408,128]{2,1,0:T(8,128)(2,1)S(1)} all-to-all(bf16[4,1408,128]{2,1,0:T(8,128)(2,1)S(1)} %bitcast.67), channel_id=1, replica_groups=mesh['z'=8,'x'=4,'y'=8,'c'=2] {'x'}, dimensions={0} | all-to-all | bytes 2883584 | tf_op jit(solution)/shard_map/all_to_all | solution.py:200
  136.4 1.0 reduce_sum.33
  137.4 3.4 %all-to-all-start.4 = ((bf16[8,176,128]{2,1,0:T(8,128)(2,1)}), bf16[8,176,128]{2,1,0:T(8,128)(2,1)S(1)}, u32[]{:S(2)}, u32[]{:S(2)}) async-start(bf16[8,176,128]{2,1,0:T(8,128)(2,1)} %bitcast.29), calls=%async_computation.4 | async-start | bytes 720896 | tf_op jit(solution)/shard_map/all_to_all | solution.py:200
  140.9 0.7 maximum_bitcast_fusion
  141.6 10.9 %all-to-all-done.4 = bf16[8,176,128]{2,1,0:T(8,128)(2,1)S(1)} async-done(((bf16[8,176,128]{2,1,0:T(8,128)(2,1)}), bf16[8,176,128]{2,1,0:T(8,128)(2,1)S(1)}, u32[]{:S(2)}, u32[]{:S(2)}) %all-to-all-start.4) | async-done | bytes 360480 | tf_op jit(solution)/shard_map/all_to_all | solution.py:200
  152.6 0.7 pad_maximum_fusion.4
  153.3 10.0 %all-to-all-start.5 = ((bf16[16,26,128]{2,1,0:T(8,128)(2,1)}), bf16[16,26,128]{2,1,0:T(8,128)(2,1)S(1)}, u32[]{:S(2)}, u32[]{:S(2)}) async-start(bf16[16,26,128]{2,1,0:T(8,128)(2,1)} %pad_maximum_fusion.4), calls=%async_computation.5 | async-start | bytes 262144 | tf_op jit(solution)/shard_map/all_to_all | solution.py:200
  163.3 9.1 %all-to-all-done.5 = bf16[16,26,128]{2,1,0:T(8,128)(2,1)S(1)} async-done(((bf16[16,26,128]{2,1,0:T(8,128)(2,1)}), bf16[16,26,128]{2,1,0:T(8,128)(2,1)S(1)}, u32[]{:S(2)}, u32[]{:S(2)}) %all-to-all-start.5) | async-done | bytes 106528 | tf_op jit(solution)/shard_map/all_to_all | solution.py:200
  172.6 0.7 broadcast_in_dim.68
  173.4 3.9 %all-to-all-start.6 = ((bf16[32,32,128]{2,1,0:T(8,128)(2,1)}), bf16[32,32,128]{2,1,0:T(8,128)(2,1)S(1)}, u32[]{:S(2)}, u32[]{:S(2)}) async-start(bf16[32,32,128]{2,1,0:T(8,128)(2,1)} %broadcast_in_dim.68), calls=%async_computation.6 | async-start | bytes 524288 | tf_op jit(solution)/shard_map/all_to_all | solution.py:200
  177.3 0.7 maximum_bitcast_fusion.2
  177.9 0.7 maximum_bitcast_fusion.1
  178.7 0.6 copy.100
  179.3 0.6 copy.82
  179.9 8.8 %all-to-all-done.6 = bf16[32,32,128]{2,1,0:T(8,128)(2,1)S(1)} async-done(((bf16[32,32,128]{2,1,0:T(8,128)(2,1)}), bf16[32,32,128]{2,1,0:T(8,128)(2,1)S(1)}, u32[]{:S(2)}, u32[]{:S(2)}) %all-to-all-start.6) | async-done | bytes 262176 | tf_op jit(solution)/shard_map/all_to_all | solution.py:200
  188.8 0.3 copy.81
  189.1 0.2 reshape.94
  189.3 0.7 slice_bitcast_fusion
  190.0 0.8 pad_maximum_fusion.1
  (58 shorter events, 1.0 us)
Async XLA Ops:
  3.0 20.4 %all-to-all-start = ((bf16[16,2,1280]{2,1,0:T(2,128)(2,1)}), bf16[16,2,1280]{2,1,0:T(2,128)(2,1)S(1)}, u32[]{:S(2)}, u32[]{:S(2)}) async-start(bf16[16,2,1280]{2,1,0:T(2,128)(2,1)} %broadcast_in_dim.56), calls=%async_computation | async-start | bytes 163840 | tf_op jit(solution)/shard_map/all_to_all | solution.py:200
  13.8 6.0 %copy-start = (bf16[1,128,5120]{2,1,0:T(8,128)(2,1)S(1)}, bf16[1,128,5120]{2,1,0:T(8,128)(2,1)}, u32[]{:S(2)}) copy-start(bf16[1,128,5120]{2,1,0:T(8,128)(2,1)} %param.11) | copy-start | bytes 3932164
  13.8 9.5 %copy-start.2 = (bf16[3,64,512]{2,1,0:T(8,128)(2,1)S(1)}, bf16[3,64,512]{2,1,0:T(8,128)(2,1)}, u32[]{:S(2)}) copy-start(bf16[3,64,512]{2,1,0:T(8,128)(2,1)} %param.19) | copy-start | bytes 589828
  17.7 5.8 %collective-permute-start = (bf16[528,256]{1,0:T(8,128)(2,1)S(1)}, bf16[528,256]{1,0:T(8,128)(2,1)S(1)}, u32[]{:S(2)}, u32[]{:S(2)}) collective-permute-start(bf16[528,256]{1,0:T(8,128)(2,1)S(1)} %fusion.2), channel_id=1, source_target_pairs={{0,1},{1,0},{2,3},{3,2},{4,5},{5,4},{6,7},{7,6},{8,9},{9,8},{10,11... | collective-permute-start | bytes 811016 | tf_op jit(solution)/shard_map/ppermute | solution.py:208
  19.8 39.1 %collective-permute-start.5 = (bf16[128,5120]{1,0:T(8,128)(2,1)S(1)}, bf16[128,5120]{1,0:T(8,128)(2,1)}, u32[]{:S(2)}, u32[]{:S(2)}) collective-permute-start(bf16[128,5120]{1,0:T(8,128)(2,1)S(1)} %bitcast.69), channel_id=1, source_target_pairs={{0,1},{1,0},{2,3},{3,2},{4,5},{5,4},{6,7},{7,6},{8,9},{9,8},{10,11... | collective-permute-start | bytes 3932168 | tf_op jit(solution)/shard_map/ppermute | solution.py:208
  22.0 44.3 %collective-permute-start.6 = (bf16[128,5120]{1,0:T(8,128)(2,1)}, bf16[128,5120]{1,0:T(8,128)(2,1)}, u32[]{:S(2)}, u32[]{:S(2)}) collective-permute-start(bf16[128,5120]{1,0:T(8,128)(2,1)} %bitcast.17.yo_ref.refs_3_), channel_id=1, source_target_pairs={{0,1},{2,3},{4,5},{6,7},{8,9},{10,11},{12,13},{14,15},{16,17},{18,... | collective-permute-start | bytes 3932168 | tf_op jit(solution)/shard_map/ppermute | solution.py:246
  23.6 9.4 %copy-start.3 = (bf16[512,64]{0,1:T(8,128)(2,1)S(1)}, bf16[512,64]{0,1:T(8,128)(2,1)}, u32[]{:S(2)}) copy-start(bf16[512,64]{0,1:T(8,128)(2,1)} %param.20) | copy-start | bytes 196612
  23.7 20.6 %copy-start.1 = (bf16[2,528,256]{2,1,0:T(8,128)(2,1)}, bf16[2,528,256]{2,1,0:T(8,128)(2,1)S(1)}, u32[]{:S(2)}) copy-start(bf16[2,528,256]{2,1,0:T(8,128)(2,1)S(1)} %pad_maximum_fusion) | copy-start | bytes 1622020
  24.5 18.4 %all-to-all-start.1 = ((bf16[8,160,128]{2,1,0:T(8,128)(2,1)}), bf16[8,160,128]{2,1,0:T(8,128)(2,1)S(1)}, u32[]{:S(2)}, u32[]{:S(2)}) async-start(bf16[8,160,128]{2,1,0:T(8,128)(2,1)} %broadcast_in_dim.57), calls=%async_computation.1 | async-start | bytes 655360 | tf_op jit(solution)/shard_map/all_to_all | solution.py:200
  44.2 22.1 %all-to-all-start.2 = ((bf16[4,1280,128]{2,1,0:T(8,128)(2,1)}), bf16[4,1280,128]{2,1,0:T(8,128)(2,1)S(1)}, u32[]{:S(2)}, u32[]{:S(2)}) async-start(bf16[4,1280,128]{2,1,0:T(8,128)(2,1)} %broadcast_in_dim.59), calls=%async_computation.2 | async-start | bytes 2621440 | tf_op jit(solution)/shard_map/all_to_all | solution.py:200
  50.8 26.9 %collective-permute-start.3 = (bf16[256,512]{1,0:T(8,128)(2,1)S(1)}, bf16[256,512]{1,0:T(8,128)(2,1)}, u32[]{:S(2)}, u32[]{:S(2)}) collective-permute-start(bf16[256,512]{1,0:T(8,128)(2,1)S(1)} %bitcast.72), channel_id=1, source_target_pairs={{2,0},{4,2},{6,4},{8,6},{10,8},{12,10},{14,12},{16,14},{18,16},{20... | collective-permute-start | bytes 786440 | tf_op jit(solution)/shard_map/ppermute | solution.py:213
  52.1 25.6 %collective-permute-start.2 = (bf16[256,512]{1,0:T(8,128)(2,1)S(1)}, bf16[256,512]{1,0:T(8,128)(2,1)}, u32[]{:S(2)}, u32[]{:S(2)}) collective-permute-start(bf16[256,512]{1,0:T(8,128)(2,1)S(1)} %bitcast.73), channel_id=1, source_target_pairs={{0,2},{2,4},{4,6},{6,8},{8,10},{10,12},{12,14},{14,16},{16,18},{18... | collective-permute-start | bytes 786440 | tf_op jit(solution)/shard_map/ppermute | solution.py:213
  57.7 20.0 %collective-permute-start.4 = (bf16[128,512]{1,0:T(8,128)(2,1)}, bf16[128,512]{1,0:T(8,128)(2,1)}, u32[]{:S(2)}, u32[]{:S(2)}) collective-permute-start(bf16[128,512]{1,0:T(8,128)(2,1)} %get-tuple-element.109), channel_id=1, source_target_pairs={{4,0},{6,2},{8,4},{10,6},{12,8},{14,10},{16,12},{18,14},{20,16},{2... | collective-permute-start | bytes 393224 | tf_op jit(solution)/shard_map/ppermute | solution.py:213
  59.0 18.7 %collective-permute-start.1 = (bf16[128,512]{1,0:T(8,128)(2,1)}, bf16[128,512]{1,0:T(8,128)(2,1)}, u32[]{:S(2)}, u32[]{:S(2)}) collective-permute-start(bf16[128,512]{1,0:T(8,128)(2,1)} %get-tuple-element.110), channel_id=1, source_target_pairs={{0,4},{2,6},{4,8},{6,10},{8,12},{10,14},{12,16},{14,18},{16,20},{1... | collective-permute-start | bytes 393224 | tf_op jit(solution)/shard_map/ppermute | solution.py:213
  81.5 17.3 %collective-permute-start.8 = (bf16[256,512]{1,0:T(8,128)(2,1)S(1)}, bf16[256,512]{1,0:T(8,128)(2,1)S(1)}, u32[]{:S(2)}, u32[]{:S(2)}) collective-permute-start(bf16[256,512]{1,0:T(8,128)(2,1)S(1)} %get-tuple-element.40), channel_id=1, source_target_pairs={{2,0},{4,2},{6,4},{8,6},{10,8},{12,10},{14,12},{16,14},{18,16},{20... | collective-permute-start | bytes 786440 | tf_op jit(solution)/shard_map/ppermute | solution.py:213
  82.8 16.0 %collective-permute-start.9 = (bf16[256,512]{1,0:T(8,128)(2,1)S(1)}, bf16[256,512]{1,0:T(8,128)(2,1)S(1)}, u32[]{:S(2)}, u32[]{:S(2)}) collective-permute-start(bf16[256,512]{1,0:T(8,128)(2,1)S(1)} %get-tuple-element.41), channel_id=1, source_target_pairs={{0,2},{2,4},{4,6},{6,8},{8,10},{10,12},{12,14},{14,16},{16,18},{18... | collective-permute-start | bytes 786440 | tf_op jit(solution)/shard_map/ppermute | solution.py:213
  86.8 9.1 %collective-permute-start.10 = (bf16[128,512]{1,0:T(8,128)(2,1)S(1)}, bf16[128,512]{1,0:T(8,128)(2,1)S(1)}, u32[]{:S(2)}, u32[]{:S(2)}) collective-permute-start(bf16[128,512]{1,0:T(8,128)(2,1)S(1)} %get-tuple-element.42), channel_id=1, source_target_pairs={{0,4},{2,6},{4,8},{6,10},{8,12},{10,14},{12,16},{14,18},{16,20},{1... | collective-permute-start | bytes 393224 | tf_op jit(solution)/shard_map/ppermute | solution.py:213
  91.7 7.0 %collective-permute-start.11 = (bf16[128,512]{1,0:T(8,128)(2,1)S(1)}, bf16[128,512]{1,0:T(8,128)(2,1)S(1)}, u32[]{:S(2)}, u32[]{:S(2)}) collective-permute-start(bf16[128,512]{1,0:T(8,128)(2,1)S(1)} %get-tuple-element.43), channel_id=1, source_target_pairs={{4,0},{6,2},{8,4},{10,6},{12,8},{14,10},{16,12},{18,14},{20,16},{2... | collective-permute-start | bytes 393224 | tf_op jit(solution)/shard_map/ppermute | solution.py:213
  93.0 10.6 %collective-permute-start.7 = (bf16[384,256]{1,0:T(8,128)(2,1)S(1)}, bf16[384,256]{1,0:T(8,128)(2,1)S(1)}, u32[]{:S(2)}, u32[]{:S(2)}) collective-permute-start(bf16[384,256]{1,0:T(8,128)(2,1)S(1)} %get-tuple-element.38), channel_id=1, source_target_pairs={{0,1},{1,0},{2,3},{3,2},{4,5},{5,4},{6,7},{7,6},{8,9},{9,8},{10,11... | collective-permute-start | bytes 589832 | tf_op jit(solution)/shard_map/ppermute | solution.py:208
  98.9 5.8 %collective-permute-start.12 = (bf16[384,256]{1,0:T(8,128)(2,1)S(1)}, bf16[384,256]{1,0:T(8,128)(2,1)S(1)}, u32[]{:S(2)}, u32[]{:S(2)}) collective-permute-start(bf16[384,256]{1,0:T(8,128)(2,1)S(1)} %pad_maximum_fusion.3), channel_id=1, source_target_pairs={{0,1},{1,0},{2,3},{3,2},{4,5},{5,4},{6,7},{7,6},{8,9},{9,8},{10,11... | collective-permute-start | bytes 589832 | tf_op jit(solution)/shard_map/ppermute | solution.py:208
  137.4 15.1 %all-to-all-start.4 = ((bf16[8,176,128]{2,1,0:T(8,128)(2,1)}), bf16[8,176,128]{2,1,0:T(8,128)(2,1)S(1)}, u32[]{:S(2)}, u32[]{:S(2)}) async-start(bf16[8,176,128]{2,1,0:T(8,128)(2,1)} %bitcast.29), calls=%async_computation.4 | async-start | bytes 720896 | tf_op jit(solution)/shard_map/all_to_all | solution.py:200
  153.3 19.2 %all-to-all-start.5 = ((bf16[16,26,128]{2,1,0:T(8,128)(2,1)}), bf16[16,26,128]{2,1,0:T(8,128)(2,1)S(1)}, u32[]{:S(2)}, u32[]{:S(2)}) async-start(bf16[16,26,128]{2,1,0:T(8,128)(2,1)} %pad_maximum_fusion.4), calls=%async_computation.5 | async-start | bytes 262144 | tf_op jit(solution)/shard_map/all_to_all | solution.py:200
  173.4 15.3 %all-to-all-start.6 = ((bf16[32,32,128]{2,1,0:T(8,128)(2,1)}), bf16[32,32,128]{2,1,0:T(8,128)(2,1)S(1)}, u32[]{:S(2)}, u32[]{:S(2)}) async-start(bf16[32,32,128]{2,1,0:T(8,128)(2,1)} %broadcast_in_dim.68), calls=%async_computation.6 | async-start | bytes 524288 | tf_op jit(solution)/shard_map/all_to_all | solution.py:200

commit v6 on v5

--- a/solution.py
+++ b/solution.py
@@ -87,7 +87,7 @@
     )(core, q, *windows, fog, low, odp_half, bias)
 
 
-Z_STEP = 2
+Z_STEP = 4
 
 
 def low_kernel(core_ref, xo_ref, xt_ref, yo_ref, yt_ref, w_ref, low_ref, own_acc, other_acc):
@@ -163,13 +163,13 @@
 
     f_own = f_ref[pl.ds(pl.multiple_of(core * rows, rows), rows)]
     f_other = f_ref[pl.ds(pl.multiple_of((1 - core) * rows, rows), rows)]
-    line = lax.broadcasted_iota(jnp.int32, (2 * rank, block), 0)
-    from_y = (line < rank) & (core == 1)
+    from_y = jnp.full((rank, block), core) == 1
     for zz in range(Z_STEP):
         cols = slice(zz * block, (zz + 1) * block)
         gx = dot(f_own, xo_ref[:, cols], 0, 0) + dot(f_other, xt_ref[:, cols], 0, 0)
-        gy = dot(f_own, yo_ref[:, cols], 0, 0) + dot(f_other, yt_ref[:, cols], 0, 0)
-        g = (jnp.where(from_y, gy, gx) * scale).T.astype(BF)
+        gy = dot(f_own[:, :rank], yo_ref[:, cols], 0, 0) + dot(f_other[:, :rank], yt_ref[:, cols], 0, 0)
+        g = jnp.concatenate([jnp.where(from_y, gy, gx[:rank]), gx[rank:]], axis=0)
+        g = (g * scale).T.astype(BF)
         at = pl.ds(pl.multiple_of((step * Z_STEP + zz) * extra, extra), extra)
         for i in range(NX):
             g_ref[i, zz, :piece] = g[i * piece : (i + 1) * piece]
@@ -233,8 +233,8 @@
     shard = jnp.concatenate([down_qkv[0], down_qkv[1], up_out.T, down_qkv[2]], axis=1)
     copies = jnp.broadcast_to(shard.reshape(1, 2, -1), (2 * NY, 2, 2 * own_cols * rank))
     saved = (queries[0], frozen_output_gradient[0], key_rows[0], values[0])
-    copies, saved = lax.optimization_barrier((copies, saved))
     stack = jnp.concatenate(saved, axis=0)
+    copies, stack = lax.optimization_barrier((copies, stack))
     line = exchange(copies, ("y", "c")).reshape(2 * NY * own_cols, 4 * rank)
     line = lax.dynamic_slice_in_dim(line, core * 2 * rank, 2 * rank, 1)
 
@@ -242,9 +242,9 @@
     kept = jnp.concatenate([jnp.where(first, stack[:, :half], stack[:, half:]), lists], axis=0)
     got = swap(jnp.concatenate([jnp.where(first, stack[:, half:], stack[:, :half]), lists], axis=0))
     chip_stack = jnp.stack([jnp.where(first, kept, got), jnp.where(first, got, kept)])
+    line, chip_stack, x_own, y_own = lax.optimization_barrier((line, chip_stack, x_own, y_own))
     x_other = swap(x_own)
     y_other = lax.ppermute(y_own, "c", [(0, 1)])
-    line, chip_stack = lax.optimization_barrier((line, chip_stack))
 
     q_chip = chip_stack[:, :rows].reshape(2 * rows, half)
     fog_chip = chip_stack[:, rows : 2 * rows].reshape(2 * rows, half)
@@ -261,13 +261,12 @@
 
     plane = spread(line, "z", NZ)
     copies = jnp.broadcast_to(plane.reshape(1, -1, 2 * rank), (NX, NZ * plane.shape[1], 2 * rank))
-    copies, kv_late = lax.optimization_barrier((copies, kv_chip))
+    m_a = jnp.where(first, up_qkv[0].T, output_down_projection)
+    m_b = jnp.where(first, up_qkv[1].T, up_qkv[2].T)
+    copies, kv_late, bias, m_a, m_b = lax.optimization_barrier((copies, kv_chip, bias, m_a, m_b))
     windows = (chip_shift(kv_late[rows:], 2), l1, kv_chip, r1, chip_shift(kv_late[:rows], -2))
     weights = exchange(copies, "x").reshape(NX, NZ, -1, 2 * rank)
     low = low_factors(core_id, x_own, x_other, y_own, y_other, weights)
-    m_a = jnp.where(first, up_qkv[0].T, output_down_projection)
-    m_b = jnp.where(first, up_qkv[1].T, up_qkv[2].T)
-    low, m_a, m_b = lax.optimization_barrier((low, m_a, m_b))
     low_both = lax.all_gather(low, "c")
     odp_half = lax.dynamic_slice_in_dim(output_down_projection, core * half, half, 0)
 

time: 192 us -> 187 us (0.974)
  waiting for transfers between devices: 40.2 us -> 62.9 us
  blocking collectives: 34.1 us -> 25.3 us
  starting transfers between devices: 77.5 us -> 69.2 us
  local copies, waits for them, and re-layouts: 16.6 us -> 9.42 us
  Pallas kernels: 12.7 us -> 10.7 us
    all_to_all x6, waiting for transfers between devices: 36.3 us -> 55.2 us  [exchange(): return lax.all_to_all(parts, axes, split_axis=0, concat_axis=0, tiled=True)]
    unnamed x21 -> x20, local copies, waits for them, and re-layouts: 6.51 us -> 1.74 us
    all_to_all x1, blocking collectives: 26.9 us -> 22.2 us  [exchange(): return lax.all_to_all(parts, axes, split_axis=0, concat_axis=0, tiled=True)]
    all_gather x1, blocking collectives: 7.23 us -> 3.18 us  [shards(): low_both = lax.all_gather(low, 'c')]
    ppermute x8, waiting for transfers between devices: 2.87 us -> 6.63 us  [chip_shift(): lax.ppermute(block, ('x', 'y'), [(i, i + by) for i in range(chips) if 0 <...]
    ppermute x8, starting transfers between devices: 24.4 us -> 20.7 us  [chip_shift(): lax.ppermute(block, ('x', 'y'), [(i, i + by) for i in range(chips) if 0 <...]
    all_to_all x6, starting transfers between devices: 40 us -> 37.7 us  [exchange(): return lax.all_to_all(parts, axes, split_axis=0, concat_axis=0, tiled=True)]
    ppermute x4, starting transfers between devices: 11.8 us -> 9.58 us  [swap(): return lax.ppermute(block, 'c', [(0, 1), (1, 0)])]
  transfers between devices with their start and end apart: 19 -> 19, of which waited for: 6 -> 9; matrix products, arithmetic and copies ran while one was open for 9% -> 4% of each run, Pallas kernels for 2% -> 2%
where the time goes in v6:
time: 187 us; the launch traced here: 186 us
  starting transfers between devices  69.2 us (37%)
  waiting for transfers between devices  62.9 us (34%)
  blocking collectives  25.3 us (14%)
  Pallas kernels  10.7 us (6%)
  local copies, waits for them, and re-layouts  9.42 us (5%)
  other arithmetic  7.26 us (4%)
    all_to_all x6, waiting for transfers between devices, exchange(): return lax.all_to_all(parts, axes, split_axis=0, concat_axis=0, tiled=True)  55.2 us
    all_to_all x6, starting transfers between devices, exchange(): return lax.all_to_all(parts, axes, split_axis=0, concat_axis=0, tiled=True)  37.7 us
    all_to_all x1, blocking collectives, exchange(): return lax.all_to_all(parts, axes, split_axis=0, concat_axis=0, tiled=True)  22.2 us
    ppermute x8, starting transfers between devices, chip_shift(): lax.ppermute(block, ('x', 'y'), [(i, i + by) for i in range(chips) if 0 <...  20.7 us
    ppermute x4, starting transfers between devices, swap(): return lax.ppermute(block, 'c', [(0, 1), (1, 0)])  9.58 us
    ppermute x8, waiting for transfers between devices, chip_shift(): lax.ppermute(block, ('x', 'y'), [(i, i + by) for i in range(chips) if 0 <...  6.63 us
    pallas_call x1, Pallas kernels, attention(): pl.pallas_call(attention_kernel, out_shape=outs, in_specs=[pl.BlockSpec(m...  3.75 us
  transfers between devices with their start and end apart: 19, of which 9 were waited for; matrix products, arithmetic and copies ran while one was open for 4% of the time, Pallas kernels for 2%

profile of v6, /device:TPU:1, one launch (start us, length us, event | category | flops | bytes accessed | tf_op | source)
XLA Modules:
  0.0 186.1 jit_solution(9090889487821056339)
XLA Ops:
  0.6 0.8 fusion.9
  1.5 0.8 pad_maximum_fusion.7
  2.3 1.2 pad_maximum_fusion.1
  3.5 0.7 broadcast_in_dim.56
  4.2 10.2 %all-to-all-start = ((bf16[16,2,1280]{2,1,0:T(2,128)(2,1)}), bf16[16,2,1280]{2,1,0:T(2,128)(2,1)S(1)}, u32[]{:S(2)}, u32[]{:S(2)}) async-start(bf16[16,2,1280]{2,1,0:T(2,128)(2,1)} %broadcast_in_dim.56), calls=%async_computation | async-start | bytes 163840 | tf_op jit(solution)/shard_map/all_to_all | solution.py:200
  14.4 2.1 %collective-permute-start = (bf16[528,256]{1,0:T(8,128)(2,1)S(1)}, bf16[528,256]{1,0:T(8,128)(2,1)S(1)}, u32[]{:S(2)}, u32[]{:S(2)}) collective-permute-start(bf16[528,256]{1,0:T(8,128)(2,1)S(1)} %fusion.2), channel_id=1, source_target_pairs={{0,1},{1,0},{2,3},{3,2},{4,5},{5,4},{6,7},{7,6},{8,9},{9,8},{10,11... | collective-permute-start | bytes 811016 | tf_op jit(solution)/shard_map/ppermute | solution.py:208
  16.6 0.1 copy.75
  16.8 0.1 copy.89
  16.9 0.1 copy.88
  17.0 0.1 copy.87
  17.2 5.3 %all-to-all-done = bf16[16,2,1280]{2,1,0:T(2,128)(2,1)S(1)} async-done(((bf16[16,2,1280]{2,1,0:T(2,128)(2,1)}), bf16[16,2,1280]{2,1,0:T(2,128)(2,1)S(1)}, u32[]{:S(2)}, u32[]{:S(2)}) %all-to-all-start) | async-done | bytes 81952 | tf_op jit(solution)/shard_map/all_to_all | solution.py:200
  22.6 0.1 select_bitcast_fusion.1
  22.8 0.1 copy.73
  22.9 0.8 broadcast_in_dim.57
  23.7 8.4 %all-to-all-start.1 = ((bf16[8,160,128]{2,1,0:T(8,128)(2,1)}), bf16[8,160,128]{2,1,0:T(8,128)(2,1)S(1)}, u32[]{:S(2)}, u32[]{:S(2)}) async-start(bf16[8,160,128]{2,1,0:T(8,128)(2,1)} %broadcast_in_dim.57), calls=%async_computation.1 | async-start | bytes 655360 | tf_op jit(solution)/shard_map/all_to_all | solution.py:200
  32.1 2.2 %collective-permute-start.5 = (bf16[128,5120]{1,0:T(8,128)(2,1)S(1)}, bf16[128,5120]{1,0:T(8,128)(2,1)}, u32[]{:S(2)}, u32[]{:S(2)}) collective-permute-start(bf16[128,5120]{1,0:T(8,128)(2,1)S(1)} %bitcast.69), channel_id=1, source_target_pairs={{0,1},{1,0},{2,3},{3,2},{4,5},{5,4},{6,7},{7,6},{8,9},{9,8},{10,11... | collective-permute-start | bytes 3932168 | tf_op jit(solution)/shard_map/ppermute | solution.py:208
  34.4 0.1 compare_reduce_fusion
  34.5 0.1 broadcast_in_dim.62
  34.6 0.1 reshape.86.bias_ref
  34.7 1.3 collective-permute-start.6
  36.1 9.8 %all-to-all-done.1 = bf16[8,160,128]{2,1,0:T(8,128)(2,1)S(1)} async-done(((bf16[8,160,128]{2,1,0:T(8,128)(2,1)}), bf16[8,160,128]{2,1,0:T(8,128)(2,1)S(1)}, u32[]{:S(2)}, u32[]{:S(2)}) %all-to-all-start.1) | async-done | bytes 327712 | tf_op jit(solution)/shard_map/all_to_all | solution.py:200
  45.9 1.2 broadcast_in_dim.59
  47.1 4.0 %all-to-all-start.2 = ((bf16[4,1280,128]{2,1,0:T(8,128)(2,1)}), bf16[4,1280,128]{2,1,0:T(8,128)(2,1)S(1)}, u32[]{:S(2)}, u32[]{:S(2)}) async-start(bf16[4,1280,128]{2,1,0:T(8,128)(2,1)} %broadcast_in_dim.59), calls=%async_computation.2 | async-start | bytes 2621440 | tf_op jit(solution)/shard_map/all_to_all | solution.py:200
  51.2 1.3 collective-permute-start.3
  52.4 4.7 %collective-permute-start.2 = (bf16[256,512]{1,0:T(8,128)(2,1)S(1)}, bf16[256,512]{1,0:T(8,128)(2,1)}, u32[]{:S(2)}, u32[]{:S(2)}) collective-permute-start(bf16[256,512]{1,0:T(8,128)(2,1)S(1)} %bitcast.73), channel_id=1, source_target_pairs={{0,2},{2,4},{4,6},{6,8},{8,10},{10,12},{12,14},{14,16},{16,18},{18... | collective-permute-start | bytes 786440 | tf_op jit(solution)/shard_map/ppermute | solution.py:213
  57.1 0.7 fusion.6
  57.9 1.3 collective-permute-start.4
  59.2 5.5 %collective-permute-start.1 = (bf16[128,512]{1,0:T(8,128)(2,1)}, bf16[128,512]{1,0:T(8,128)(2,1)}, u32[]{:S(2)}, u32[]{:S(2)}) collective-permute-start(bf16[128,512]{1,0:T(8,128)(2,1)} %get-tuple-element.108), channel_id=1, source_target_pairs={{0,4},{2,6},{4,8},{6,10},{8,12},{10,14},{12,16},{14,18},{16,20},{1... | collective-permute-start | bytes 393224 | tf_op jit(solution)/shard_map/ppermute | solution.py:213
  64.7 0.8 constant_dynamic-slice_fusion.odp_ref
  65.6 11.3 %all-to-all-done.2 = bf16[4,1280,128]{2,1,0:T(8,128)(2,1)S(1)} async-done(((bf16[4,1280,128]{2,1,0:T(8,128)(2,1)}), bf16[4,1280,128]{2,1,0:T(8,128)(2,1)S(1)}, u32[]{:S(2)}, u32[]{:S(2)}) %all-to-all-start.2) | async-done | bytes 1310752 | tf_op jit(solution)/shard_map/all_to_all | solution.py:200
  76.8 3.3 %low_factors.1.refs_9_ = bf16[256,128]{1,0:T(8,128)(2,1)S(1)} custom-call(s32[1]{0:T(128)} %bitcast.core_ref.refs_0_, bf16[128,5120]{1,0:T(8,128)(2,1)S(1)} %bitcast.70, bf16[128,5120]{1,0:T(8,128)(2,1)} %collective-permute-done.5.xt_ref.refs_2_, bf16[128,5120]{1,0:T(8,128)(2,1)} %bitcast.13.yo_ref.refs_3_, ...), custom_call_target="tpu_custom_call" | custom-call | flops 700000000 | bytes 6600000 | tf_op jit(solution)/shard_map/low_factors/pallas_call | solution.py:123
  80.1 3.2 %all-gather = bf16[512,128]{1,0:T(8,128)(2,1)S(1)} all-gather(bf16[256,128]{1,0:T(8,128)(2,1)S(1)} %low_factors.1.refs_9_), channel_id=2, replica_groups=mesh['z'=8,'x'=4,'y'=8,'c'=2] {'c'}, dimensions={0}, use_global_device_ids=true | all-gather | bytes 196608 | tf_op jit(solution)/shard_map/all_gather | solution.py:270
  83.3 3.7 %attention.1 = (bf16[256,256]{1,0:T(8,128)(2,1)S(1)}, bf16[384,256]{1,0:T(8,128)(2,1)S(1)}, bf16[256,256]{1,0:T(8,128)(2,1)S(1)}, bf16[128,512]{1,0:T(8,128)(2,1...) custom-call(s32[1]{0:T(128)} %bitcast.core_ref.refs_0_, ...), custom_call_target="tpu_custom_call" | custom-call | flops 700000000 | bytes 4000000 | tf_op jit(solution)/shard_map/attention/pallas_call | solution.py:78
  87.0 1.3 collective-permute-start.8
  88.3 4.0 %collective-permute-start.9 = (bf16[256,512]{1,0:T(8,128)(2,1)S(1)}, bf16[256,512]{1,0:T(8,128)(2,1)S(1)}, u32[]{:S(2)}, u32[]{:S(2)}) collective-permute-start(bf16[256,512]{1,0:T(8,128)(2,1)S(1)} %get-tuple-element.39), channel_id=1, source_target_pairs={{0,2},{2,4},{4,6},{6,8},{8,10},{10,12},{12,14},{14,16},{16,18},{18... | collective-permute-start | bytes 786440 | tf_op jit(solution)/shard_map/ppermute | solution.py:213
  92.3 1.3 collective-permute-start.10
  93.7 1.3 collective-permute-start.11
  95.0 2.8 %collective-permute-start.7 = (bf16[384,256]{1,0:T(8,128)(2,1)S(1)}, bf16[384,256]{1,0:T(8,128)(2,1)S(1)}, u32[]{:S(2)}, u32[]{:S(2)}) collective-permute-start(bf16[384,256]{1,0:T(8,128)(2,1)S(1)} %get-tuple-element.36), channel_id=1, source_target_pairs={{0,1},{1,0},{2,3},{3,2},{4,5},{5,4},{6,7},{7,6},{8,9},{9,8},{10,11... | collective-permute-start | bytes 589832 | tf_op jit(solution)/shard_map/ppermute | solution.py:208
  97.8 5.2 %collective-permute-done.10 = bf16[128,512]{1,0:T(8,128)(2,1)S(1)} collective-permute-done((bf16[128,512]{1,0:T(8,128)(2,1)S(1)}, bf16[128,512]{1,0:T(8,128)(2,1)S(1)}, u32[]{:S(2)}, u32[]{:S(2)}) %collective-permute-start.10) | collective-permute-done | bytes 131104 | tf_op jit(solution)/shard_map/ppermute | solution.py:213
  103.0 1.4 collective-permute-done.11
  104.4 0.1 add_convert_fusion
  104.6 2.4 %collective-permute-start.12 = (bf16[384,256]{1,0:T(8,128)(2,1)S(1)}, bf16[384,256]{1,0:T(8,128)(2,1)S(1)}, u32[]{:S(2)}, u32[]{:S(2)}) collective-permute-start(bf16[384,256]{1,0:T(8,128)(2,1)S(1)} %pad_maximum_fusion.4), channel_id=1, source_target_pairs={{0,1},{1,0},{2,3},{3,2},{4,5},{5,4},{6,7},{7,6},{8,9},{9,8},{10,11... | collective-permute-start | bytes 589832 | tf_op jit(solution)/shard_map/ppermute | solution.py:208
  107.0 1.0 collective-permute-done.12.refs_8_
  108.1 3.7 %grad_partials.1 = bf16[4,8,176,128]{3,2,1,0:T(8,128)(2,1)S(1)} custom-call(s32[1]{0:T(128)} %bitcast.core_ref.refs_0_, bf16[128,5120]{1,0:T(8,128)(2,1)S(1)} %bitcast.71, bf16[128,5120]{1,0:T(8,128)(2,1)} %collective-permute-done.5.xt_ref.refs_2_, bf16[128,5120]{1,0:T(8,128)(2,1)} %bitcast.13.yo_ref.refs_3_, ...), custom_call_target="tpu_custom_call" | custom-call | flops 800000000 | bytes 7500000 | tf_op jit(solution)/shard_map/grad_partials/pallas_call | solution.py:186
  111.8 22.2 %all_to_all.35 = bf16[4,1408,128]{2,1,0:T(8,128)(2,1)S(1)} all-to-all(bf16[4,1408,128]{2,1,0:T(8,128)(2,1)S(1)} %bitcast.67), channel_id=1, replica_groups=mesh['z'=8,'x'=4,'y'=8,'c'=2] {'x'}, dimensions={0} | all-to-all | bytes 2883584 | tf_op jit(solution)/shard_map/all_to_all | solution.py:200
  133.9 1.0 reduce_sum.33
  135.0 3.4 %all-to-all-start.4 = ((bf16[8,176,128]{2,1,0:T(8,128)(2,1)}), bf16[8,176,128]{2,1,0:T(8,128)(2,1)S(1)}, u32[]{:S(2)}, u32[]{:S(2)}) async-start(bf16[8,176,128]{2,1,0:T(8,128)(2,1)} %bitcast.29), calls=%async_computation.4 | async-start | bytes 720896 | tf_op jit(solution)/shard_map/all_to_all | solution.py:200
  138.4 0.7 maximum_bitcast_fusion
  139.1 10.9 %all-to-all-done.4 = bf16[8,176,128]{2,1,0:T(8,128)(2,1)S(1)} async-done(((bf16[8,176,128]{2,1,0:T(8,128)(2,1)}), bf16[8,176,128]{2,1,0:T(8,128)(2,1)S(1)}, u32[]{:S(2)}, u32[]{:S(2)}) %all-to-all-start.4) | async-done | bytes 360480 | tf_op jit(solution)/shard_map/all_to_all | solution.py:200
  150.1 0.7 pad_maximum_fusion.5
  150.8 7.7 %all-to-all-start.5 = ((bf16[16,26,128]{2,1,0:T(8,128)(2,1)}), bf16[16,26,128]{2,1,0:T(8,128)(2,1)S(1)}, u32[]{:S(2)}, u32[]{:S(2)}) async-start(bf16[16,26,128]{2,1,0:T(8,128)(2,1)} %pad_maximum_fusion.5), calls=%async_computation.5 | async-start | bytes 262144 | tf_op jit(solution)/shard_map/all_to_all | solution.py:200
  158.6 9.1 %all-to-all-done.5 = bf16[16,26,128]{2,1,0:T(8,128)(2,1)S(1)} async-done(((bf16[16,26,128]{2,1,0:T(8,128)(2,1)}), bf16[16,26,128]{2,1,0:T(8,128)(2,1)S(1)}, u32[]{:S(2)}, u32[]{:S(2)}) %all-to-all-start.5) | async-done | bytes 106528 | tf_op jit(solution)/shard_map/all_to_all | solution.py:200
  167.8 0.1 convert_reduce_fusion
  167.9 0.7 broadcast_in_dim.68
  168.6 3.9 %all-to-all-start.6 = ((bf16[32,32,128]{2,1,0:T(8,128)(2,1)}), bf16[32,32,128]{2,1,0:T(8,128)(2,1)S(1)}, u32[]{:S(2)}, u32[]{:S(2)}) async-start(bf16[32,32,128]{2,1,0:T(8,128)(2,1)} %broadcast_in_dim.68), calls=%async_computation.6 | async-start | bytes 524288 | tf_op jit(solution)/shard_map/all_to_all | solution.py:200
  172.5 0.7 maximum_bitcast_fusion.2
  173.2 0.7 maximum_bitcast_fusion.1
  173.9 0.6 copy.100
  174.6 0.6 copy.82
  175.2 8.8 %all-to-all-done.6 = bf16[32,32,128]{2,1,0:T(8,128)(2,1)S(1)} async-done(((bf16[32,32,128]{2,1,0:T(8,128)(2,1)}), bf16[32,32,128]{2,1,0:T(8,128)(2,1)S(1)}, u32[]{:S(2)}, u32[]{:S(2)}) %all-to-all-start.6) | async-done | bytes 262176 | tf_op jit(solution)/shard_map/all_to_all | solution.py:200
  184.0 0.3 copy.81
  184.4 0.2 reshape.94
  184.6 0.7 slice_bitcast_fusion
  185.3 0.8 pad_maximum_fusion.2
  (57 shorter events, 0.8 us)
Async XLA Ops:
  0.6 13.7 %copy-start.4 = (s32[1,4,12]{2,1,0:T(4,128)S(1)}, s32[1,4,12]{2,1,0:T(4,128)}, u32[]{:S(2)}) copy-start(s32[1,4,12]{2,1,0:T(4,128)} %param.17) | copy-start | bytes 580
  2.3 14.3 %copy-start.3 = (bf16[512,64]{0,1:T(8,128)(2,1)S(1)}, bf16[512,64]{0,1:T(8,128)(2,1)}, u32[]{:S(2)}) copy-start(bf16[512,64]{0,1:T(8,128)(2,1)} %param.20) | copy-start | bytes 196612
  2.3 14.4 %copy-start.2 = (bf16[3,64,512]{2,1,0:T(8,128)(2,1)S(1)}, bf16[3,64,512]{2,1,0:T(8,128)(2,1)}, u32[]{:S(2)}) copy-start(bf16[3,64,512]{2,1,0:T(8,128)(2,1)} %param.19) | copy-start | bytes 589828
  4.2 18.4 %all-to-all-start = ((bf16[16,2,1280]{2,1,0:T(2,128)(2,1)}), bf16[16,2,1280]{2,1,0:T(2,128)(2,1)S(1)}, u32[]{:S(2)}, u32[]{:S(2)}) async-start(bf16[16,2,1280]{2,1,0:T(2,128)(2,1)} %broadcast_in_dim.56), calls=%async_computation | async-start | bytes 163840 | tf_op jit(solution)/shard_map/all_to_all | solution.py:200
  14.4 8.2 %collective-permute-start = (bf16[528,256]{1,0:T(8,128)(2,1)S(1)}, bf16[528,256]{1,0:T(8,128)(2,1)S(1)}, u32[]{:S(2)}, u32[]{:S(2)}) collective-permute-start(bf16[528,256]{1,0:T(8,128)(2,1)S(1)} %fusion.2), channel_id=1, source_target_pairs={{0,1},{1,0},{2,3},{3,2},{4,5},{5,4},{6,7},{7,6},{8,9},{9,8},{10,11... | collective-permute-start | bytes 811016 | tf_op jit(solution)/shard_map/ppermute | solution.py:208
  16.7 5.9 %copy-start.1 = (bf16[512,64]{1,0:T(8,128)(2,1)}, bf16[512,64]{1,0:T(8,128)(2,1)S(1)}, u32[]{:S(2)}) copy-start(bf16[512,64]{1,0:T(8,128)(2,1)S(1)} %copy.75) | copy-start | bytes 196612
  22.7 9.4 %copy-start = (bf16[1,128,5120]{2,1,0:T(8,128)(2,1)S(1)}, bf16[1,128,5120]{2,1,0:T(8,128)(2,1)}, u32[]{:S(2)}) copy-start(bf16[1,128,5120]{2,1,0:T(8,128)(2,1)} %param.11) | copy-start | bytes 3932164
  23.7 22.2 %all-to-all-start.1 = ((bf16[8,160,128]{2,1,0:T(8,128)(2,1)}), bf16[8,160,128]{2,1,0:T(8,128)(2,1)S(1)}, u32[]{:S(2)}, u32[]{:S(2)}) async-start(bf16[8,160,128]{2,1,0:T(8,128)(2,1)} %broadcast_in_dim.57), calls=%async_computation.1 | async-start | bytes 655360 | tf_op jit(solution)/shard_map/all_to_all | solution.py:200
  32.1 27.0 %collective-permute-start.5 = (bf16[128,5120]{1,0:T(8,128)(2,1)S(1)}, bf16[128,5120]{1,0:T(8,128)(2,1)}, u32[]{:S(2)}, u32[]{:S(2)}) collective-permute-start(bf16[128,5120]{1,0:T(8,128)(2,1)S(1)} %bitcast.69), channel_id=1, source_target_pairs={{0,1},{1,0},{2,3},{3,2},{4,5},{5,4},{6,7},{7,6},{8,9},{9,8},{10,11... | collective-permute-start | bytes 3932168 | tf_op jit(solution)/shard_map/ppermute | solution.py:208
  34.7 30.9 %collective-permute-start.6 = (bf16[128,5120]{1,0:T(8,128)(2,1)}, bf16[128,5120]{1,0:T(8,128)(2,1)}, u32[]{:S(2)}, u32[]{:S(2)}) collective-permute-start(bf16[128,5120]{1,0:T(8,128)(2,1)} %bitcast.13.yo_ref.refs_3_), channel_id=1, source_target_pairs={{0,1},{2,3},{4,5},{6,7},{8,9},{10,11},{12,13},{14,15},{16,17},{18,... | collective-permute-start | bytes 3932168 | tf_op jit(solution)/shard_map/ppermute | solution.py:247
  47.1 29.7 %all-to-all-start.2 = ((bf16[4,1280,128]{2,1,0:T(8,128)(2,1)}), bf16[4,1280,128]{2,1,0:T(8,128)(2,1)S(1)}, u32[]{:S(2)}, u32[]{:S(2)}) async-start(bf16[4,1280,128]{2,1,0:T(8,128)(2,1)} %broadcast_in_dim.59), calls=%async_computation.2 | async-start | bytes 2621440 | tf_op jit(solution)/shard_map/all_to_all | solution.py:200
  51.2 32.1 %collective-permute-start.3 = (bf16[256,512]{1,0:T(8,128)(2,1)S(1)}, bf16[256,512]{1,0:T(8,128)(2,1)}, u32[]{:S(2)}, u32[]{:S(2)}) collective-permute-start(bf16[256,512]{1,0:T(8,128)(2,1)S(1)} %bitcast.72), channel_id=1, source_target_pairs={{2,0},{4,2},{6,4},{8,6},{10,8},{12,10},{14,12},{16,14},{18,16},{20... | collective-permute-start | bytes 786440 | tf_op jit(solution)/shard_map/ppermute | solution.py:213
  52.4 30.8 %collective-permute-start.2 = (bf16[256,512]{1,0:T(8,128)(2,1)S(1)}, bf16[256,512]{1,0:T(8,128)(2,1)}, u32[]{:S(2)}, u32[]{:S(2)}) collective-permute-start(bf16[256,512]{1,0:T(8,128)(2,1)S(1)} %bitcast.73), channel_id=1, source_target_pairs={{0,2},{2,4},{4,6},{6,8},{8,10},{10,12},{12,14},{14,16},{16,18},{18... | collective-permute-start | bytes 786440 | tf_op jit(solution)/shard_map/ppermute | solution.py:213
  57.9 25.4 %collective-permute-start.4 = (bf16[128,512]{1,0:T(8,128)(2,1)}, bf16[128,512]{1,0:T(8,128)(2,1)}, u32[]{:S(2)}, u32[]{:S(2)}) collective-permute-start(bf16[128,512]{1,0:T(8,128)(2,1)} %get-tuple-element.107), channel_id=1, source_target_pairs={{4,0},{6,2},{8,4},{10,6},{12,8},{14,10},{16,12},{18,14},{20,16},{2... | collective-permute-start | bytes 393224 | tf_op jit(solution)/shard_map/ppermute | solution.py:213
  59.2 24.1 %collective-permute-start.1 = (bf16[128,512]{1,0:T(8,128)(2,1)}, bf16[128,512]{1,0:T(8,128)(2,1)}, u32[]{:S(2)}, u32[]{:S(2)}) collective-permute-start(bf16[128,512]{1,0:T(8,128)(2,1)} %get-tuple-element.108), channel_id=1, source_target_pairs={{0,4},{2,6},{4,8},{6,10},{8,12},{10,14},{12,16},{14,18},{16,20},{1... | collective-permute-start | bytes 393224 | tf_op jit(solution)/shard_map/ppermute | solution.py:213
  87.0 17.4 %collective-permute-start.8 = (bf16[256,512]{1,0:T(8,128)(2,1)S(1)}, bf16[256,512]{1,0:T(8,128)(2,1)S(1)}, u32[]{:S(2)}, u32[]{:S(2)}) collective-permute-start(bf16[256,512]{1,0:T(8,128)(2,1)S(1)} %get-tuple-element.38), channel_id=1, source_target_pairs={{2,0},{4,2},{6,4},{8,6},{10,8},{12,10},{14,12},{16,14},{18,16},{20... | collective-permute-start | bytes 786440 | tf_op jit(solution)/shard_map/ppermute | solution.py:213
  88.3 16.1 %collective-permute-start.9 = (bf16[256,512]{1,0:T(8,128)(2,1)S(1)}, bf16[256,512]{1,0:T(8,128)(2,1)S(1)}, u32[]{:S(2)}, u32[]{:S(2)}) collective-permute-start(bf16[256,512]{1,0:T(8,128)(2,1)S(1)} %get-tuple-element.39), channel_id=1, source_target_pairs={{0,2},{2,4},{4,6},{6,8},{8,10},{10,12},{12,14},{14,16},{16,18},{18... | collective-permute-start | bytes 786440 | tf_op jit(solution)/shard_map/ppermute | solution.py:213
  92.3 10.6 %collective-permute-start.10 = (bf16[128,512]{1,0:T(8,128)(2,1)S(1)}, bf16[128,512]{1,0:T(8,128)(2,1)S(1)}, u32[]{:S(2)}, u32[]{:S(2)}) collective-permute-start(bf16[128,512]{1,0:T(8,128)(2,1)S(1)} %get-tuple-element.40), channel_id=1, source_target_pairs={{0,4},{2,6},{4,8},{6,10},{8,12},{10,14},{12,16},{14,18},{16,20},{1... | collective-permute-start | bytes 393224 | tf_op jit(solution)/shard_map/ppermute | solution.py:213
  93.7 10.7 %collective-permute-start.11 = (bf16[128,512]{1,0:T(8,128)(2,1)S(1)}, bf16[128,512]{1,0:T(8,128)(2,1)S(1)}, u32[]{:S(2)}, u32[]{:S(2)}) collective-permute-start(bf16[128,512]{1,0:T(8,128)(2,1)S(1)} %get-tuple-element.41), channel_id=1, source_target_pairs={{4,0},{6,2},{8,4},{10,6},{12,8},{14,10},{16,12},{18,14},{20,16},{2... | collective-permute-start | bytes 393224 | tf_op jit(solution)/shard_map/ppermute | solution.py:213
  95.0 12.1 %collective-permute-start.7 = (bf16[384,256]{1,0:T(8,128)(2,1)S(1)}, bf16[384,256]{1,0:T(8,128)(2,1)S(1)}, u32[]{:S(2)}, u32[]{:S(2)}) collective-permute-start(bf16[384,256]{1,0:T(8,128)(2,1)S(1)} %get-tuple-element.36), channel_id=1, source_target_pairs={{0,1},{1,0},{2,3},{3,2},{4,5},{5,4},{6,7},{7,6},{8,9},{9,8},{10,11... | collective-permute-start | bytes 589832 | tf_op jit(solution)/shard_map/ppermute | solution.py:208
  104.6 3.5 %collective-permute-start.12 = (bf16[384,256]{1,0:T(8,128)(2,1)S(1)}, bf16[384,256]{1,0:T(8,128)(2,1)S(1)}, u32[]{:S(2)}, u32[]{:S(2)}) collective-permute-start(bf16[384,256]{1,0:T(8,128)(2,1)S(1)} %pad_maximum_fusion.4), channel_id=1, source_target_pairs={{0,1},{1,0},{2,3},{3,2},{4,5},{5,4},{6,7},{7,6},{8,9},{9,8},{10,11... | collective-permute-start | bytes 589832 | tf_op jit(solution)/shard_map/ppermute | solution.py:208
  135.0 15.1 %all-to-all-start.4 = ((bf16[8,176,128]{2,1,0:T(8,128)(2,1)}), bf16[8,176,128]{2,1,0:T(8,128)(2,1)S(1)}, u32[]{:S(2)}, u32[]{:S(2)}) async-start(bf16[8,176,128]{2,1,0:T(8,128)(2,1)} %bitcast.29), calls=%async_computation.4 | async-start | bytes 720896 | tf_op jit(solution)/shard_map/all_to_all | solution.py:200
  150.8 16.9 %all-to-all-start.5 = ((bf16[16,26,128]{2,1,0:T(8,128)(2,1)}), bf16[16,26,128]{2,1,0:T(8,128)(2,1)S(1)}, u32[]{:S(2)}, u32[]{:S(2)}) async-start(bf16[16,26,128]{2,1,0:T(8,128)(2,1)} %pad_maximum_fusion.5), calls=%async_computation.5 | async-start | bytes 262144 | tf_op jit(solution)/shard_map/all_to_all | solution.py:200
  168.6 15.3 %all-to-all-start.6 = ((bf16[32,32,128]{2,1,0:T(8,128)(2,1)}), bf16[32,32,128]{2,1,0:T(8,128)(2,1)S(1)}, u32[]{:S(2)}, u32[]{:S(2)}) async-start(bf16[32,32,128]{2,1,0:T(8,128)(2,1)} %broadcast_in_dim.68), calls=%async_computation.6 | async-start | bytes 524288 | tf_op jit(solution)/shard_map/all_to_all | solution.py:200

commit v7 on v6

--- a/solution.py
+++ b/solution.py
@@ -196,6 +196,35 @@
     )(core, x_own, x_other, y_own, y_other, kept_a, got_a, kept_b, got_b, low, m_a, m_b)
 
 
+def spread_out_kernel(u_ref, up_ref, down_ref):
+    rank = down_ref.shape[0]
+    rows, cols = u_ref.shape[3:]
+    for core in range(2):
+        for z in range(NZ):
+            role, row = divmod(z * rows, rank)
+            for x in range(NX):
+                block = u_ref[x, z, core].astype(F32)
+                at = (slice(row, row + rows), slice(x * cols, (x + 1) * cols))
+                if core == 1 and role == 0:
+                    down_ref[at] = block
+                else:
+                    up_ref[(core + role, *at)] = block
+
+
+def spread_out(u_all, rank):
+    feats = NX * u_all.shape[4]
+    vmem = pl.BlockSpec(memory_space=pltpu.VMEM)
+    return pl.pallas_call(
+        spread_out_kernel,
+        out_shape=[jax.ShapeDtypeStruct((3, rank, feats), F32), jax.ShapeDtypeStruct((rank, feats), F32)],
+        in_specs=[vmem],
+        out_specs=[vmem] * 2,
+        compiler_params=pltpu.CompilerParams(vmem_limit_bytes=8 * 1024 * 1024),
+        cost_estimate=pl.CostEstimate(flops=131072, bytes_accessed=786432, transcendentals=0),
+        name="spread_out",
+    )(u_all)
+
+
 def exchange(parts, axes):
     return lax.all_to_all(parts, axes, split_axis=0, concat_axis=0, tiled=True)
 
@@ -306,9 +335,8 @@
     grad_up_out = g_out[1, :, :rank].T
     u_mine = step[:, own_cols:].astype(BF).reshape(2 * u_rows, 2 * rank)
     u_all = spread(u_mine, ("x", "z"), NX * NZ).reshape(NX, NZ, 2, u_rows, 2 * rank)
-    u_all = jnp.transpose(u_all, (2, 1, 3, 0, 4)).reshape(2, 2, rank, feats).astype(F32)
-    grad_up = jnp.stack([u_all[0, 0], u_all[0, 1], u_all[1, 1]])
-    grad_down_out = u_all[1, 0].T
+    grad_up, down_turned = spread_out(u_all, rank)
+    grad_down_out = down_turned.T
 
     def own_frame(mine, from_zero, from_one):
         left = jnp.where(first, mine[:rows], from_zero)

time: 187 us -> 186 us (level)
  no operation moved by 1% of the time
where the time goes in v7:
time: 186 us; the launch traced here: 185 us
  starting transfers between devices  69.2 us (37%)
  waiting for transfers between devices  62.9 us (34%)
  blocking collectives  25.3 us (14%)
  Pallas kernels  11.5 us (6%)
  local copies, waits for them, and re-layouts  8.17 us (4%)
  other arithmetic  6.44 us (3%)
    all_to_all x6, waiting for transfers between devices, exchange(): return lax.all_to_all(parts, axes, split_axis=0, concat_axis=0, tiled=True)  55.2 us
    all_to_all x6, starting transfers between devices, exchange(): return lax.all_to_all(parts, axes, split_axis=0, concat_axis=0, tiled=True)  37.7 us
    all_to_all x1, blocking collectives, exchange(): return lax.all_to_all(parts, axes, split_axis=0, concat_axis=0, tiled=True)  22.2 us
    ppermute x8, starting transfers between devices, chip_shift(): lax.ppermute(block, ('x', 'y'), [(i, i + by) for i in range(chips) if 0 <...  20.7 us
    ppermute x4, starting transfers between devices, swap(): return lax.ppermute(block, 'c', [(0, 1), (1, 0)])  9.58 us
    ppermute x8, waiting for transfers between devices, chip_shift(): lax.ppermute(block, ('x', 'y'), [(i, i + by) for i in range(chips) if 0 <...  6.63 us
    pallas_call x1, Pallas kernels, attention(): pl.pallas_call(attention_kernel, out_shape=outs, in_specs=[pl.BlockSpec(m...  3.75 us
  transfers between devices with their start and end apart: 19, of which 9 were waited for; matrix products, arithmetic and copies ran while one was open for 4% of the time, Pallas kernels for 2%

profile of v7, /device:TPU:1, one launch (start us, length us, event | category | flops | bytes accessed | tf_op | source)
XLA Modules:
  0.0 184.8 jit_solution(9024638952896001806)
XLA Ops:
  0.6 0.8 fusion.9
  1.5 0.8 pad_maximum_fusion.6
  2.3 1.2 pad_maximum_fusion.1
  3.5 0.7 broadcast_in_dim.56
  4.2 10.2 %all-to-all-start = ((bf16[16,2,1280]{2,1,0:T(2,128)(2,1)}), bf16[16,2,1280]{2,1,0:T(2,128)(2,1)S(1)}, u32[]{:S(2)}, u32[]{:S(2)}) async-start(bf16[16,2,1280]{2,1,0:T(2,128)(2,1)} %broadcast_in_dim.56), calls=%async_computation | async-start | bytes 163840 | tf_op jit(solution)/shard_map/all_to_all | solution.py:229
  14.4 2.1 %collective-permute-start = (bf16[528,256]{1,0:T(8,128)(2,1)S(1)}, bf16[528,256]{1,0:T(8,128)(2,1)S(1)}, u32[]{:S(2)}, u32[]{:S(2)}) collective-permute-start(bf16[528,256]{1,0:T(8,128)(2,1)S(1)} %fusion.2), channel_id=1, source_target_pairs={{0,1},{1,0},{2,3},{3,2},{4,5},{5,4},{6,7},{7,6},{8,9},{9,8},{10,11... | collective-permute-start | bytes 811016 | tf_op jit(solution)/shard_map/ppermute | solution.py:237
  16.6 0.1 copy.63
  16.8 0.1 copy.76
  16.9 0.1 copy.75
  17.0 0.1 copy.74
  17.2 5.3 %all-to-all-done = bf16[16,2,1280]{2,1,0:T(2,128)(2,1)S(1)} async-done(((bf16[16,2,1280]{2,1,0:T(2,128)(2,1)}), bf16[16,2,1280]{2,1,0:T(2,128)(2,1)S(1)}, u32[]{:S(2)}, u32[]{:S(2)}) %all-to-all-start) | async-done | bytes 81952 | tf_op jit(solution)/shard_map/all_to_all | solution.py:229
  22.5 0.1 reshape.80
  22.6 0.1 select_bitcast_fusion.1
  22.8 0.1 pad_maximum_fusion
  22.8 0.1 copy.61
  22.9 0.8 broadcast_in_dim.57
  23.7 8.4 %all-to-all-start.1 = ((bf16[8,160,128]{2,1,0:T(8,128)(2,1)}), bf16[8,160,128]{2,1,0:T(8,128)(2,1)S(1)}, u32[]{:S(2)}, u32[]{:S(2)}) async-start(bf16[8,160,128]{2,1,0:T(8,128)(2,1)} %broadcast_in_dim.57), calls=%async_computation.1 | async-start | bytes 655360 | tf_op jit(solution)/shard_map/all_to_all | solution.py:229
  32.1 2.2 %collective-permute-start.5 = (bf16[128,5120]{1,0:T(8,128)(2,1)S(1)}, bf16[128,5120]{1,0:T(8,128)(2,1)}, u32[]{:S(2)}, u32[]{:S(2)}) collective-permute-start(bf16[128,5120]{1,0:T(8,128)(2,1)S(1)} %bitcast.57), channel_id=1, source_target_pairs={{0,1},{1,0},{2,3},{3,2},{4,5},{5,4},{6,7},{7,6},{8,9},{9,8},{10,11... | collective-permute-start | bytes 3932168 | tf_op jit(solution)/shard_map/ppermute | solution.py:237
  34.4 0.1 compare_reduce_fusion
  34.5 0.1 broadcast_in_dim.62
  34.6 0.1 reshape.83.bias_ref
  34.7 1.3 collective-permute-start.6
  36.1 9.8 %all-to-all-done.1 = bf16[8,160,128]{2,1,0:T(8,128)(2,1)S(1)} async-done(((bf16[8,160,128]{2,1,0:T(8,128)(2,1)}), bf16[8,160,128]{2,1,0:T(8,128)(2,1)S(1)}, u32[]{:S(2)}, u32[]{:S(2)}) %all-to-all-start.1) | async-done | bytes 327712 | tf_op jit(solution)/shard_map/all_to_all | solution.py:229
  45.9 1.2 broadcast_in_dim.59
  47.1 4.0 %all-to-all-start.2 = ((bf16[4,1280,128]{2,1,0:T(8,128)(2,1)}), bf16[4,1280,128]{2,1,0:T(8,128)(2,1)S(1)}, u32[]{:S(2)}, u32[]{:S(2)}) async-start(bf16[4,1280,128]{2,1,0:T(8,128)(2,1)} %broadcast_in_dim.59), calls=%async_computation.2 | async-start | bytes 2621440 | tf_op jit(solution)/shard_map/all_to_all | solution.py:229
  51.2 1.3 collective-permute-start.3
  52.4 4.7 %collective-permute-start.2 = (bf16[256,512]{1,0:T(8,128)(2,1)S(1)}, bf16[256,512]{1,0:T(8,128)(2,1)}, u32[]{:S(2)}, u32[]{:S(2)}) collective-permute-start(bf16[256,512]{1,0:T(8,128)(2,1)S(1)} %bitcast.61), channel_id=1, source_target_pairs={{0,2},{2,4},{4,6},{6,8},{8,10},{10,12},{12,14},{14,16},{16,18},{18... | collective-permute-start | bytes 786440 | tf_op jit(solution)/shard_map/ppermute | solution.py:242
  57.1 0.7 fusion.6
  57.9 1.3 collective-permute-start.4
  59.2 5.5 %collective-permute-start.1 = (bf16[128,512]{1,0:T(8,128)(2,1)}, bf16[128,512]{1,0:T(8,128)(2,1)}, u32[]{:S(2)}, u32[]{:S(2)}) collective-permute-start(bf16[128,512]{1,0:T(8,128)(2,1)} %get-tuple-element.101), channel_id=1, source_target_pairs={{0,4},{2,6},{4,8},{6,10},{8,12},{10,14},{12,16},{14,18},{16,20},{1... | collective-permute-start | bytes 393224 | tf_op jit(solution)/shard_map/ppermute | solution.py:242
  64.7 0.8 constant_dynamic-slice_fusion.odp_ref
  65.6 11.3 %all-to-all-done.2 = bf16[4,1280,128]{2,1,0:T(8,128)(2,1)S(1)} async-done(((bf16[4,1280,128]{2,1,0:T(8,128)(2,1)}), bf16[4,1280,128]{2,1,0:T(8,128)(2,1)S(1)}, u32[]{:S(2)}, u32[]{:S(2)}) %all-to-all-start.2) | async-done | bytes 1310752 | tf_op jit(solution)/shard_map/all_to_all | solution.py:229
  76.8 3.3 %low_factors.1.refs_9_ = bf16[256,128]{1,0:T(8,128)(2,1)S(1)} custom-call(s32[1]{0:T(128)} %bitcast.core_ref.refs_0_, bf16[128,5120]{1,0:T(8,128)(2,1)S(1)} %bitcast.58, bf16[128,5120]{1,0:T(8,128)(2,1)} %collective-permute-done.5.xt_ref.refs_2_, bf16[128,5120]{1,0:T(8,128)(2,1)} %bitcast.13.yo_ref.refs_3_, ...), custom_call_target="tpu_custom_call" | custom-call | flops 700000000 | bytes 6600000 | tf_op jit(solution)/shard_map/low_factors/pallas_call | solution.py:123
  80.1 3.2 %all-gather = bf16[512,128]{1,0:T(8,128)(2,1)S(1)} all-gather(bf16[256,128]{1,0:T(8,128)(2,1)S(1)} %low_factors.1.refs_9_), channel_id=2, replica_groups=mesh['z'=8,'x'=4,'y'=8,'c'=2] {'c'}, dimensions={0}, use_global_device_ids=true | all-gather | bytes 196608 | tf_op jit(solution)/shard_map/all_gather | solution.py:299
  83.3 3.7 %attention.1 = (bf16[256,256]{1,0:T(8,128)(2,1)S(1)}, bf16[384,256]{1,0:T(8,128)(2,1)S(1)}, bf16[256,256]{1,0:T(8,128)(2,1)S(1)}, bf16[128,512]{1,0:T(8,128)(2,1...) custom-call(s32[1]{0:T(128)} %bitcast.core_ref.refs_0_, ...), custom_call_target="tpu_custom_call" | custom-call | flops 700000000 | bytes 4000000 | tf_op jit(solution)/shard_map/attention/pallas_call | solution.py:78
  87.0 1.3 collective-permute-start.8
  88.3 4.0 %collective-permute-start.9 = (bf16[256,512]{1,0:T(8,128)(2,1)S(1)}, bf16[256,512]{1,0:T(8,128)(2,1)S(1)}, u32[]{:S(2)}, u32[]{:S(2)}) collective-permute-start(bf16[256,512]{1,0:T(8,128)(2,1)S(1)} %get-tuple-element.41), channel_id=1, source_target_pairs={{0,2},{2,4},{4,6},{6,8},{8,10},{10,12},{12,14},{14,16},{16,18},{18... | collective-permute-start | bytes 786440 | tf_op jit(solution)/shard_map/ppermute | solution.py:242
  92.3 1.3 collective-permute-start.10
  93.7 1.3 collective-permute-start.11
  95.0 2.8 %collective-permute-start.7 = (bf16[384,256]{1,0:T(8,128)(2,1)S(1)}, bf16[384,256]{1,0:T(8,128)(2,1)S(1)}, u32[]{:S(2)}, u32[]{:S(2)}) collective-permute-start(bf16[384,256]{1,0:T(8,128)(2,1)S(1)} %get-tuple-element.38), channel_id=1, source_target_pairs={{0,1},{1,0},{2,3},{3,2},{4,5},{5,4},{6,7},{7,6},{8,9},{9,8},{10,11... | collective-permute-start | bytes 589832 | tf_op jit(solution)/shard_map/ppermute | solution.py:237
  97.8 5.2 %collective-permute-done.10 = bf16[128,512]{1,0:T(8,128)(2,1)S(1)} collective-permute-done((bf16[128,512]{1,0:T(8,128)(2,1)S(1)}, bf16[128,512]{1,0:T(8,128)(2,1)S(1)}, u32[]{:S(2)}, u32[]{:S(2)}) %collective-permute-start.10) | collective-permute-done | bytes 131104 | tf_op jit(solution)/shard_map/ppermute | solution.py:242
  103.0 1.4 collective-permute-done.11
  104.4 0.1 add_convert_fusion
  104.6 2.4 %collective-permute-start.12 = (bf16[384,256]{1,0:T(8,128)(2,1)S(1)}, bf16[384,256]{1,0:T(8,128)(2,1)S(1)}, u32[]{:S(2)}, u32[]{:S(2)}) collective-permute-start(bf16[384,256]{1,0:T(8,128)(2,1)S(1)} %pad_maximum_fusion.3), channel_id=1, source_target_pairs={{0,1},{1,0},{2,3},{3,2},{4,5},{5,4},{6,7},{7,6},{8,9},{9,8},{10,11... | collective-permute-start | bytes 589832 | tf_op jit(solution)/shard_map/ppermute | solution.py:237
  107.0 1.0 collective-permute-done.12.refs_8_
  108.1 3.7 %grad_partials.1 = bf16[4,8,176,128]{3,2,1,0:T(8,128)(2,1)S(1)} custom-call(s32[1]{0:T(128)} %bitcast.core_ref.refs_0_, bf16[128,5120]{1,0:T(8,128)(2,1)S(1)} %bitcast.59, bf16[128,5120]{1,0:T(8,128)(2,1)} %collective-permute-done.5.xt_ref.refs_2_, bf16[128,5120]{1,0:T(8,128)(2,1)} %bitcast.13.yo_ref.refs_3_, ...), custom_call_target="tpu_custom_call" | custom-call | flops 800000000 | bytes 7500000 | tf_op jit(solution)/shard_map/grad_partials/pallas_call | solution.py:186
  111.8 22.2 %all_to_all.35 = bf16[4,1408,128]{2,1,0:T(8,128)(2,1)S(1)} all-to-all(bf16[4,1408,128]{2,1,0:T(8,128)(2,1)S(1)} %bitcast.55), channel_id=1, replica_groups=mesh['z'=8,'x'=4,'y'=8,'c'=2] {'x'}, dimensions={0} | all-to-all | bytes 2883584 | tf_op jit(solution)/shard_map/all_to_all | solution.py:229
  133.9 1.0 reduce_sum.33
  135.0 3.4 %all-to-all-start.4 = ((bf16[8,176,128]{2,1,0:T(8,128)(2,1)}), bf16[8,176,128]{2,1,0:T(8,128)(2,1)S(1)}, u32[]{:S(2)}, u32[]{:S(2)}) async-start(bf16[8,176,128]{2,1,0:T(8,128)(2,1)} %bitcast.29), calls=%async_computation.4 | async-start | bytes 720896 | tf_op jit(solution)/shard_map/all_to_all | solution.py:229
  138.4 0.7 maximum_bitcast_fusion
  139.1 10.9 %all-to-all-done.4 = bf16[8,176,128]{2,1,0:T(8,128)(2,1)S(1)} async-done(((bf16[8,176,128]{2,1,0:T(8,128)(2,1)}), bf16[8,176,128]{2,1,0:T(8,128)(2,1)S(1)}, u32[]{:S(2)}, u32[]{:S(2)}) %all-to-all-start.4) | async-done | bytes 360480 | tf_op jit(solution)/shard_map/all_to_all | solution.py:229
  150.1 0.7 pad_maximum_fusion.4
  150.8 7.7 %all-to-all-start.5 = ((bf16[16,26,128]{2,1,0:T(8,128)(2,1)}), bf16[16,26,128]{2,1,0:T(8,128)(2,1)S(1)}, u32[]{:S(2)}, u32[]{:S(2)}) async-start(bf16[16,26,128]{2,1,0:T(8,128)(2,1)} %pad_maximum_fusion.4), calls=%async_computation.5 | async-start | bytes 262144 | tf_op jit(solution)/shard_map/all_to_all | solution.py:229
  158.6 9.1 %all-to-all-done.5 = bf16[16,26,128]{2,1,0:T(8,128)(2,1)S(1)} async-done(((bf16[16,26,128]{2,1,0:T(8,128)(2,1)}), bf16[16,26,128]{2,1,0:T(8,128)(2,1)S(1)}, u32[]{:S(2)}, u32[]{:S(2)}) %all-to-all-start.5) | async-done | bytes 106528 | tf_op jit(solution)/shard_map/all_to_all | solution.py:229
  167.8 0.1 convert_reduce_fusion
  167.9 0.7 broadcast_in_dim.68
  168.6 3.9 %all-to-all-start.6 = ((bf16[32,32,128]{2,1,0:T(8,128)(2,1)}), bf16[32,32,128]{2,1,0:T(8,128)(2,1)S(1)}, u32[]{:S(2)}, u32[]{:S(2)}) async-start(bf16[32,32,128]{2,1,0:T(8,128)(2,1)} %broadcast_in_dim.68), calls=%async_computation.6 | async-start | bytes 524288 | tf_op jit(solution)/shard_map/all_to_all | solution.py:229
  172.5 0.7 maximum_bitcast_fusion.2
  173.2 0.7 maximum_bitcast_fusion.1
  173.9 0.1 slice.167
  173.9 0.6 copy.87
  174.6 0.6 copy.69
  175.2 8.8 %all-to-all-done.6 = bf16[32,32,128]{2,1,0:T(8,128)(2,1)S(1)} async-done(((bf16[32,32,128]{2,1,0:T(8,128)(2,1)}), bf16[32,32,128]{2,1,0:T(8,128)(2,1)S(1)}, u32[]{:S(2)}, u32[]{:S(2)}) %all-to-all-start.6) | async-done | bytes 262176 | tf_op jit(solution)/shard_map/all_to_all | solution.py:229
  184.0 0.8 spread_out.1
  (53 shorter events, 0.6 us)
Async XLA Ops:
  0.6 13.7 %copy-start.4 = (s32[1,4,12]{2,1,0:T(4,128)S(1)}, s32[1,4,12]{2,1,0:T(4,128)}, u32[]{:S(2)}) copy-start(s32[1,4,12]{2,1,0:T(4,128)} %param.17) | copy-start | bytes 580
  2.3 14.3 %copy-start.3 = (bf16[512,64]{0,1:T(8,128)(2,1)S(1)}, bf16[512,64]{0,1:T(8,128)(2,1)}, u32[]{:S(2)}) copy-start(bf16[512,64]{0,1:T(8,128)(2,1)} %param.20) | copy-start | bytes 196612
  2.3 14.4 %copy-start.2 = (bf16[3,64,512]{2,1,0:T(8,128)(2,1)S(1)}, bf16[3,64,512]{2,1,0:T(8,128)(2,1)}, u32[]{:S(2)}) copy-start(bf16[3,64,512]{2,1,0:T(8,128)(2,1)} %param.19) | copy-start | bytes 589828
  4.2 18.4 %all-to-all-start = ((bf16[16,2,1280]{2,1,0:T(2,128)(2,1)}), bf16[16,2,1280]{2,1,0:T(2,128)(2,1)S(1)}, u32[]{:S(2)}, u32[]{:S(2)}) async-start(bf16[16,2,1280]{2,1,0:T(2,128)(2,1)} %broadcast_in_dim.56), calls=%async_computation | async-start | bytes 163840 | tf_op jit(solution)/shard_map/all_to_all | solution.py:229
  14.4 8.2 %collective-permute-start = (bf16[528,256]{1,0:T(8,128)(2,1)S(1)}, bf16[528,256]{1,0:T(8,128)(2,1)S(1)}, u32[]{:S(2)}, u32[]{:S(2)}) collective-permute-start(bf16[528,256]{1,0:T(8,128)(2,1)S(1)} %fusion.2), channel_id=1, source_target_pairs={{0,1},{1,0},{2,3},{3,2},{4,5},{5,4},{6,7},{7,6},{8,9},{9,8},{10,11... | collective-permute-start | bytes 811016 | tf_op jit(solution)/shard_map/ppermute | solution.py:237
  16.7 5.9 %copy-start.1 = (bf16[512,64]{1,0:T(8,128)(2,1)}, bf16[512,64]{1,0:T(8,128)(2,1)S(1)}, u32[]{:S(2)}) copy-start(bf16[512,64]{1,0:T(8,128)(2,1)S(1)} %copy.63) | copy-start | bytes 196612
  22.7 9.4 %copy-start = (bf16[1,128,5120]{2,1,0:T(8,128)(2,1)S(1)}, bf16[1,128,5120]{2,1,0:T(8,128)(2,1)}, u32[]{:S(2)}) copy-start(bf16[1,128,5120]{2,1,0:T(8,128)(2,1)} %param.11) | copy-start | bytes 3932164
  23.7 22.2 %all-to-all-start.1 = ((bf16[8,160,128]{2,1,0:T(8,128)(2,1)}), bf16[8,160,128]{2,1,0:T(8,128)(2,1)S(1)}, u32[]{:S(2)}, u32[]{:S(2)}) async-start(bf16[8,160,128]{2,1,0:T(8,128)(2,1)} %broadcast_in_dim.57), calls=%async_computation.1 | async-start | bytes 655360 | tf_op jit(solution)/shard_map/all_to_all | solution.py:229
  32.1 27.0 %collective-permute-start.5 = (bf16[128,5120]{1,0:T(8,128)(2,1)S(1)}, bf16[128,5120]{1,0:T(8,128)(2,1)}, u32[]{:S(2)}, u32[]{:S(2)}) collective-permute-start(bf16[128,5120]{1,0:T(8,128)(2,1)S(1)} %bitcast.57), channel_id=1, source_target_pairs={{0,1},{1,0},{2,3},{3,2},{4,5},{5,4},{6,7},{7,6},{8,9},{9,8},{10,11... | collective-permute-start | bytes 3932168 | tf_op jit(solution)/shard_map/ppermute | solution.py:237
  34.7 30.9 %collective-permute-start.6 = (bf16[128,5120]{1,0:T(8,128)(2,1)}, bf16[128,5120]{1,0:T(8,128)(2,1)}, u32[]{:S(2)}, u32[]{:S(2)}) collective-permute-start(bf16[128,5120]{1,0:T(8,128)(2,1)} %bitcast.13.yo_ref.refs_3_), channel_id=1, source_target_pairs={{0,1},{2,3},{4,5},{6,7},{8,9},{10,11},{12,13},{14,15},{16,17},{18,... | collective-permute-start | bytes 3932168 | tf_op jit(solution)/shard_map/ppermute | solution.py:276
  47.1 29.7 %all-to-all-start.2 = ((bf16[4,1280,128]{2,1,0:T(8,128)(2,1)}), bf16[4,1280,128]{2,1,0:T(8,128)(2,1)S(1)}, u32[]{:S(2)}, u32[]{:S(2)}) async-start(bf16[4,1280,128]{2,1,0:T(8,128)(2,1)} %broadcast_in_dim.59), calls=%async_computation.2 | async-start | bytes 2621440 | tf_op jit(solution)/shard_map/all_to_all | solution.py:229
  51.2 32.1 %collective-permute-start.3 = (bf16[256,512]{1,0:T(8,128)(2,1)S(1)}, bf16[256,512]{1,0:T(8,128)(2,1)}, u32[]{:S(2)}, u32[]{:S(2)}) collective-permute-start(bf16[256,512]{1,0:T(8,128)(2,1)S(1)} %bitcast.60), channel_id=1, source_target_pairs={{2,0},{4,2},{6,4},{8,6},{10,8},{12,10},{14,12},{16,14},{18,16},{20... | collective-permute-start | bytes 786440 | tf_op jit(solution)/shard_map/ppermute | solution.py:242
  52.4 30.8 %collective-permute-start.2 = (bf16[256,512]{1,0:T(8,128)(2,1)S(1)}, bf16[256,512]{1,0:T(8,128)(2,1)}, u32[]{:S(2)}, u32[]{:S(2)}) collective-permute-start(bf16[256,512]{1,0:T(8,128)(2,1)S(1)} %bitcast.61), channel_id=1, source_target_pairs={{0,2},{2,4},{4,6},{6,8},{8,10},{10,12},{12,14},{14,16},{16,18},{18... | collective-permute-start | bytes 786440 | tf_op jit(solution)/shard_map/ppermute | solution.py:242
  57.9 25.4 %collective-permute-start.4 = (bf16[128,512]{1,0:T(8,128)(2,1)}, bf16[128,512]{1,0:T(8,128)(2,1)}, u32[]{:S(2)}, u32[]{:S(2)}) collective-permute-start(bf16[128,512]{1,0:T(8,128)(2,1)} %get-tuple-element.100), channel_id=1, source_target_pairs={{4,0},{6,2},{8,4},{10,6},{12,8},{14,10},{16,12},{18,14},{20,16},{2... | collective-permute-start | bytes 393224 | tf_op jit(solution)/shard_map/ppermute | solution.py:242
  59.2 24.1 %collective-permute-start.1 = (bf16[128,512]{1,0:T(8,128)(2,1)}, bf16[128,512]{1,0:T(8,128)(2,1)}, u32[]{:S(2)}, u32[]{:S(2)}) collective-permute-start(bf16[128,512]{1,0:T(8,128)(2,1)} %get-tuple-element.101), channel_id=1, source_target_pairs={{0,4},{2,6},{4,8},{6,10},{8,12},{10,14},{12,16},{14,18},{16,20},{1... | collective-permute-start | bytes 393224 | tf_op jit(solution)/shard_map/ppermute | solution.py:242
  87.0 17.4 %collective-permute-start.8 = (bf16[256,512]{1,0:T(8,128)(2,1)S(1)}, bf16[256,512]{1,0:T(8,128)(2,1)S(1)}, u32[]{:S(2)}, u32[]{:S(2)}) collective-permute-start(bf16[256,512]{1,0:T(8,128)(2,1)S(1)} %get-tuple-element.40), channel_id=1, source_target_pairs={{2,0},{4,2},{6,4},{8,6},{10,8},{12,10},{14,12},{16,14},{18,16},{20... | collective-permute-start | bytes 786440 | tf_op jit(solution)/shard_map/ppermute | solution.py:242
  88.3 16.1 %collective-permute-start.9 = (bf16[256,512]{1,0:T(8,128)(2,1)S(1)}, bf16[256,512]{1,0:T(8,128)(2,1)S(1)}, u32[]{:S(2)}, u32[]{:S(2)}) collective-permute-start(bf16[256,512]{1,0:T(8,128)(2,1)S(1)} %get-tuple-element.41), channel_id=1, source_target_pairs={{0,2},{2,4},{4,6},{6,8},{8,10},{10,12},{12,14},{14,16},{16,18},{18... | collective-permute-start | bytes 786440 | tf_op jit(solution)/shard_map/ppermute | solution.py:242
  92.3 10.6 %collective-permute-start.10 = (bf16[128,512]{1,0:T(8,128)(2,1)S(1)}, bf16[128,512]{1,0:T(8,128)(2,1)S(1)}, u32[]{:S(2)}, u32[]{:S(2)}) collective-permute-start(bf16[128,512]{1,0:T(8,128)(2,1)S(1)} %get-tuple-element.42), channel_id=1, source_target_pairs={{0,4},{2,6},{4,8},{6,10},{8,12},{10,14},{12,16},{14,18},{16,20},{1... | collective-permute-start | bytes 393224 | tf_op jit(solution)/shard_map/ppermute | solution.py:242
  93.7 10.7 %collective-permute-start.11 = (bf16[128,512]{1,0:T(8,128)(2,1)S(1)}, bf16[128,512]{1,0:T(8,128)(2,1)S(1)}, u32[]{:S(2)}, u32[]{:S(2)}) collective-permute-start(bf16[128,512]{1,0:T(8,128)(2,1)S(1)} %get-tuple-element.43), channel_id=1, source_target_pairs={{4,0},{6,2},{8,4},{10,6},{12,8},{14,10},{16,12},{18,14},{20,16},{2... | collective-permute-start | bytes 393224 | tf_op jit(solution)/shard_map/ppermute | solution.py:242
  95.0 12.1 %collective-permute-start.7 = (bf16[384,256]{1,0:T(8,128)(2,1)S(1)}, bf16[384,256]{1,0:T(8,128)(2,1)S(1)}, u32[]{:S(2)}, u32[]{:S(2)}) collective-permute-start(bf16[384,256]{1,0:T(8,128)(2,1)S(1)} %get-tuple-element.38), channel_id=1, source_target_pairs={{0,1},{1,0},{2,3},{3,2},{4,5},{5,4},{6,7},{7,6},{8,9},{9,8},{10,11... | collective-permute-start | bytes 589832 | tf_op jit(solution)/shard_map/ppermute | solution.py:237
  104.6 3.5 %collective-permute-start.12 = (bf16[384,256]{1,0:T(8,128)(2,1)S(1)}, bf16[384,256]{1,0:T(8,128)(2,1)S(1)}, u32[]{:S(2)}, u32[]{:S(2)}) collective-permute-start(bf16[384,256]{1,0:T(8,128)(2,1)S(1)} %pad_maximum_fusion.3), channel_id=1, source_target_pairs={{0,1},{1,0},{2,3},{3,2},{4,5},{5,4},{6,7},{7,6},{8,9},{9,8},{10,11... | collective-permute-start | bytes 589832 | tf_op jit(solution)/shard_map/ppermute | solution.py:237
  135.0 15.1 %all-to-all-start.4 = ((bf16[8,176,128]{2,1,0:T(8,128)(2,1)}), bf16[8,176,128]{2,1,0:T(8,128)(2,1)S(1)}, u32[]{:S(2)}, u32[]{:S(2)}) async-start(bf16[8,176,128]{2,1,0:T(8,128)(2,1)} %bitcast.29), calls=%async_computation.4 | async-start | bytes 720896 | tf_op jit(solution)/shard_map/all_to_all | solution.py:229
  150.8 16.9 %all-to-all-start.5 = ((bf16[16,26,128]{2,1,0:T(8,128)(2,1)}), bf16[16,26,128]{2,1,0:T(8,128)(2,1)S(1)}, u32[]{:S(2)}, u32[]{:S(2)}) async-start(bf16[16,26,128]{2,1,0:T(8,128)(2,1)} %pad_maximum_fusion.4), calls=%async_computation.5 | async-start | bytes 262144 | tf_op jit(solution)/shard_map/all_to_all | solution.py:229
  168.6 15.3 %all-to-all-start.6 = ((bf16[32,32,128]{2,1,0:T(8,128)(2,1)}), bf16[32,32,128]{2,1,0:T(8,128)(2,1)S(1)}, u32[]{:S(2)}, u32[]{:S(2)}) async-start(bf16[32,32,128]{2,1,0:T(8,128)(2,1)} %broadcast_in_dim.68), calls=%async_computation.6 | async-start | bytes 524288 | tf_op jit(solution)/shard_map/all_to_all | solution.py:229
